TPU v7x, 32 devices: a whole 2x2x4 slice. The times are simulated.
32 devices in a mesh: groups: 2 (over x), outc: 8 (over z, y), inc: 2 (over core).
Axes of the slice: x: 2, y: 2, z: 4, core: 2. Of those that a mesh axis runs over, the one named last changes fastest.
Arguments:
- tokens: bfloat16 [1024, 8192], P(('groups', 'outc'), 'inc'), parts along dimension 0, may hold values from -6 to 6
- w_zx: bfloat16 [8192, 128, 128], P('inc', 'outc'), may hold values from -0.0625 to 0.0625
- w_dt: bfloat16 [8192, 128], P('inc', 'outc'), may hold values from -0.0625 to 0.0625
- w_bc: bfloat16 [8192, 1024], P('inc', 'outc'), may hold values from -0.0625 to 0.0625
- conv_x: float32 [4, 128, 64], P(None, ('outc', 'inc')), may hold values from -3 to 3
- conv_bc: float32 [4, 1024], replicated, may hold values from -3 to 3
- dt_bias: float32 [128], P(('outc', 'inc')), may hold values from -3 to 1
- decay_rate: float32 [128], P(('outc', 'inc')), may hold values from 0.05 to 4
- skip_gain: float32 [128], P(('outc', 'inc')), may hold values from 0.5 to 1.5
- norm_gain: float32 [128, 64], P(('outc', 'inc')), may hold values from 0.1 to 1.9
- w_out: bfloat16 [8192, 8192], P('outc', 'inc'), may hold values from -0.0625 to 0.0625
- conv_x_state: bfloat16 [128, 3, 128, 64], P('groups', None, ('outc', 'inc')), parts along dimension 0, may hold values from -6 to 6
- conv_bc_state: bfloat16 [128, 3, 1024], P('groups'), parts along dimension 0, may hold values from -6 to 6
- ssm_state: bfloat16 [128, 128, 64, 128], P('groups', ('outc', 'inc')), parts along dimension 0, may hold values from -6 to 6
- span_start: int32 [128], P('groups'), parts along dimension 0, may hold values from 0 to 8
- accepted: int32 [128], P('groups'), parts along dimension 0, may hold values from 0 to 8
Outputs:
- output: bfloat16 [1024, 8192], P(('groups', 'outc'), 'inc'), parts along dimension 0
- new_state: bfloat16 [128, 128, 64, 128], P('groups', ('outc', 'inc')), parts along dimension 0
- new_conv_x: bfloat16 [128, 3, 128, 64], P('groups', None, ('outc', 'inc')), parts along dimension 0
- new_conv_bc: bfloat16 [128, 3, 1024], P('groups'), parts along dimension 0
There are 2 independent parts, one for each index of `groups`. A program takes and returns all parts, laid end to end along the dimension named above; an argument that names none is the same for every part. Nothing has to cross between parts.
Inputs may be any that keep to these rules, and one draw needn't show every extreme that they name: `span_start`: 8 means that no new span begins among the drafts.
All inputs are finite; a program needn't handle non-finite values.
Results may differ from a plain program's by a relative error of at most 0.0075.
Values may be sent and summed in bfloat16 or wider, within the bound.
No kernel may reach another device: no remote copies, remote signals or barrier semaphores. Data moves between devices by JAX's collectives and lax.ppermute only.
A program may use at most 192 MiB of HBM per device.

v0:
```python
import jax
import jax.numpy as jnp
from jax import lax
from jax.sharding import PartitionSpec as P

HEADS = 128
G = 4
KW = 4
DRAFT = 8


def causal_conv(history, kernel, span_start):
    kernel_len = kernel.shape[0]
    draft_len = history.shape[1] - kernel_len + 1
    positions = jnp.arange(draft_len, dtype=jnp.int32)
    summed = jnp.zeros((history.shape[0], draft_len, history.shape[2]), jnp.float32)
    for offset in range(kernel_len):
        source_pos = positions + offset - (kernel_len - 1)
        visible = (positions[None, :] < span_start[:, None]) | (
            source_pos[None, :] >= span_start[:, None]
        )
        summed = summed + kernel[offset][None, None, :] * history[
            :, offset : offset + draft_len
        ].astype(jnp.float32) * visible[:, :, None].astype(jnp.float32)
    return summed


def conv_tail(history, span_start, accepted):
    offsets = jnp.arange(KW - 1, dtype=jnp.int32)
    wanted = accepted[:, None] + offsets[None, :]
    source_pos = wanted - (KW - 1)
    slots = jnp.arange(history.shape[1], dtype=jnp.int32)
    picker = (slots[None, None, :] == wanted[:, :, None]).astype(jnp.float32)
    picked = jnp.einsum(
        "rjl,rlc->rjc", picker, history.astype(jnp.float32), precision=lax.Precision.HIGHEST
    )
    cleared = (source_pos < span_start[:, None]) & (span_start[:, None] < accepted[:, None])
    return jnp.where(cleared[:, :, None], jnp.zeros_like(picked), picked).astype(jnp.bfloat16)


def shards(
    tokens,
    w_zx,
    w_dt,
    w_bc,
    conv_x,
    conv_bc,
    dt_bias,
    decay_rate,
    skip_gain,
    norm_gain,
    w_out,
    conv_x_state,
    conv_bc_state,
    ssm_state,
    span_start,
    accepted,
):
    heads_dev = ssm_state.shape[1]
    width_p = ssm_state.shape[2]
    width_n = ssm_state.shape[3]
    half_d = tokens.shape[1]
    block_heads = w_zx.shape[1]
    inner = 2 * width_p
    zx_flat = w_zx.reshape(half_d, block_heads * inner)
    piece = lax.all_gather(tokens, "outc", axis=0, tiled=True)
    partial_value = jnp.concatenate(
        [
            jnp.dot(piece, zx_flat, preferred_element_type=jnp.float32),
            jnp.dot(piece, w_dt, preferred_element_type=jnp.float32),
            jnp.dot(piece, w_bc, preferred_element_type=jnp.float32),
        ],
        axis=1,
    )
    rows_all = partial_value.shape[0]
    zx_part = partial_value[:, : block_heads * inner].reshape(rows_all, block_heads, inner)
    dt_part = partial_value[:, block_heads * inner : block_heads * inner + block_heads]
    bc_part = partial_value[:, block_heads * inner + block_heads :]
    zx_sum, dt_sum, bc_sum = (
        lax.psum_scatter(zx_part, "inc", scatter_dimension=1, tiled=True),
        lax.psum_scatter(dt_part, "inc", scatter_dimension=1, tiled=True),
        lax.psum_scatter(bc_part, "inc", scatter_dimension=1, tiled=True),
    )
    zx_proj = zx_sum.astype(jnp.bfloat16)
    dt_proj = dt_sum.astype(jnp.bfloat16)
    bc_proj = lax.all_gather(bc_sum.astype(jnp.bfloat16), ("outc", "inc"), axis=1, tiled=True)
    req_count = rows_all // DRAFT
    projected = zx_proj.reshape(req_count, DRAFT, heads_dev, inner)
    gate_raw = projected[..., :width_p]
    x_raw = projected[..., width_p:]
    device = lax.axis_index(("outc", "inc"))
    heads_group = HEADS // G
    group = device * heads_dev // heads_group
    x_history = jnp.concatenate(
        [
            conv_x_state.reshape(req_count, KW - 1, heads_dev * width_p),
            x_raw.reshape(req_count, DRAFT, heads_dev * width_p),
        ],
        axis=1,
    )
    bc_history = jnp.concatenate([conv_bc_state, bc_proj.reshape(req_count, DRAFT, -1)], axis=1)
    x_conv = jax.nn.silu(
        causal_conv(x_history, conv_x.reshape(KW, heads_dev * width_p), span_start)
    ).reshape(req_count, DRAFT, heads_dev, width_p)
    b_history = lax.dynamic_slice_in_dim(bc_history, group * width_n, width_n, 2)
    c_history = lax.dynamic_slice_in_dim(bc_history, (G + group) * width_n, width_n, 2)
    b_kernel = lax.dynamic_slice_in_dim(conv_bc, group * width_n, width_n, 1)
    c_kernel = lax.dynamic_slice_in_dim(conv_bc, (G + group) * width_n, width_n, 1)
    b_conv = jax.nn.silu(causal_conv(b_history, b_kernel, span_start))
    c_conv = jax.nn.silu(causal_conv(c_history, c_kernel, span_start))
    step_size = jax.nn.softplus(
        dt_proj.astype(jnp.float32).reshape(req_count, DRAFT, heads_dev) + dt_bias
    )
    cumulative = jnp.cumsum(-step_size * decay_rate, axis=1)
    positions = jnp.arange(DRAFT, dtype=jnp.int32)
    later = positions[None, :, None]
    earlier = positions[None, None, :]
    start_col = span_start[:, None, None]
    linked = (earlier <= later) & jnp.logical_not((earlier < start_col) & (start_col <= later))
    gap = cumulative[:, :, None, :] - cumulative[:, None, :, :]
    pair_decay = jnp.where(linked[..., None], jnp.exp(jnp.where(linked[..., None], gap, 0.0)), 0.0)
    scores = jnp.einsum("rtn,rqn->rtq", c_conv, b_conv, precision=lax.Precision.HIGHEST)
    mixing = pair_decay * (scores[..., None] * step_size[:, None, :, :])
    intra = jnp.einsum("rtqh,rqhp->rthp", mixing, x_conv, precision=lax.Precision.HIGHEST)
    prior = ssm_state.astype(jnp.float32)
    from_start = jnp.where(
        (positions[None, :] < span_start[:, None])[..., None], jnp.exp(cumulative), 0.0
    )
    carried = jnp.einsum("rhpn,rtn->rthp", prior, c_conv, precision=lax.Precision.HIGHEST)
    mixed = from_start[..., None] * carried + intra + skip_gain[None, None, :, None] * x_conv
    padded = jnp.concatenate(
        [jnp.zeros((req_count, 1, heads_dev), jnp.float32), cumulative], axis=1
    )
    pick_acc = (jnp.arange(DRAFT + 1, dtype=jnp.int32)[None, :] == accepted[:, None]).astype(
        jnp.float32
    )
    cum_acc = jnp.sum(pick_acc[..., None] * padded, axis=1)
    reset_before = span_start < accepted
    start_weight = jnp.where(reset_before[:, None], 0.0, jnp.exp(cum_acc))
    counted = (positions[None, :] < accepted[:, None]) & jnp.logical_not(
        (positions[None, :] < span_start[:, None]) & reset_before[:, None]
    )
    token_weight = (
        jnp.where(
            counted[..., None],
            jnp.exp(jnp.where(counted[..., None], cum_acc[:, None, :] - cumulative, 0.0)),
            0.0,
        )
        * step_size
    )
    added = jnp.einsum(
        "rqhp,rqn->rhpn", token_weight[..., None] * x_conv, b_conv, precision=lax.Precision.HIGHEST
    )
    new_state = (start_weight[:, :, None, None] * prior + added).astype(jnp.bfloat16)
    gated = mixed * jax.nn.silu(gate_raw.astype(jnp.float32))
    row_squares = jnp.sum(gated * gated, axis=(2, 3))
    selector = (jnp.arange(G, dtype=jnp.int32) == group).astype(jnp.float32)
    totals = lax.psum(row_squares[..., None] * selector, ("outc", "inc"))
    group_sq = jnp.sum(totals * selector, axis=-1)
    mean_sq = group_sq / (heads_group * width_p)
    normed = gated * lax.rsqrt(mean_sq + 1e-05)[:, :, None, None] * norm_gain
    normed = normed.astype(jnp.bfloat16).reshape(rows_all, heads_dev * width_p)
    head_block = lax.all_gather(normed, "inc", axis=1, tiled=True)
    output = lax.psum_scatter(
        jnp.dot(head_block, w_out, preferred_element_type=jnp.float32),
        "outc",
        scatter_dimension=0,
        tiled=True,
    ).astype(jnp.bfloat16)
    new_conv_x = conv_tail(x_history, span_start, accepted).reshape(
        req_count, KW - 1, heads_dev, width_p
    )
    new_conv_bc = conv_tail(bc_history, span_start, accepted)
    return (output, new_state, new_conv_x, new_conv_bc)


def solution(mesh):
    placed = (
        P(("groups", "outc"), "inc"),
        P("inc", "outc", None),
        P("inc", "outc"),
        P("inc", "outc"),
        P(None, ("outc", "inc"), None),
        P(),
        P(("outc", "inc")),
        P(("outc", "inc")),
        P(("outc", "inc")),
        P(("outc", "inc"), None),
        P("outc", "inc"),
        P("groups", None, ("outc", "inc"), None),
        P("groups", None, None),
        P("groups", ("outc", "inc"), None, None),
        P("groups"),
        P("groups"),
    )
    return jax.shard_map(
        shards,
        mesh=mesh,
        in_specs=placed,
        out_specs=(
            P(("groups", "outc"), "inc"),
            P("groups", ("outc", "inc"), None, None),
            P("groups", None, ("outc", "inc"), None),
            P("groups", None, None),
        ),
        check_vma=False,
    )
```

profile of v0, /device:TPU:0, one launch (start us, length us, event | category | flops | bytes accessed | tf_op | source)
XLA Modules:
  0.0 446.3 jit_solution(7683274469972079917)
XLA Ops:
  8.0 78.3 %all-gather.4.cloned.1.call-done = bf16[512,4096]{1,0:T(8,128)(2,1)} async-done(((bf16[64,4096]{1,0:T(8,128)(2,1)}), bf16[512,4096]{1,0:T(8,128)(2,1)}) %all-gather.4.cloned.1.call-update) | async-done | bytes 4194320 | tf_op jit(solution)/shard_map/all_gather | solution.py:66
  86.3 4.4 fusion.54
  90.8 4.0 fusion.53
  94.8 1.9 reduce-scatter.7.cloned.1.call-done
  96.8 1.5 convert_element_type.126
  98.4 17.2 %copy.201 = bf16[512,8,16,128]{3,1,2,0:T(8,128)(2,1)} copy(bf16[512,8,16,128]{3,2,1,0:T(8,128)(2,1)} %bitcast.70) | data formatting | bytes 33554432
  115.6 20.8 %copy.158 = bf16[2048,4096]{1,0:T(8,128)(2,1)} copy(bf16[2048,4096]{0,1:T(8,128)(2,1)} %bitcast.69) | data formatting | bytes 33554432 | tf_op jit(solution)/shard_map/dot_general | solution.py:69
  136.4 14.2 %fusion = f32[512,16,128]{2,0,1:T(8,128)} fusion(bf16[16,128,4096]{2,1,0:T(8,128)(2,1)} %bitcast.71, bf16[512,4096]{1,0:T(8,128)(2,1)} %all-gather.4.cloned.1.call-done), kind=kOutput, calls=%fused_computation.2 | convolution fusion | flops 8589934592 | bytes 25165824 | tf_op jit(solution)/shard_map/dot_general | solution.py:69
  156.3 1.4 reduce_window_sum.11
  160.6 1.7 copy.151
  163.7 1.3 fusion.55
  165.0 1.8 convert_element_type.135
  170.9 5.5 %fusion.9 = f32[64,8,64,8]{2,3,1,0:T(8,128)S(1)} fusion(f32[64,8,8,64]{3,2,1,0:T(8,128)S(1)} %reshape.566, f32[64,8,8]{1,2,0:T(8,128)} %copy.169, f32[64,8,8]{2,1,0:T(8,128)} %fusion.55, f32[64,8,8]{1,2,0:T(8,128)} %copy.167, pred[64,8,8]{2,1,0:T(8,128)(4,1)S(1)} %not_and_fusion), kind=kOutput, calls=%fused_computation.21 | convolution fusion | flops 25329664 | bytes 2150400 | tf_op jit(solution)/shard_map/rtqh,rqhp->rthp/dot_general | solution.py:124
  177.5 23.1 %multiply_reduce_fusion = (f32[64,8]{1,0:T(8,128)S(1)}, f32[64,8,8,64]{3,1,2,0:T(8,128)}) fusion(f32[64,8,8,64]{3,2,1,0:T(8,128)S(1)} %reshape.566, f32[8]{0:T(128)S(1)} %copy-done.23, f32[64,8,64,8]{2,3,1,0:T(8,128)S(1)} %fusion.9, bf16[64,8,64,128]{3,2,1,0:T(8,128)(2,1)} %param.29, f32[64,8,128]{2,1,0:T(8,128)S(1)} %copy-done.9, ...), kind=kOutput, calls=%fused_computation.20 | convolution fusion | flops 405798400 | bytes 12863520 | tf_op jit(solution)/shard_map/rhpn,rtn->rthp/dot_general | solution.py:129
  200.7 62.1 %psum.7 = f32[64,8,4]{0,1,2:T(8,128)S(1)} all-reduce(f32[64,8,4]{0,1,2:T(8,128)S(1)} %broadcast_multiply_fusion.1), channel_id=1, replica_groups=mesh['groups'=2,'outc'=8,'inc'=2] {'outc','inc'}, use_global_device_ids=true, to_apply=%region_5.6 | all-reduce | flops 2048 | bytes 16384 | tf_op jit(solution)/shard_map/psum | solution.py:158
  263.0 1.9 multiply_convert_fusion
  266.2 2.6 reshape.567
  268.8 6.4 %all-gather.8.cloned.1.call-done = bf16[512,1024]{1,0:T(8,128)(2,1)} async-done(((bf16[512,512]{1,0:T(8,128)(2,1)}), bf16[512,1024]{1,0:T(8,128)(2,1)}) %all-gather.8.cloned.1.call-update) | async-done | bytes 1048592 | tf_op jit(solution)/shard_map/all_gather | solution.py:163
  275.2 11.5 %fusion.56 = f32[512,4096]{1,0:T(8,128)} fusion(bf16[512,1024]{1,0:T(8,128)(2,1)} %all-gather.8.cloned.1.call-done, bf16[1024,4096]{1,0:T(8,128)(2,1)} %param.26), kind=kOutput, calls=%fused_computation.114 | convolution fusion | flops 4294967296 | bytes 17825792 | tf_op jit(solution)/shard_map/dot_general | solution.py:165
  287.0 1.8 copy.178
  288.8 2.0 fusion.18
  294.1 32.6 %add_convert_fusion = bf16[64,8,64,128]{3,2,1,0:T(8,128)(2,1)} fusion(bf16[64,8,64,128]{3,2,1,0:T(8,128)(2,1)} %param.29, f32[64,8]{1,0:T(8,128)S(1)} %copy.176, f32[64,8,8,64]{3,2,1,0:T(8,128)S(1)} %broadcast_multiply_fusion, f32[64,8,128]{2,1,0:T(8,128)S(1)} %divide_multiply_fusion.1), kind=kOutput, calls=%fused_computation.1 | convolution fusion | flops 419430400 | bytes 18089984 | tf_op jit(solution)/shard_map/rqhp,rqn->rhpn/dot_general | solution.py:151
  326.7 110.3 %reduce-scatter.11.cloned.1.call-done = f32[64,4096]{1,0:T(8,128)} async-done(((f32[512,4096]{1,0:T(8,128)}), f32[64,4096]{1,0:T(8,128)}) %reduce-scatter.11.cloned.1.call-update) | async-done | bytes 1048592 | tf_op jit(solution)/shard_map/reduce_scatter | solution.py:164
  437.0 2.1 convert_element_type.147
  (124 shorter events, 21.0 us)
Async XLA Ops:
  7.2 79.1 %copy-start = (bf16[4096,128]{1,0:T(8,128)(2,1)S(1)}, bf16[4096,128]{1,0:T(8,128)(2,1)}, u32[]{:S(2)}) copy-start(bf16[4096,128]{1,0:T(8,128)(2,1)} %param.19) | copy-start | bytes 3145732
  7.2 79.1 %all-gather.4.cloned.1.call-start = ((), (), s32[]{:S(2)}) async-start(), calls=%async_computation.4 | async-start | bytes 4718592 | tf_op jit(solution)/shard_map/all_gather | solution.py:66
  7.9 82.8 %copy-start.16 = (bf16[4096,16]{0,1:T(8,128)(2,1)S(1)}, bf16[4096,16]{0,1:T(8,128)(2,1)}, u32[]{:S(2)}) copy-start(bf16[4096,16]{0,1:T(8,128)(2,1)} %param.18) | copy-start | bytes 393220
  7.9 88.8 %reduce-scatter.7.cloned.1.call-start = ((), (), s32[]{:S(2)}) async-start(), calls=%async_computation.6 | async-start | bytes 393216 | tf_op jit(solution)/shard_map/reduce_scatter | solution.py:82
  90.7 63.6 %reduce-scatter.5.cloned.1.call-start = ((), (), s32[]{:S(2)}) async-start(), calls=%async_computation.5 | async-start | bytes 49152 | tf_op jit(solution)/shard_map/reduce_scatter | solution.py:81
  94.8 65.8 %all-gather.6.cloned.1.call-start = ((), (), s32[]{:S(2)}) async-start(), calls=%async_computation.7 | async-start | bytes 1114112 | tf_op jit(solution)/shard_map/all_gather | solution.py:86
  98.3 66.6 %reduce-scatter.9.cloned.1.call-start = ((), (), s32[]{:S(2)}) async-start(), calls=%async_computation.8 | async-start | bytes 6291456 | tf_op jit(solution)/shard_map/reduce_scatter | solution.py:80
  150.6 1.3 copy-start.20
  150.6 1.5 copy-start.17
  150.6 2.1 copy-start.13
  150.6 4.6 %copy-start.21 = (f32[8]{0:T(128)S(1)}, f32[8]{0:T(128)}, u32[]{:S(2)}) copy-start(f32[8]{0:T(128)} %param.23) | copy-start | bytes 100
  150.6 4.6 %copy-start.22 = (f32[8]{0:T(128)S(1)}, f32[8]{0:T(128)}, u32[]{:S(2)}) copy-start(f32[8]{0:T(128)} %param.22) | copy-start | bytes 100
  150.6 124.5 %all-gather.8.cloned.1.call-start = ((), (), s32[]{:S(2)}) async-start(), calls=%async_computation.9 | async-start | bytes 1572864 | tf_op jit(solution)/shard_map/all_gather | solution.py:163
  151.9 16.5 %copy-start.10 = (bf16[64,3,512]{2,1,0:T(4,128)(2,1)}, bf16[64,3,512]{2,1,0:T(4,128)(2,1)S(1)}, u32[]{:S(2)}) copy-start(bf16[64,3,512]{2,1,0:T(4,128)(2,1)S(1)} %reshape.574) | copy-start | bytes 589828
  153.0 9.2 %copy-start.5 = (bf16[64,3,1024]{2,1,0:T(4,128)(2,1)}, bf16[64,3,1024]{2,1,0:T(4,128)(2,1)S(1)}, u32[]{:S(2)}) copy-start(bf16[64,3,1024]{2,1,0:T(4,128)(2,1)S(1)} %copy.152) | copy-start | bytes 1179652
  162.3 2.7 copy-start.3
  170.9 5.5 %copy-start.2 = (f32[512,8,128]{2,0,1:T(8,128)S(1)}, f32[512,8,128]{2,0,1:T(8,128)}, u32[]{:S(2)}) copy-start(f32[512,8,128]{2,0,1:T(8,128)} %reduce-scatter.9.cloned.1.call-done) | copy-start | bytes 6291460
  177.5 85.5 %copy-start.19 = (f32[8,64]{1,0:T(8,128)S(1)}, f32[8,64]{1,0:T(8,128)}, u32[]{:S(2)}) copy-start(f32[8,64]{1,0:T(8,128)} %param.25) | copy-start | bytes 6148
  268.7 168.2 %reduce-scatter.11.cloned.1.call-start = ((), (), s32[]{:S(2)}) async-start(), calls=%async_computation.10 | async-start | bytes 9437184 | tf_op jit(solution)/shard_map/reduce_scatter | solution.py:164
  286.7 2.2 copy-start.4
  288.8 2.9 copy-start.7
  288.8 2.9 copy-start.11
  290.8 2.6 copy-start.12
  294.0 145.0 %copy-start.1 = (bf16[4096,128]{1,0:T(8,128)(2,1)S(1)}, bf16[4096,128]{1,0:T(8,128)(2,1)}, u32[]{:S(2)}) copy-start(bf16[4096,128]{1,0:T(8,128)(2,1)} %param.19) | copy-start | bytes 3145732
  (7 other events, 6.8 us)
Sparse Core Ops, SparseCore 0:
  10.1 76.0 all-gather.3
  90.8 5.9 reduce-scatter.6
  99.6 8.6 reduce-scatter.4
  111.1 39.0 all-gather.5
  153.1 11.1 reduce-scatter.8
  268.9 6.2 all-gather.7
  286.8 150.1 reduce-scatter.10
where the time goes:
time: 452 us; the launch traced here: 446 us
  waiting for transfers between devices  198 us (44%)
  matrix products  99.1 us (22%)
  blocking collectives  62.1 us (14%)
  local copies, waits for them, and re-layouts  57.6 us (13%)
  between operations  15 us (3%)
  other arithmetic  14.4 us (3%)
    reduce_scatter x1, waiting for transfers between devices, shards(): lax.psum_scatter(jnp.dot(head_block, w_out, preferred_element_type=jnp.fl...  110 us
    all_gather x1, waiting for transfers between devices, shards(): piece = lax.all_gather(tokens, 'outc', axis=0, tiled=True)  78.3 us
    psum x1, blocking collectives, shards(): totals = lax.psum(row_squares[..., None] * selector, ('outc', 'inc'))  62.1 us
    dot_general x1, matrix products, shards(): jnp.einsum('rqhp,rqn->rhpn', token_weight[..., None] * x_conv, b_conv, pr...  32.6 us
    dot_general x1, matrix products, shards(): jnp.einsum('rhpn,rtn->rthp', prior, c_conv, precision=lax.Precision.HIGHEST)  23.1 us
    unnamed x52, local copies, waits for them, and re-layouts  22 us
    dot_general x1, local copies, waits for them, and re-layouts, shards(): jnp.dot(piece, zx_flat, preferred_element_type=jnp.float32)  20.8 us
    dot_general x1, matrix products, shards(): jnp.dot(piece, zx_flat, preferred_element_type=jnp.float32)  14.2 us
  transfers between devices with their start and end apart: 7, of which 4 were waited for; matrix products, arithmetic and copies ran while one was open for 25% of the time, Pallas kernels for 0%

commit v1 on v0

v1 whole, which is shorter than its diff:
```python
import functools

import jax
import jax.numpy as jnp
from jax import lax
from jax.experimental import pallas as pl
from jax.experimental.pallas import tpu as pltpu
from jax.sharding import PartitionSpec as P

HEADS = 128
G = 4
KW = 4
DRAFT = 8
LANES = 128
BF = jnp.bfloat16
F32 = jnp.float32
HIGH = lax.Precision.HIGHEST
NT = (((1,), (1,)), ((), ()))
TN = (((0,), (0,)), ((), ()))
MIB = 1 << 20


def params(mib):
    return pltpu.CompilerParams(vmem_limit_bytes=mib * MIB)


def cost(flops, nbytes):
    return pl.CostEstimate(flops=int(flops), bytes_accessed=int(nbytes), transcendentals=0)


def whole_block(shape):
    return pl.BlockSpec(shape, lambda *_: (0,) * len(shape))


def relayout_kernel(heads, w_ref, o_ref, perm):
    kb = 256 // heads

    @pl.when(pl.program_id(0) == 0)
    def _():
        r = lax.broadcasted_iota(jnp.int32, (256, 256), 0)
        c = lax.broadcasted_iota(jnp.int32, (256, 256), 1)
        hit = (r // kb == lax.rem(c, heads)) & (lax.rem(r, kb) == c // heads)
        perm[...] = jnp.where(hit, 1.0, 0.0).astype(BF)

    bk = w_ref.shape[0]
    half = heads // 2
    for i in range(0, bk // kb, 2):
        first = w_ref[i * kb : (i + 1) * kb].reshape(256, LANES)
        second = w_ref[(i + 1) * kb : (i + 2) * kb].reshape(256, LANES)
        both = jnp.concatenate([first, second], axis=1)
        out = jnp.dot(perm[...], both, preferred_element_type=F32).astype(BF)
        for u in range(2):
            for h in range(heads):
                at = (h % half) * LANES
                o_ref[h // half, (i + u) * kb : (i + u + 1) * kb, at : at + LANES] = out[
                    h * kb : (h + 1) * kb, u * LANES : (u + 1) * LANES
                ]


def relayout(w_zx, bk=128):
    k, heads, width = w_zx.shape
    cols = heads // 2 * width
    return pl.pallas_call(
        functools.partial(relayout_kernel, heads),
        grid=(k // bk,),
        in_specs=[pl.BlockSpec((bk, heads, width), lambda i: (i, 0, 0))],
        out_specs=pl.BlockSpec((2, bk, cols), lambda i: (0, i, 0)),
        out_shape=jax.ShapeDtypeStruct((2, k, cols), BF),
        scratch_shapes=[pltpu.VMEM((256, 256), BF)],
        compiler_params=params(24),
        cost_estimate=cost(2 * k * heads * width * 256, 4 * k * heads * width),
        name="relayout",
    )(w_zx)


def gather_kernel(n, at_ref, own_ref, w_ref, *rest):
    ups, downs = rest[: n - 1], rest[n - 1 : 2 * (n - 1)]
    rows_ref, keep_ref, send_ref = rest[2 * (n - 1) :]
    rc, width = own_ref.shape
    half = width // 2

    def at(i):
        return pl.ds(pl.multiple_of(at_ref[i] * rc, 16), rc)

    rows_ref[at(0), :] = own_ref[...]
    for s in range(1, n):
        rows_ref[at(s), :half] = ups[s - 1][...]
        rows_ref[at(n + s), half:] = downs[s - 1][...]
    total = jnp.dot(rows_ref[...], w_ref[...], preferred_element_type=F32)
    keep_ref[...] = total
    send_ref[...] = total.astype(BF)


def gather_rows(owners, own, w_ext, ups, downs):
    n = len(ups) + 1
    rc, width = own.shape
    rows, cols = n * rc, w_ext.shape[1]
    arrays = [own, w_ext, *ups, *downs]
    return pl.pallas_call(
        functools.partial(gather_kernel, n),
        grid_spec=pltpu.PrefetchScalarGridSpec(
            num_scalar_prefetch=1,
            grid=(1,),
            in_specs=[whole_block(a.shape) for a in arrays],
            out_specs=[
                whole_block((rows, width)),
                whole_block((rows, cols)),
                whole_block((rows, cols)),
            ],
        ),
        out_shape=[
            jax.ShapeDtypeStruct((rows, width), BF),
            jax.ShapeDtypeStruct((rows, cols), F32),
            jax.ShapeDtypeStruct((rows, cols), BF),
        ],
        compiler_params=params(40),
        cost_estimate=cost(2 * rows * width * cols, 4 * rows * width + 2 * width * cols),
        name="gather_rows",
    )(owners, *arrays)


def project_kernel(which_ref, rows_ref, w_ref, o_ref):
    o_ref[...] = jnp.dot(rows_ref[...], w_ref[0], preferred_element_type=F32).astype(o_ref.dtype)


def project(which, rows, w, dtype, bn=256):
    m, k = rows.shape
    cols = w.shape[2]
    return pl.pallas_call(
        project_kernel,
        grid_spec=pltpu.PrefetchScalarGridSpec(
            num_scalar_prefetch=1,
            grid=(cols // bn,),
            in_specs=[
                pl.BlockSpec((m, k), lambda j, which: (0, 0)),
                pl.BlockSpec((1, k, bn), lambda j, which: (which[0], 0, j)),
            ],
            out_specs=pl.BlockSpec((m, bn), lambda j, which: (0, j)),
        ),
        out_shape=jax.ShapeDtypeStruct((m, cols), dtype),
        compiler_params=params(40),
        cost_estimate=cost(2 * m * k * cols, 2 * k * cols + 2 * m * k),
        name="project",
    )(which, rows, w)


def silu(v):
    return v / (1.0 + jnp.exp(-v))


def ssm_kernel(
    meta_ref, recv_ref, mine_ref, dt_ref, braw_ref, craw_ref, own_ref, prevx_ref, prevb_ref, prevc_ref,
    prevo_ref, tapx_ref, tapb_ref, tapc_ref, bias_ref, rate_ref, skip_ref, gain_ref, state_ref,
    gated_ref, ssq_ref, xw_ref, bconv_ref, sw_ref, xraw_ref, tail_ref,
):
    rb = recv_ref.shape[0]
    hp = gated_ref.shape[1]
    pairs = hp // LANES
    ss = meta_ref[..., 0:1].reshape(rb, 1)
    acc = meta_ref[..., 1:2].reshape(rb, 1)
    t = lax.broadcasted_iota(jnp.int32, (rb, 1), 0) & (DRAFT - 1)
    low = lax.broadcasted_iota(jnp.int32, (rb, LANES), 1) < LANES // 2
    seen = [
        jnp.where((t < ss) | (t - d >= ss), 1.0, 0.0).reshape(rb // DRAFT, DRAFT, 1) for d in range(KW)
    ]
    t3 = t.reshape(rb // DRAFT, DRAFT, 1)

    def conv(x, prev, taps):
        width = x.shape[1]
        x3 = x.reshape(rb // DRAFT, DRAFT, width)
        p3 = prev.reshape(rb // DRAFT, DRAFT, width)
        total = x3 * taps[KW - 1 : KW, :].reshape(1, 1, width)
        for d in range(1, KW):
            source = jnp.where(t3 >= d, pltpu.roll(x3, d, 1), pltpu.roll(p3, d, 1))
            total = total + (source * seen[d]) * taps[KW - 1 - d : KW - d, :].reshape(1, 1, width)
        return silu(total).reshape(rb, width)

    zx = (mine_ref[...].astype(F32) + recv_ref[...].astype(F32)).astype(BF).astype(F32)
    gates, xs = [], []
    for j in range(pairs):
        a = zx[:, 2 * j * LANES : (2 * j + 1) * LANES]
        b = zx[:, (2 * j + 1) * LANES : (2 * j + 2) * LANES]
        gates.append(jnp.where(low, a, pltpu.roll(b, LANES // 2, 1)))
        xs.append(jnp.where(low, pltpu.roll(a, LANES // 2, 1), b))
    prev_x = prevx_ref[...].reshape(rb, hp).astype(F32)
    convs = []
    for j in range(pairs):
        cut = slice(j * LANES, (j + 1) * LANES)
        xraw_ref[:, cut] = xs[j].astype(BF)
        convs.append(conv(xs[j], prev_x[:, cut], tapx_ref[:, cut]))
    b_conv = conv(braw_ref[...].astype(F32), prevb_ref[...].reshape(rb, LANES).astype(F32), tapb_ref[...])
    c_conv = conv(craw_ref[...].astype(F32), prevc_ref[...].reshape(rb, LANES).astype(F32), tapc_ref[...])
    bconv_ref[...] = b_conv.astype(BF)

    raw = dt_ref[...].astype(F32) + bias_ref[...]
    step = jnp.maximum(raw, 0.0) + jnp.log1p(jnp.exp(-jnp.abs(raw)))
    log_a = -step * rate_ref[...]
    ri = lax.broadcasted_iota(jnp.int32, (rb, rb), 0)
    ci = lax.broadcasted_iota(jnp.int32, (rb, rb), 1)
    same = (ri // DRAFT) == (ci // DRAFT)
    tt, tq = ri & (DRAFT - 1), ci & (DRAFT - 1)
    lower = same & (tq <= tt)
    linked = lower & jnp.logical_not((tq < ss) & (ss <= tt))
    cum = jnp.dot(jnp.where(lower, 1.0, 0.0), log_a, precision=HIGH, preferred_element_type=F32)
    cum_acc = jnp.dot(
        jnp.where(same & (tq < acc), 1.0, 0.0), log_a, precision=HIGH, preferred_element_type=F32
    )
    cum_t = cum.T
    step_t = step.T
    scores = lax.dot_general(c_conv, b_conv, NT, precision=HIGH, preferred_element_type=F32)

    def spread(v, j):
        return jnp.where(low, v[:, 2 * j : 2 * j + 1], v[:, 2 * j + 1 : 2 * j + 2])

    odd = (lax.broadcasted_iota(jnp.int32, (rb, 1), 0) & DRAFT) != 0
    c_pair = jnp.concatenate(
        [jnp.where(odd, 0.0, c_conv).astype(BF), jnp.where(odd, c_conv, 0.0).astype(BF)], axis=1
    )
    state = state_ref[...].reshape(rb // DRAFT, hp, LANES)
    carried = []
    for i in range(rb // (2 * DRAFT)):
        both = jnp.concatenate([state[2 * i], state[2 * i + 1]], axis=1)
        carried.append(
            lax.dot_general(
                c_pair[2 * DRAFT * i : 2 * DRAFT * (i + 1)], both, NT, preferred_element_type=F32
            )
        )
    carried = jnp.concatenate(carried, axis=0)

    kept = jnp.where(t < ss, jnp.exp(cum), 0.0)
    counted = (t < acc) & jnp.logical_not((t < ss) & (ss < acc))
    weight = jnp.where(counted, jnp.exp(jnp.where(counted, cum_acc - cum, 0.0)), 0.0) * step
    sw_ref[...] = jnp.where(ss < acc, 0.0, jnp.exp(cum_acc))
    squares = jnp.zeros((rb, LANES), F32)
    for j in range(pairs):
        cut = slice(j * LANES, (j + 1) * LANES)
        mixes = []
        for h in (2 * j, 2 * j + 1):
            gap = cum[:, h : h + 1] - cum_t[h : h + 1, :]
            mixes.append((jnp.exp(jnp.where(linked, gap, -1e30)) * (scores * step_t[h : h + 1, :])).astype(BF))
        x_conv = convs[j]
        x_pair = jnp.concatenate(
            [jnp.where(low, x_conv, 0.0).astype(BF), jnp.where(low, 0.0, x_conv).astype(BF)], axis=0
        )
        intra = jnp.dot(jnp.concatenate(mixes, axis=1), x_pair, preferred_element_type=F32)
        mixed = spread(kept, j) * carried[:, cut] + intra + skip_ref[:, cut] * x_conv
        gated = mixed * silu(gates[j])
        squares = squares + gated * gated
        gated_ref[:, cut] = (gated * gain_ref[:, cut]).astype(BF)
        xw_ref[:, cut] = (spread(weight, j) * x_conv).astype(BF)
    row_sum = jnp.broadcast_to(jnp.sum(squares, axis=1, keepdims=True), (rb, LANES))
    ssq_ref[...] = row_sum.T[:8]

    tail_ref[...] = pick_tail(ss, acc, own_ref[...], prevo_ref[...].reshape(own_ref.shape)).astype(BF)


def pick_tail(ss, acc, raw, prev):
    rb = raw.shape[0]
    ri = lax.broadcasted_iota(jnp.int32, (rb, rb), 0)
    ci = lax.broadcasted_iota(jnp.int32, (rb, rb), 1)
    same = (ri // DRAFT) == (ci // DRAFT)
    j, q = ri & (DRAFT - 1), ci & (DRAFT - 1)
    source = acc + j - (KW - 1)
    live = same & (j < KW - 1) & jnp.logical_not((source < ss) & (ss < acc))
    new = jnp.where(live & (q == source), 1.0, 0.0).astype(BF)
    old = jnp.where(live & (q == source + DRAFT), 1.0, 0.0).astype(BF)
    return jnp.dot(new, raw.astype(BF), preferred_element_type=F32) + jnp.dot(
        old, prev.astype(BF), preferred_element_type=F32
    )


def ssm(chunk, rb, per_row, tables, state):
    rows = per_row[1].shape[0]
    n, _, rq, hp, width_n = state.shape
    rc = rq * DRAFT
    ob = rb // rc
    cw = per_row[6].shape[1]

    def row_spec(a):
        if a.ndim == 2:
            return pl.BlockSpec((rb, a.shape[1]), lambda i: (i, 0))
        return pl.BlockSpec((ob, 1, rc, a.shape[3]), lambda i: (i, chunk, 0, 0))

    def flat(w):
        return pl.BlockSpec((rb, w), lambda i: (i, 0))

    return pl.pallas_call(
        ssm_kernel,
        grid=(rows // rb,),
        in_specs=[row_spec(a) for a in per_row]
        + [whole_block(a.shape) for a in tables]
        + [pl.BlockSpec((ob, 1, rq, hp, width_n), lambda i: (i, chunk, 0, 0, 0))],
        out_specs=[
            flat(hp),
            pl.BlockSpec((8, rb), lambda i: (0, i)),
            flat(hp),
            flat(LANES),
            flat(LANES),
            flat(hp),
            flat(cw),
        ],
        out_shape=[
            jax.ShapeDtypeStruct((rows, hp), BF),
            jax.ShapeDtypeStruct((8, rows), F32),
            jax.ShapeDtypeStruct((rows, hp), BF),
            jax.ShapeDtypeStruct((rows, LANES), BF),
            jax.ShapeDtypeStruct((rows, LANES), F32),
            jax.ShapeDtypeStruct((rows, hp), BF),
            jax.ShapeDtypeStruct((rows, cw), BF),
        ],
        compiler_params=params(40),
        cost_estimate=cost(2 * rows * hp * 4096, 6 * rows * hp * 16),
        name="ssm",
    )(*per_row, *tables, state)


def state_kernel(meta_ref, xw_ref, bconv_ref, sw_ref, xraw_ref, prevx_ref, state_ref, o_ref, tail_ref):
    rb, hp = xw_ref.shape
    width_p = LANES // 2
    ss = meta_ref[..., 0:1].reshape(rb, 1)
    acc = meta_ref[..., 1:2].reshape(rb, 1)
    tail_ref[...] = pick_tail(ss, acc, xraw_ref[...], prevx_ref[...].reshape(rb, hp)).astype(BF)
    request = lax.broadcasted_iota(jnp.int32, (rb, 1), 0) // DRAFT
    b_conv = bconv_ref[...].astype(F32)
    xw_t = xw_ref[...].astype(F32).T.astype(BF)
    rq = state_ref.shape[2]
    sw = sw_ref[...]
    for i in range(0, rb // DRAFT, 2):
        both = jnp.concatenate(
            [jnp.where(request == i + u, b_conv, 0.0).astype(BF) for u in range(2)], axis=1
        )
        added = jnp.dot(xw_t, both, preferred_element_type=F32)
        for u in range(2):
            r = i + u
            for h in range(hp // width_p):
                cut = slice(h * width_p, (h + 1) * width_p)
                old = state_ref[r // rq, 0, r % rq, cut, :].astype(F32)
                new = sw[r * DRAFT : r * DRAFT + 1, h : h + 1] * old + added[cut, u * LANES : (u + 1) * LANES]
                o_ref[r // rq, 0, r % rq, cut, :] = new.astype(BF)


def new_state(chunk, rb, meta, xw, bconv, sw, xraw, prev_x, state, into):
    rows, hp = xw.shape
    n, _, rq, _, width_n = state.shape
    rc = rq * DRAFT
    ob = rb // rc

    def four(w):
        return pl.BlockSpec((ob, 1, rc, w), lambda i: (i, chunk, 0, 0))

    def flat(w):
        return pl.BlockSpec((rb, w), lambda i: (i, 0))

    states = pl.BlockSpec((ob, 1, rq, hp, width_n), lambda i: (i, chunk, 0, 0, 0))
    args = [meta, xw, bconv, sw, xraw, prev_x, state]
    specs = [four(2), flat(hp), flat(LANES), flat(LANES), flat(hp), four(hp), states]
    kernel, aliases = state_kernel, {}
    if into is not None:
        args.append(into)
        specs.append(pl.BlockSpec(memory_space=pl.ANY))
        aliases = {7: 0}

        def kernel(*refs):
            return state_kernel(*refs[:7], *refs[8:])

    return pl.pallas_call(
        kernel,
        grid=(rows // rb,),
        in_specs=specs,
        out_specs=[states, flat(hp)],
        out_shape=[jax.ShapeDtypeStruct(state.shape, BF), jax.ShapeDtypeStruct((rows, hp), BF)],
        input_output_aliases=aliases,
        compiler_params=params(40),
        cost_estimate=cost(2 * rows * hp * 4096, 8 * rows * hp * 16),
        name="new_state",
    )(*args)


def out_kernel(scale_by, inc_ref, mine_ref, theirs_ref, w_mine_ref, w_theirs_ref, ssq_ref, o_ref):
    product = jnp.dot(mine_ref[...], w_mine_ref[...], preferred_element_type=F32) + jnp.dot(
        theirs_ref[...], w_theirs_ref[...], preferred_element_type=F32
    )
    scale = lax.rsqrt(ssq_ref[...] * scale_by + 1e-05)
    rows = scale.shape[1]
    column = jnp.broadcast_to(scale[0:1], (LANES, rows)).T[:, 0:1]
    o_ref[...] = (product * column).astype(o_ref.dtype)


def out_project(inc, mine, theirs, w_out, ssq, scale_by, bn=512):
    rows, hp = mine.shape
    cols = w_out.shape[1]
    return pl.pallas_call(
        functools.partial(out_kernel, scale_by),
        grid_spec=pltpu.PrefetchScalarGridSpec(
            num_scalar_prefetch=1,
            grid=(cols // bn,),
            in_specs=[
                pl.BlockSpec((rows, hp), lambda j, inc: (0, 0)),
                pl.BlockSpec((rows, hp), lambda j, inc: (0, 0)),
                pl.BlockSpec((hp, bn), lambda j, inc: (inc[0], j)),
                pl.BlockSpec((hp, bn), lambda j, inc: (1 - inc[0], j)),
                pl.BlockSpec((8, rows), lambda j, inc: (0, 0)),
            ],
            out_specs=pl.BlockSpec((rows, bn), lambda j, inc: (0, j)),
        ),
        out_shape=jax.ShapeDtypeStruct((rows, cols), F32),
        compiler_params=params(40),
        cost_estimate=cost(4 * rows * hp * cols, 4 * hp * cols + 4 * rows * cols),
        name="out_project",
    )(inc, mine, theirs, w_out, w_out, ssq)


def shards(n, chunks, tokens, w_zx, w_dt, w_bc, conv_x, conv_bc, dt_bias, decay_rate, skip_gain, norm_gain,
           w_out, conv_x_state, conv_bc_state, ssm_state, span_start, accepted):
    req, hd, width_p, width_n = ssm_state.shape
    hp = hd * width_p
    block_rows, half_d = tokens.shape
    cw = w_bc.shape[1]
    rc = block_rows // chunks
    rq = rc // DRAFT
    rows = n * rc
    rb = min(128, rows)
    order = list(range(0, n, 2)) + list(range(n - 1, 0, -2))
    place = [order.index(i) for i in range(n)]
    up = [(order[i], order[(i + 1) % n]) for i in range(n)]
    down = [(b, a) for a, b in up]
    swap = [(0, 1), (1, 0)]
    me = lax.axis_index("outc")
    inc = lax.axis_index("inc")
    pos = jnp.array(place, jnp.int32)[me]
    order_a = jnp.array(order, jnp.int32)
    steps = jnp.arange(n, dtype=jnp.int32)
    above = order_a[(pos - steps) % n]
    below = order_a[(pos + steps) % n]
    owners = jnp.concatenate([above, below])
    inc1 = inc.astype(jnp.int32).reshape(1)

    def other(a):
        return lax.ppermute(a, "inc", swap)

    member = n // G
    group = me // member
    seat = me % member
    w_ext = jnp.concatenate([w_bc, w_dt, jnp.zeros((half_d, LANES - w_dt.shape[1]), BF)], axis=1)
    if w_ext.shape[1] % LANES:
        w_ext = jnp.pad(w_ext, ((0, 0), (0, LANES - w_ext.shape[1] % LANES)))

    def history(a):
        a = a.reshape(req, KW - 1, -1)
        a = jnp.pad(a, ((0, 0), (DRAFT - KW + 1, 0), (0, 0)))
        return a.reshape(n, chunks, rc, a.shape[-1])

    def columns(a, start, size):
        return lax.dynamic_slice_in_dim(a, start, size, a.ndim - 1)

    prev_x = history(conv_x_state)
    prev_b = history(columns(conv_bc_state, group * width_n, width_n))
    prev_c = history(columns(conv_bc_state, (G + group) * width_n, width_n))
    prev_own = history(columns(conv_bc_state, me * cw, cw))
    meta = jnp.stack([span_start, accepted], axis=-1).astype(jnp.int32)
    meta = jnp.broadcast_to(meta[:, None, :], (req, DRAFT, 2)).reshape(n, chunks, rc, 2)

    def lanes(v):
        return jnp.pad(v, (0, LANES - hd)).reshape(1, LANES)

    tables = [
        conv_x.reshape(KW, hp),
        columns(conv_bc, group * width_n, width_n),
        columns(conv_bc, (G + group) * width_n, width_n),
        lanes(dt_bias),
        lanes(decay_rate),
        jnp.repeat(skip_gain, width_p).reshape(1, hp),
        norm_gain.reshape(1, hp),
    ]
    state = ssm_state.reshape(n, chunks, rq, hp, width_n)
    w = relayout(w_zx)
    scale_by = 1.0 / (HEADS // G * width_p)

    halves = []
    for c in range(chunks):
        own = tokens[c * rc : (c + 1) * rc]
        a, b = own[:, : half_d // 2], own[:, half_d // 2 :]
        ups, downs = [], []
        for s in range(n - 1):
            a = lax.ppermute(a, "outc", up)
            b = lax.ppermute(b, "outc", down)
            ups.append(a)
            downs.append(b)
        halves.append((own, ups, downs))

    outs, tails_x, tails_bc = [], [], []
    into = None
    for c in range(chunks):
        own, ups, downs = halves[c]
        rows_all, ext_keep, ext_send = gather_rows(owners, own, w_ext, ups, downs)
        ext = (ext_keep + other(ext_send).astype(F32)).astype(BF)
        bc_own = ext[:, :cw]
        dt = columns(ext[:, cw : cw + 2 * hd], inc * hd, hd)
        dt = jnp.pad(dt, ((0, 0), (0, LANES - hd)))
        got = []
        for k in range(member):
            pairs = []
            for g in range(G):
                width = member // 2
                sources = [g * width + i for i in range(width)] + [n // 2 + g * width + i for i in range(width)]
                for i in range(member):
                    pairs.append((sources[(i + k) % member], g * member + i))
            got.append(lax.ppermute(bc_own, "outc", pairs))
        pieces = []
        for i in range(member):
            piece = got[0]
            for k in range(1, member):
                piece = jnp.where((i - seat) % member == k, got[k], piece)
            pieces.append(piece)
        b_raw = jnp.concatenate(pieces[: member // 2], axis=1)
        c_raw = jnp.concatenate(pieces[member // 2 :], axis=1)
        theirs = other(project(1 - inc1, rows_all, w, BF))
        mine = project(inc1, rows_all, w, F32)
        gated, ssq, xw, bconv, sw, xraw, tail = ssm(
            c, rb, [meta, theirs, mine, dt, b_raw, c_raw, bc_own, prev_x, prev_b, prev_c, prev_own], tables, state
        )
        tails_bc.append(tail)
        gated_theirs = other(gated)
        ssq = ssq + other(ssq)
        d = 1
        while d < member:
            ssq = ssq + lax.ppermute(ssq, "outc", [(i, i ^ d) for i in range(n)])
            d *= 2
        partial = out_project(inc1, gated, gated_theirs, w_out, ssq, scale_by)
        half = partial.shape[1] // 2

        def part(i, side):
            owner = owners[i]
            return lax.dynamic_slice(partial, (owner * rc, side * half), (rc, half))

        p = part(1, 0).astype(BF)
        q = part(n + 1, 1).astype(BF)
        for s in range(n - 1):
            p = (lax.ppermute(p, "outc", up).astype(F32) + part((s + 2) % n, 0)).astype(BF)
            q = (lax.ppermute(q, "outc", down).astype(F32) + part(n + (s + 2) % n, 1)).astype(BF)
        outs.append(jnp.concatenate([p, q], axis=1))
        into, tail_x = new_state(c, rb, meta, xw, bconv, sw, xraw, prev_x, state, into)
        tails_x.append(tail_x)

    def tails(parts):
        a = jnp.stack([x.reshape(n, rq, DRAFT, x.shape[1]) for x in parts], axis=1)
        return a.reshape(req, DRAFT, a.shape[-1])[:, : KW - 1]

    new_x = tails(tails_x).reshape(req, KW - 1, hd, width_p)
    new_bc = lax.all_gather(tails(tails_bc), "outc", axis=2, tiled=True)
    return jnp.concatenate(outs, axis=0), into.reshape(ssm_state.shape), new_x, new_bc


def solution(mesh):
    n = mesh.shape["outc"]
    placed = (
        P(("groups", "outc"), "inc"),
        P("inc", "outc", None),
        P("inc", "outc"),
        P("inc", "outc"),
        P(None, ("outc", "inc"), None),
        P(),
        P(("outc", "inc")),
        P(("outc", "inc")),
        P(("outc", "inc")),
        P(("outc", "inc"), None),
        P("outc", "inc"),
        P("groups", None, ("outc", "inc"), None),
        P("groups", None, None),
        P("groups", ("outc", "inc"), None, None),
        P("groups"),
        P("groups"),
    )
    return jax.shard_map(
        functools.partial(shards, n, 2),
        mesh=mesh,
        in_specs=placed,
        out_specs=(
            P(("groups", "outc"), "inc"),
            P("groups", ("outc", "inc"), None, None),
            P("groups", None, ("outc", "inc"), None),
            P("groups", None, None),
        ),
        check_vma=False,
    )
```

time: 452 us -> 262 us (0.58)
  waiting for transfers between devices: 198 us -> 22.6 us
  matrix products: 99.1 us -> 0 us
  starting transfers between devices: 0.46 us -> 76.2 us
  Pallas kernels: 0 us -> 74.6 us
  blocking collectives: 62.1 us -> 27.2 us
  local copies, waits for them, and re-layouts: 57.6 us -> 40.4 us
  other arithmetic: 14.4 us -> 7.66 us
    reduce_scatter x4 -> x0, waiting for transfers between devices: 112 us -> none  [the longest x1 110 us: shards(): lax.psum_scatter(jnp.dot(head_block, w_out, preferred_element_type=jnp.fl...]
    dot_general x10 -> x0, matrix products: 99.1 us -> none  [the longest x1 32.6 us: shards(): jnp.einsum('rqhp,rqn->rhpn', token_weight[..., None] * x_conv, b_conv, pr...]
    all_gather x3 -> x0, waiting for transfers between devices: 84.7 us -> none  [the longest x1 78.3 us: shards(): piece = lax.all_gather(tokens, 'outc', axis=0, tiled=True)]
    ppermute x0 -> x70, starting transfers between devices: none -> 76.2 us  [the longest x14 28 us: shards(): b = lax.ppermute(b, 'outc', down)]
    pallas_call x0 -> x13, Pallas kernels: none -> 74.6 us  [the longest x1 23 us: relayout(): pl.pallas_call(functools.partial(relayout_kernel, heads), grid=(k // bk,)...]
    psum x1 -> x0, blocking collectives: 62.1 us -> none  [shards(): totals = lax.psum(row_squares[..., None] * selector, ('outc', 'inc'))]
    all_gather x0 -> x1, blocking collectives: none -> 27.2 us  [shards(): new_bc = lax.all_gather(tails(tails_bc), 'outc', axis=2, tiled=True)]
    ppermute x0 -> x70, waiting for transfers between devices: none -> 22.6 us  [the longest x14 9.6 us: shards(): lax.ppermute(q, 'outc', down).astype(F32) + part(n + (s + 2) % n, 1)]
  transfers between devices with their start and end apart: 7 -> 70, of which waited for: 4 -> 22; matrix products, arithmetic and copies ran while one was open for 25% -> 11% of each run, Pallas kernels for 0% -> 29%
where the time goes in v1:
time: 262 us; the launch traced here: 260 us
  starting transfers between devices  76.2 us (29%)
  Pallas kernels  74.6 us (28%)
  local copies, waits for them, and re-layouts  40.4 us (15%)
  blocking collectives  27.2 us (10%)
  waiting for transfers between devices  22.6 us (9%)
  between operations  11.7 us (4%)
  other arithmetic  7.66 us (3%)
    ppermute x14, starting transfers between devices, shards(): b = lax.ppermute(b, 'outc', down)  28 us
    all_gather x1, blocking collectives, shards(): new_bc = lax.all_gather(tails(tails_bc), 'outc', axis=2, tiled=True)  27.2 us
    pallas_call x1, Pallas kernels, relayout(): pl.pallas_call(functools.partial(relayout_kernel, heads), grid=(k // bk,)...  23 us
    pallas_call x4, Pallas kernels, project(): pl.pallas_call(project_kernel, grid_spec=pltpu.PrefetchScalarGridSpec(num...  22.9 us
    unnamed x79, local copies, waits for them, and re-layouts  22.7 us
    ppermute x14, starting transfers between devices, shards(): lax.ppermute(q, 'outc', down).astype(F32) + part(n + (s + 2) % n, 1)  16.4 us
    ppermute x14, starting transfers between devices, shards(): lax.ppermute(p, 'outc', up).astype(F32) + part((s + 2) % n, 0)  14.9 us
    ppermute x4, starting transfers between devices, shards(): got.append(lax.ppermute(bc_own, 'outc', pairs))  10.4 us
  transfers between devices with their start and end apart: 70, of which 22 were waited for; matrix products, arithmetic and copies ran while one was open for 11% of the time, Pallas kernels for 29%

profile of v1, /device:TPU:0, one launch (start us, length us, event | category | flops | bytes accessed | tf_op | source)
XLA Modules:
  0.0 260.2 jit_solution(16047859481098926688)
XLA Ops:
  2.4 3.0 %collective-permute-start.7 = (bf16[32,2048]{1,0:T(8,128)(2,1)S(1)}, bf16[32,2048]{1,0:T(8,128)(2,1)S(1)}, u32[]{:S(2)}, u32[]{:S(2)}) collective-permute-start(bf16[32,2048]{1,0:T(8,128)(2,1)S(1)} %get-tuple-element.88), channel_id=1, source_target_pairs={{4,0},{8,4},{12,8},{14,12},{10,14},{6,10},{2,6},{0,2},{5,1},{9,5},... | collective-permute-start | bytes 393224 | tf_op jit(solution)/shard_map/ppermute | solution.py:486
  16.1 23.0 %relayout.1.w_ref = bf16[2,4096,1024]{2,1,0:T(8,128)(2,1)S(1)} custom-call(bf16[4096,16,128]{2,1,0:T(8,128)(2,1)} %w_ref.1), custom_call_target="tpu_custom_call" | custom-call | flops 4294967296 | bytes 33554432 | tf_op jit(solution)/shard_map/relayout/pallas_call | solution.py:63
  39.2 5.8 %copy-done = bf16[2,4096,1024]{2,1,0:T(8,128)(2,1)} copy-done((bf16[2,4096,1024]{2,1,0:T(8,128)(2,1)}, bf16[2,4096,1024]{2,1,0:T(8,128)(2,1)S(1)}, u32[]{:S(2)}) %copy-start) | copy-done | bytes 16777240
  58.0 2.4 collective-permute-start.46
  102.0 2.7 %gather_rows.3 = (bf16[256,4096]{1,0:T(8,128)(2,1)S(1)}, f32[256,256]{1,0:T(8,128)S(1)}, bf16[256,256]{1,0:T(8,128)(2,1)S(1)}) custom-call(s32[16]{0:T(128)S(1)} %pad_add_fusion.1.at_ref, bf16[32,4096]{1,0:T(8,128)(2,1)S(1)} %get-tuple-element.93.own_ref, bf16[4096,256]{1,0:T(8,128)(2,1)S(1)} %maximum_maximum_fusion.w_ref, bf16[32,2048]{1,0:T(8,128)(2,1)S(1)} %copy-done.14, ...), custom_call_target="tpu_custom_call" | custom-call | flops 536870912 | bytes 6291456 | tf_op jit(solution)/shard_map/gather_rows/pallas_call | solution.py:99
  104.8 2.6 %gather_rows.2 = (bf16[256,4096]{1,0:T(8,128)(2,1)S(1)}, f32[256,256]{1,0:T(8,128)S(1)}, bf16[256,256]{1,0:T(8,128)(2,1)S(1)}) custom-call(s32[16]{0:T(128)S(1)} %pad_add_fusion.1.at_ref, bf16[32,4096]{1,0:T(8,128)(2,1)S(1)} %get-tuple-element.92.own_ref, bf16[4096,256]{1,0:T(8,128)(2,1)S(1)} %maximum_maximum_fusion.w_ref, bf16[32,2048]{1,0:T(8,128)(2,1)S(1)} %copy-done.6, ...), custom_call_target="tpu_custom_call" | custom-call | flops 536870912 | bytes 6291456 | tf_op jit(solution)/shard_map/gather_rows/pallas_call | solution.py:99
  108.0 5.6 %project.7.mine_ref = f32[256,1024]{1,0:T(8,128)S(1)} custom-call(s32[1]{0:T(128)} %bitcast.which_ref.inc_ref, bf16[256,4096]{1,0:T(8,128)(2,1)S(1)} %get-tuple-element.33.rows_ref, bf16[2,4096,1024]{2,1,0:T(8,128)(2,1)} %copy-done), custom_call_target="tpu_custom_call" | custom-call | flops 2147483648 | bytes 10485760 | tf_op jit(solution)/shard_map/project/pallas_call | solution.py:129
  113.6 5.6 %project.6 = bf16[256,1024]{1,0:T(8,128)(2,1)S(1)} custom-call(s32[1]{0:T(128)S(6)} %sub.29.which_ref, bf16[256,4096]{1,0:T(8,128)(2,1)S(1)} %get-tuple-element.33.rows_ref, bf16[2,4096,1024]{2,1,0:T(8,128)(2,1)} %copy-done), custom_call_target="tpu_custom_call" | custom-call | flops 2147483648 | bytes 10485760 | tf_op jit(solution)/shard_map/project/pallas_call | solution.py:129
  119.2 5.8 %project.4 = bf16[256,1024]{1,0:T(8,128)(2,1)S(1)} custom-call(s32[1]{0:T(128)S(6)} %sub.29.which_ref, bf16[256,4096]{1,0:T(8,128)(2,1)S(1)} %get-tuple-element.28.rows_ref, bf16[2,4096,1024]{2,1,0:T(8,128)(2,1)} %copy-done), custom_call_target="tpu_custom_call" | custom-call | flops 2147483648 | bytes 10485760 | tf_op jit(solution)/shard_map/project/pallas_call | solution.py:129
  125.6 5.9 %project.5.mine_ref = f32[256,1024]{1,0:T(8,128)S(1)} custom-call(s32[1]{0:T(128)} %bitcast.which_ref.inc_ref, bf16[256,4096]{1,0:T(8,128)(2,1)S(1)} %get-tuple-element.28.rows_ref, bf16[2,4096,1024]{2,1,0:T(8,128)(2,1)} %copy-done), custom_call_target="tpu_custom_call" | custom-call | flops 2147483648 | bytes 10485760 | tf_op jit(solution)/shard_map/project/pallas_call | solution.py:129
  132.3 4.6 %collective-permute-start.51 = (bf16[256,128]{1,0:T(8,128)(2,1)S(1)}, bf16[256,128]{1,0:T(8,128)(2,1)S(1)}, u32[]{:S(2)}, u32[]{:S(2)}) collective-permute-start(bf16[256,128]{1,0:T(8,128)(2,1)S(1)} %slice.139.own_ref), channel_id=1, source_target_pairs={{8,0},{0,2},{10,4},{2,6},{12,8},{4,10},{14,12},{6,14},{9,1},{1,3},... | collective-permute-start | bytes 196616 | tf_op jit(solution)/shard_map/ppermute | solution.py:508
  137.9 4.5 %collective-permute-start.16 = (bf16[256,128]{1,0:T(8,128)(2,1)S(1)}, bf16[256,128]{1,0:T(8,128)(2,1)S(1)}, u32[]{:S(2)}, u32[]{:S(2)}) collective-permute-start(bf16[256,128]{1,0:T(8,128)(2,1)S(1)} %slice.137.own_ref), channel_id=1, source_target_pairs={{8,0},{0,2},{10,4},{2,6},{12,8},{4,10},{14,12},{6,14},{9,1},{1,3},... | collective-permute-start | bytes 196616 | tf_op jit(solution)/shard_map/ppermute | solution.py:508
  142.4 4.6 %collective-permute-done.16 = bf16[256,128]{1,0:T(8,128)(2,1)S(1)} collective-permute-done((bf16[256,128]{1,0:T(8,128)(2,1)S(1)}, bf16[256,128]{1,0:T(8,128)(2,1)S(1)}, u32[]{:S(2)}, u32[]{:S(2)}) %collective-permute-start.16) | collective-permute-done | bytes 65568 | tf_op jit(solution)/shard_map/ppermute | solution.py:508
  147.1 3.6 %ssm.2 = (bf16[256,512]{1,0:T(8,128)(2,1)S(1)}, f32[8,256]{1,0:T(8,128)S(1)}, bf16[256,512]{1,0:T(8,128)(2,1)S(1)}, bf16[256,128]{1,0:T(8,128)(2,1)S(1)}, f32[25...) custom-call(s32[8,2,32,2]{3,2,1,0:T(8,128)S(1)} %bitcast.57, ...), custom_call_target="tpu_custom_call" | custom-call | flops 1073741824 | bytes 12582912 | tf_op jit(solution)/shard_map/ssm/pallas_call | solution.py:287
  151.3 3.6 %ssm.3 = (bf16[256,512]{1,0:T(8,128)(2,1)S(1)}, f32[8,256]{1,0:T(8,128)S(1)}, bf16[256,512]{1,0:T(8,128)(2,1)S(1)}, bf16[256,128]{1,0:T(8,128)(2,1)S(1)}, f32[25...) custom-call(s32[8,2,32,2]{3,2,1,0:T(8,128)S(1)} %bitcast.58, ...), custom_call_target="tpu_custom_call" | custom-call | flops 1073741824 | bytes 12582912 | tf_op jit(solution)/shard_map/ssm/pallas_call | solution.py:287
  155.6 27.2 %all_gather.3 = bf16[64,3,1024]{2,0,1:T(8,128)(2,1)S(1)} all-gather(bf16[64,3,128]{2,0,1:T(8,128)(2,1)S(1)} %slice.141), channel_id=1, replica_groups=mesh['groups'=2,'outc'=8,'inc'=2] {'outc'}, dimensions={2}, use_global_device_ids=true | all-gather | bytes 442368 | tf_op jit(solution)/shard_map/all_gather | solution.py:550
  182.8 3.6 %new_state.2 = (bf16[8,2,4,512,128]{4,3,2,1,0:T(8,128)(2,1)}, bf16[256,512]{1,0:T(8,128)(2,1)S(1)}) custom-call(s32[8,2,32,2]{3,2,1,0:T(8,128)S(1)} %bitcast.59, bf16[256,512]{1,0:T(8,128)(2,1)S(1)} %get-tuple-element.42.xw_ref, bf16[256,128]{1,0:T(8,128)(2,1)S(1)} %get-tuple-element.43.bconv_ref, f32[256,128]{1,0:T(8,128)S(1)} %get-tuple-element.44.sw_ref, ...), custom_call_target="tpu_custom_call" | custom-call | flops 1073741824 | bytes 16777216 | tf_op jit(solution)/shard_map/new_state/pallas_call | solution.py:366
  186.4 3.6 %new_state.3 = (bf16[8,2,4,512,128]{4,3,2,1,0:T(8,128)(2,1)}, bf16[256,512]{1,0:T(8,128)(2,1)S(1)}) custom-call(s32[8,2,32,2]{3,2,1,0:T(8,128)S(1)} %bitcast.60, bf16[256,512]{1,0:T(8,128)(2,1)S(1)} %get-tuple-element.38.refs_1_, bf16[256,128]{1,0:T(8,128)(2,1)S(1)} %get-tuple-element.39.refs_2_, ...), custom_call_target="tpu_custom_call", output_to_operand_aliasing={{0}: (7, {})} | custom-call | flops 1073741824 | bytes 16777216 | tf_op jit(solution)/shard_map/new_state/pallas_call | solution.py:366
  193.8 3.4 %copy-done.1 = bf16[1024,4096]{1,0:T(8,128)(2,1)S(1)} copy-done((bf16[1024,4096]{1,0:T(8,128)(2,1)S(1)}, bf16[1024,4096]{1,0:T(8,128)(2,1)}, u32[]{:S(2)}) %copy-start.1) | copy-done | bytes 8388632
  197.2 4.5 %out_project.3 = f32[256,4096]{1,0:T(8,128)S(1)} custom-call(s32[1]{0:T(128)} %bitcast.which_ref.inc_ref, bf16[256,512]{1,0:T(8,128)(2,1)S(1)} %get-tuple-element.36.mine_ref, bf16[256,512]{1,0:T(8,128)(2,1)S(1)} %collective-permute-done.53.theirs_ref, bf16[1024,4096]{1,0:T(8,128)(2,1)S(1)} %copy-done.1, bf16[1024,4096]{1,0:T(8,128)(2,1)S(1)} %copy-done.1, ...), custom_call_target="tpu_custom_call" | custom-call | flops 2147483648 | bytes 12582912 | tf_op jit(solution)/shard_map/out_project/pallas_call | solution.py:392
  203.8 3.4 %copy-done.2 = bf16[1024,4096]{1,0:T(8,128)(2,1)S(1)} copy-done((bf16[1024,4096]{1,0:T(8,128)(2,1)S(1)}, bf16[1024,4096]{1,0:T(8,128)(2,1)}, u32[]{:S(2)}) %copy-start.2) | copy-done | bytes 8388632
  207.2 4.5 %out_project.2 = f32[256,4096]{1,0:T(8,128)S(1)} custom-call(s32[1]{0:T(128)} %bitcast.which_ref.inc_ref, bf16[256,512]{1,0:T(8,128)(2,1)S(1)} %get-tuple-element.31.mine_ref, bf16[256,512]{1,0:T(8,128)(2,1)S(1)} %collective-permute-done.18.theirs_ref, bf16[1024,4096]{1,0:T(8,128)(2,1)S(1)} %copy-done.2, bf16[1024,4096]{1,0:T(8,128)(2,1)S(1)} %copy-done.2, ...), custom_call_target="tpu_custom_call" | custom-call | flops 2147483648 | bytes 12582912 | tf_op jit(solution)/shard_map/out_project/pallas_call | solution.py:392
  223.8 2.5 collective-permute-start.30
  240.9 2.9 %collective-permute-start.61 = (bf16[32,2048]{1,0:T(8,128)(2,1)S(1)}, bf16[32,2048]{1,0:T(8,128)(2,1)S(1)}, u32[]{:S(2)}, u32[]{:S(2)}) collective-permute-start(bf16[32,2048]{1,0:T(8,128)(2,1)S(1)} %get-tuple-element.76), channel_id=1, source_target_pairs={{0,4},{4,8},{8,12},{12,14},{14,10},{10,6},{6,2},{2,0},{1,5},{5,9},... | collective-permute-start | bytes 393224 | tf_op jit(solution)/shard_map/ppermute | solution.py:539
  (278 shorter events, 109.7 us)
Async XLA Ops:
  2.4 9.5 %collective-permute-start.7 = (bf16[32,2048]{1,0:T(8,128)(2,1)S(1)}, bf16[32,2048]{1,0:T(8,128)(2,1)S(1)}, u32[]{:S(2)}, u32[]{:S(2)}) collective-permute-start(bf16[32,2048]{1,0:T(8,128)(2,1)S(1)} %get-tuple-element.88), channel_id=1, source_target_pairs={{4,0},{8,4},{12,8},{14,12},{10,14},{6,10},{2,6},{0,2},{5,1},{9,5},... | collective-permute-start | bytes 393224 | tf_op jit(solution)/shard_map/ppermute | solution.py:486
  5.4 8.7 %collective-permute-start.42 = (bf16[32,2048]{1,0:T(8,128)(2,1)S(1)}, bf16[32,2048]{1,0:T(8,128)(2,1)S(1)}, u32[]{:S(2)}, u32[]{:S(2)}) collective-permute-start(bf16[32,2048]{1,0:T(8,128)(2,1)S(1)} %get-tuple-element.90), channel_id=1, source_target_pairs={{4,0},{8,4},{12,8},{14,12},{10,14},{6,10},{2,6},{0,2},{5,1},{9,5},... | collective-permute-start | bytes 393224 | tf_op jit(solution)/shard_map/ppermute | solution.py:486
  7.4 8.6 %collective-permute-start.35 = (bf16[32,2048]{1,0:T(8,128)(2,1)}, bf16[32,2048]{1,0:T(8,128)(2,1)S(1)}, u32[]{:S(2)}, u32[]{:S(2)}) collective-permute-start(bf16[32,2048]{1,0:T(8,128)(2,1)} %get-tuple-element.91), channel_id=1, source_target_pairs={{0,4},{4,8},{8,12},{12,14},{14,10},{10,6},{6,2},{2,0},{1,5},{5,9},... | collective-permute-start | bytes 393224 | tf_op jit(solution)/shard_map/ppermute | solution.py:485
  11.9 37.2 %collective-permute-start.8 = (bf16[32,2048]{1,0:T(8,128)(2,1)S(1)}, bf16[32,2048]{1,0:T(8,128)(2,1)S(1)}, u32[]{:S(2)}, u32[]{:S(2)}) collective-permute-start(bf16[32,2048]{1,0:T(8,128)(2,1)S(1)} %collective-permute-done.7.rest_7_), channel_id=1, source_target_pairs={{4,0},{8,4},{12,8},{14,12},{10,14},{6,10},{2,6},{0,2},{5,1},{9,5},... | collective-permute-start | bytes 393224 | tf_op jit(solution)/shard_map/ppermute | solution.py:486
  14.0 37.1 %collective-permute-start.1 = (bf16[32,2048]{1,0:T(8,128)(2,1)S(1)}, bf16[32,2048]{1,0:T(8,128)(2,1)S(1)}, u32[]{:S(2)}, u32[]{:S(2)}) collective-permute-start(bf16[32,2048]{1,0:T(8,128)(2,1)S(1)} %collective-permute-done.rest_0_), channel_id=1, source_target_pairs={{0,4},{4,8},{8,12},{12,14},{14,10},{10,6},{6,2},{2,0},{1,5},{5,9},... | collective-permute-start | bytes 393224 | tf_op jit(solution)/shard_map/ppermute | solution.py:485
  14.1 30.9 %collective-permute-start.43 = (bf16[32,2048]{1,0:T(8,128)(2,1)S(1)}, bf16[32,2048]{1,0:T(8,128)(2,1)S(1)}, u32[]{:S(2)}, u32[]{:S(2)}) collective-permute-start(bf16[32,2048]{1,0:T(8,128)(2,1)S(1)} %collective-permute-done.42.rest_7_), channel_id=1, source_target_pairs={{4,0},{8,4},{12,8},{14,12},{10,14},{6,10},{2,6},{0,2},{5,1},{9,5},... | collective-permute-start | bytes 393224 | tf_op jit(solution)/shard_map/ppermute | solution.py:486
  16.0 30.9 %collective-permute-start.36 = (bf16[32,2048]{1,0:T(8,128)(2,1)S(1)}, bf16[32,2048]{1,0:T(8,128)(2,1)}, u32[]{:S(2)}, u32[]{:S(2)}) collective-permute-start(bf16[32,2048]{1,0:T(8,128)(2,1)S(1)} %collective-permute-done.35.rest_0_), channel_id=1, source_target_pairs={{0,4},{4,8},{8,12},{12,14},{14,10},{10,6},{6,2},{2,0},{1,5},{5,9},... | collective-permute-start | bytes 393224 | tf_op jit(solution)/shard_map/ppermute | solution.py:485
  68.3 26.3 %collective-permute-start.12 = (bf16[32,2048]{1,0:T(8,128)(2,1)}, bf16[32,2048]{1,0:T(8,128)(2,1)}, u32[]{:S(2)}, u32[]{:S(2)}) collective-permute-start(bf16[32,2048]{1,0:T(8,128)(2,1)} %collective-permute-done.11.rest_11_), channel_id=1, source_target_pairs={{4,0},{8,4},{12,8},{14,12},{10,14},{6,10},{2,6},{0,2},{5,1},{9,5},... | collective-permute-start | bytes 393224 | tf_op jit(solution)/shard_map/ppermute | solution.py:486
  70.1 26.4 %collective-permute-start.5 = (bf16[32,2048]{1,0:T(8,128)(2,1)}, bf16[32,2048]{1,0:T(8,128)(2,1)}, u32[]{:S(2)}, u32[]{:S(2)}) collective-permute-start(bf16[32,2048]{1,0:T(8,128)(2,1)} %collective-permute-done.4.rest_4_), channel_id=1, source_target_pairs={{0,4},{4,8},{8,12},{12,14},{14,10},{10,6},{6,2},{2,0},{1,5},{5,9},... | collective-permute-start | bytes 393224 | tf_op jit(solution)/shard_map/ppermute | solution.py:485
  71.6 25.9 %collective-permute-start.48 = (bf16[32,2048]{1,0:T(8,128)(2,1)}, bf16[32,2048]{1,0:T(8,128)(2,1)}, u32[]{:S(2)}, u32[]{:S(2)}) collective-permute-start(bf16[32,2048]{1,0:T(8,128)(2,1)} %collective-permute-done.47.rest_12_), channel_id=1, source_target_pairs={{4,0},{8,4},{12,8},{14,12},{10,14},{6,10},{2,6},{0,2},{5,1},{9,5},... | collective-permute-start | bytes 393224 | tf_op jit(solution)/shard_map/ppermute | solution.py:486
  73.3 24.1 %collective-permute-start.41 = (bf16[32,2048]{1,0:T(8,128)(2,1)}, bf16[32,2048]{1,0:T(8,128)(2,1)}, u32[]{:S(2)}, u32[]{:S(2)}) collective-permute-start(bf16[32,2048]{1,0:T(8,128)(2,1)} %collective-permute-done.40.rest_5_), channel_id=1, source_target_pairs={{0,4},{4,8},{8,12},{12,14},{14,10},{10,6},{6,2},{2,0},{1,5},{5,9},... | collective-permute-start | bytes 393224 | tf_op jit(solution)/shard_map/ppermute | solution.py:485
  94.6 10.2 %collective-permute-start.13 = (bf16[32,2048]{1,0:T(8,128)(2,1)}, bf16[32,2048]{1,0:T(8,128)(2,1)S(1)}, u32[]{:S(2)}, u32[]{:S(2)}) collective-permute-start(bf16[32,2048]{1,0:T(8,128)(2,1)} %collective-permute-done.12.rest_12_), channel_id=1, source_target_pairs={{4,0},{8,4},{12,8},{14,12},{10,14},{6,10},{2,6},{0,2},{5,1},{9,5},... | collective-permute-start | bytes 393224 | tf_op jit(solution)/shard_map/ppermute | solution.py:486
  104.7 26.9 %collective-permute-start.50 = (bf16[256,256]{1,0:T(8,128)(2,1)S(1)}, bf16[256,256]{1,0:T(8,128)(2,1)S(1)}, u32[]{:S(2)}, u32[]{:S(2)}) collective-permute-start(bf16[256,256]{1,0:T(8,128)(2,1)S(1)} %get-tuple-element.35), channel_id=1, source_target_pairs={{0,1},{1,0},{2,3},{3,2},{4,5},{5,4},{6,7},{7,6},{8,9},{9,8},{10,11... | collective-permute-start | bytes 393224 | tf_op jit(solution)/shard_map/ppermute | solution.py:439
  107.4 29.5 %collective-permute-start.15 = (bf16[256,256]{1,0:T(8,128)(2,1)S(1)}, bf16[256,256]{1,0:T(8,128)(2,1)S(1)}, u32[]{:S(2)}, u32[]{:S(2)}) collective-permute-start(bf16[256,256]{1,0:T(8,128)(2,1)S(1)} %get-tuple-element.30), channel_id=1, source_target_pairs={{0,1},{1,0},{2,3},{3,2},{4,5},{5,4},{6,7},{7,6},{8,9},{9,8},{10,11... | collective-permute-start | bytes 393224 | tf_op jit(solution)/shard_map/ppermute | solution.py:439
  125.1 21.9 %collective-permute-start.14 = (bf16[256,1024]{1,0:T(8,128)(2,1)S(1)}, bf16[256,1024]{1,0:T(8,128)(2,1)S(1)}, u32[]{:S(2)}, u32[]{:S(2)}) collective-permute-start(bf16[256,1024]{1,0:T(8,128)(2,1)S(1)} %project.4), channel_id=1, source_target_pairs={{0,1},{1,0},{2,3},{3,2},{4,5},{5,4},{6,7},{7,6},{8,9},{9,8},{10,11... | collective-permute-start | bytes 1572872 | tf_op jit(solution)/shard_map/ppermute | solution.py:439
  125.2 26.1 %collective-permute-start.49 = (bf16[256,1024]{1,0:T(8,128)(2,1)S(1)}, bf16[256,1024]{1,0:T(8,128)(2,1)S(1)}, u32[]{:S(2)}, u32[]{:S(2)}) collective-permute-start(bf16[256,1024]{1,0:T(8,128)(2,1)S(1)} %project.6), channel_id=1, source_target_pairs={{0,1},{1,0},{2,3},{3,2},{4,5},{5,4},{6,7},{7,6},{8,9},{9,8},{10,11... | collective-permute-start | bytes 1572872 | tf_op jit(solution)/shard_map/ppermute | solution.py:439
  132.3 10.0 %collective-permute-start.51 = (bf16[256,128]{1,0:T(8,128)(2,1)S(1)}, bf16[256,128]{1,0:T(8,128)(2,1)S(1)}, u32[]{:S(2)}, u32[]{:S(2)}) collective-permute-start(bf16[256,128]{1,0:T(8,128)(2,1)S(1)} %slice.139.own_ref), channel_id=1, source_target_pairs={{8,0},{0,2},{10,4},{2,6},{12,8},{4,10},{14,12},{6,14},{9,1},{1,3},... | collective-permute-start | bytes 196616 | tf_op jit(solution)/shard_map/ppermute | solution.py:508
  137.9 9.1 %collective-permute-start.16 = (bf16[256,128]{1,0:T(8,128)(2,1)S(1)}, bf16[256,128]{1,0:T(8,128)(2,1)S(1)}, u32[]{:S(2)}, u32[]{:S(2)}) collective-permute-start(bf16[256,128]{1,0:T(8,128)(2,1)S(1)} %slice.137.own_ref), channel_id=1, source_target_pairs={{8,0},{0,2},{10,4},{2,6},{12,8},{4,10},{14,12},{6,14},{9,1},{1,3},... | collective-permute-start | bytes 196616 | tf_op jit(solution)/shard_map/ppermute | solution.py:508
  150.7 39.3 %collective-permute-start.19 = (f32[8,256]{1,0:T(8,128)S(1)}, f32[8,256]{1,0:T(8,128)S(1)}, u32[]{:S(2)}, u32[]{:S(2)}) collective-permute-start(f32[8,256]{1,0:T(8,128)S(1)} %get-tuple-element.32), channel_id=1, source_target_pairs={{0,1},{1,0},{2,3},{3,2},{4,5},{5,4},{6,7},{7,6},{8,9},{9,8},{10,11... | collective-permute-start | bytes 24584 | tf_op jit(solution)/shard_map/ppermute | solution.py:439
  150.8 53.0 %collective-permute-start.18 = (bf16[256,512]{1,0:T(8,128)(2,1)S(1)}, bf16[256,512]{1,0:T(8,128)(2,1)S(1)}, u32[]{:S(2)}, u32[]{:S(2)}) collective-permute-start(bf16[256,512]{1,0:T(8,128)(2,1)S(1)} %get-tuple-element.31.mine_ref), channel_id=1, source_target_pairs={{0,1},{1,0},{2,3},{3,2},{4,5},{5,4},{6,7},{7,6},{8,9},{9,8},{10,11... | collective-permute-start | bytes 786440 | tf_op jit(solution)/shard_map/ppermute | solution.py:439
  154.9 35.1 %collective-permute-start.54 = (f32[8,256]{1,0:T(8,128)S(1)}, f32[8,256]{1,0:T(8,128)S(1)}, u32[]{:S(2)}, u32[]{:S(2)}) collective-permute-start(f32[8,256]{1,0:T(8,128)S(1)} %get-tuple-element.37), channel_id=1, source_target_pairs={{0,1},{1,0},{2,3},{3,2},{4,5},{5,4},{6,7},{7,6},{8,9},{9,8},{10,11... | collective-permute-start | bytes 24584 | tf_op jit(solution)/shard_map/ppermute | solution.py:439
  155.1 38.6 %collective-permute-start.53 = (bf16[256,512]{1,0:T(8,128)(2,1)S(1)}, bf16[256,512]{1,0:T(8,128)(2,1)S(1)}, u32[]{:S(2)}, u32[]{:S(2)}) collective-permute-start(bf16[256,512]{1,0:T(8,128)(2,1)S(1)} %get-tuple-element.36.mine_ref), channel_id=1, source_target_pairs={{0,1},{1,0},{2,3},{3,2},{4,5},{5,4},{6,7},{7,6},{8,9},{9,8},{10,11... | collective-permute-start | bytes 786440 | tf_op jit(solution)/shard_map/ppermute | solution.py:439
  201.7 12.1 %collective-permute-start.56 = (bf16[32,2048]{1,0:T(8,128)(2,1)S(1)}, bf16[32,2048]{1,0:T(8,128)(2,1)S(1)}, u32[]{:S(2)}, u32[]{:S(2)}) collective-permute-start(bf16[32,2048]{1,0:T(8,128)(2,1)S(1)} %get-tuple-element.86), channel_id=1, source_target_pairs={{0,4},{4,8},{8,12},{12,14},{14,10},{10,6},{6,2},{2,0},{1,5},{5,9},... | collective-permute-start | bytes 393224 | tf_op jit(solution)/shard_map/ppermute | solution.py:539
  202.2 11.7 %collective-permute-start.63 = (bf16[32,2048]{1,0:T(8,128)(2,1)S(1)}, bf16[32,2048]{1,0:T(8,128)(2,1)S(1)}, u32[]{:S(2)}, u32[]{:S(2)}) collective-permute-start(bf16[32,2048]{1,0:T(8,128)(2,1)S(1)} %get-tuple-element.87), channel_id=1, source_target_pairs={{4,0},{8,4},{12,8},{14,12},{10,14},{6,10},{2,6},{0,2},{5,1},{9,5},... | collective-permute-start | bytes 393224 | tf_op jit(solution)/shard_map/ppermute | solution.py:540
  (83 other events, 1008.1 us)

commit v2 on v1

--- a/solution.py
+++ b/solution.py
@@ -12,6 +12,7 @@
 KW = 4
 DRAFT = 8
 LANES = 128
+STREAMS = 2
 BF = jnp.bfloat16
 F32 = jnp.float32
 HIGH = lax.Precision.HIGHEST
@@ -57,91 +58,99 @@
                 ]
 
 
-def relayout(w_zx, bk=128):
+def relayout(piece, pieces, w_zx, into, bk=512):
     k, heads, width = w_zx.shape
     cols = heads // 2 * width
+    bk = min(bk, k // pieces)
+    steps = k // bk // pieces
+    kernel = functools.partial(relayout_kernel, heads)
+    specs = [pl.BlockSpec((bk, heads, width), lambda i: (piece * steps + i, 0, 0))]
+    args, aliases = [w_zx], {}
+    if into is not None:
+        args.append(into)
+        specs.append(pl.BlockSpec(memory_space=pl.ANY))
+        aliases = {1: 0}
+
+        def kernel(w_ref, _, o_ref, perm):
+            relayout_kernel(heads, w_ref, o_ref, perm)
+
     return pl.pallas_call(
-        functools.partial(relayout_kernel, heads),
-        grid=(k // bk,),
-        in_specs=[pl.BlockSpec((bk, heads, width), lambda i: (i, 0, 0))],
-        out_specs=pl.BlockSpec((2, bk, cols), lambda i: (0, i, 0)),
+        kernel,
+        grid=(steps,),
+        in_specs=specs,
+        out_specs=pl.BlockSpec((2, bk, cols), lambda i: (0, piece * steps + i, 0)),
         out_shape=jax.ShapeDtypeStruct((2, k, cols), BF),
         scratch_shapes=[pltpu.VMEM((256, 256), BF)],
-        compiler_params=params(24),
-        cost_estimate=cost(2 * k * heads * width * 256, 4 * k * heads * width),
+        input_output_aliases=aliases,
+        compiler_params=params(52),
+        cost_estimate=cost(2 * k * heads * width * 256 // pieces, 4 * k * heads * width // pieces),
         name="relayout",
-    )(w_zx)
-
-
-def gather_kernel(n, at_ref, own_ref, w_ref, *rest):
-    ups, downs = rest[: n - 1], rest[n - 1 : 2 * (n - 1)]
-    rows_ref, keep_ref, send_ref = rest[2 * (n - 1) :]
-    rc, width = own_ref.shape
-    half = width // 2
-
-    def at(i):
-        return pl.ds(pl.multiple_of(at_ref[i] * rc, 16), rc)
-
-    rows_ref[at(0), :] = own_ref[...]
-    for s in range(1, n):
-        rows_ref[at(s), :half] = ups[s - 1][...]
-        rows_ref[at(n + s), half:] = downs[s - 1][...]
-    total = jnp.dot(rows_ref[...], w_ref[...], preferred_element_type=F32)
-    keep_ref[...] = total
-    send_ref[...] = total.astype(BF)
-
-
-def gather_rows(owners, own, w_ext, ups, downs):
-    n = len(ups) + 1
-    rc, width = own.shape
-    rows, cols = n * rc, w_ext.shape[1]
-    arrays = [own, w_ext, *ups, *downs]
+    )(*args)
+
+
+def project_kernel(parts, old, seq_ref, which_ref, *refs):
+    ins, w_ref, ext_ref = refs[:parts], refs[parts], refs[parts + 1]
+    rest = refs[parts + 2 :]
+    olds, rest = rest[:old], rest[old:]
+    o_ref, exts, rows = rest[0], rest[1:-1], rest[-1]
+    piece = ins[0].shape[0]
+    blocks = parts // STREAMS
+    rc = piece * STREAMS
+
+    def put(out, new, before):
+        if not old:
+            out[...] = new.astype(out.dtype)
+            return
+        for i in range(blocks):
+            at = pl.ds(pl.multiple_of(seq_ref[i] * rc, 16), rc)
+            out[at, :] = before[i * rc : (i + 1) * rc, :].astype(out.dtype)
+            at = pl.ds(pl.multiple_of(seq_ref[blocks + i] * rc, 16), rc)
+            out[at, :] = new[i * rc : (i + 1) * rc].astype(out.dtype)
+
+    @pl.when(pl.program_id(0) == 0)
+    def _():
+        for i in range(parts):
+            rows[i * piece : (i + 1) * piece, :] = ins[i][...]
+        if exts:
+            total = jnp.dot(rows[...], ext_ref[...], preferred_element_type=F32)
+            for e in exts:
+                put(e, total, olds[1] if old else None)
+
+    total = jnp.dot(rows[...], w_ref[0], preferred_element_type=F32)
+    put(o_ref, total, olds[0] if old else None)
+
+
+def project(seq, which, ins, w, w_ext, dtype, ext_dtypes, olds=(), bn=512):
+    parts = len(ins)
+    rc, k = ins[0].shape
+    m = rc * parts
+    out_m = 2 * m if olds else m
+    cols, ext_cols = w.shape[2], w_ext.shape[1]
+    bn = min(bn, cols)
+    in_specs = [whole_block((rc, k)) for _ in ins] + [
+        pl.BlockSpec((1, k, bn), lambda j, seq, which: (which[0], 0, j)),
+        whole_block((k, ext_cols)) if ext_dtypes else pl.BlockSpec(memory_space=pl.ANY),
+    ]
+    if olds:
+        in_specs.append(pl.BlockSpec((m, bn), lambda j, seq, which: (0, j)))
+        if ext_dtypes:
+            in_specs.append(whole_block((m, ext_cols)))
     return pl.pallas_call(
-        functools.partial(gather_kernel, n),
+        functools.partial(project_kernel, parts, len(olds)),
         grid_spec=pltpu.PrefetchScalarGridSpec(
-            num_scalar_prefetch=1,
-            grid=(1,),
-            in_specs=[whole_block(a.shape) for a in arrays],
-            out_specs=[
-                whole_block((rows, width)),
-                whole_block((rows, cols)),
-                whole_block((rows, cols)),
-            ],
+            num_scalar_prefetch=2,
+            grid=(cols // bn,),
+            in_specs=in_specs,
+            out_specs=[pl.BlockSpec((out_m, bn), lambda j, seq, which: (0, j))]
+            + [whole_block((out_m, ext_cols)) for _ in ext_dtypes],
+            scratch_shapes=[pltpu.VMEM((m, k), BF)],
         ),
-        out_shape=[
-            jax.ShapeDtypeStruct((rows, width), BF),
-            jax.ShapeDtypeStruct((rows, cols), F32),
-            jax.ShapeDtypeStruct((rows, cols), BF),
-        ],
-        compiler_params=params(40),
-        cost_estimate=cost(2 * rows * width * cols, 4 * rows * width + 2 * width * cols),
-        name="gather_rows",
-    )(owners, *arrays)
-
-
-def project_kernel(which_ref, rows_ref, w_ref, o_ref):
-    o_ref[...] = jnp.dot(rows_ref[...], w_ref[0], preferred_element_type=F32).astype(o_ref.dtype)
-
-
-def project(which, rows, w, dtype, bn=256):
-    m, k = rows.shape
-    cols = w.shape[2]
-    return pl.pallas_call(
-        project_kernel,
-        grid_spec=pltpu.PrefetchScalarGridSpec(
-            num_scalar_prefetch=1,
-            grid=(cols // bn,),
-            in_specs=[
-                pl.BlockSpec((m, k), lambda j, which: (0, 0)),
-                pl.BlockSpec((1, k, bn), lambda j, which: (which[0], 0, j)),
-            ],
-            out_specs=pl.BlockSpec((m, bn), lambda j, which: (0, j)),
-        ),
-        out_shape=jax.ShapeDtypeStruct((m, cols), dtype),
-        compiler_params=params(40),
-        cost_estimate=cost(2 * m * k * cols, 2 * k * cols + 2 * m * k),
+        out_shape=[jax.ShapeDtypeStruct((out_m, cols), dtype)]
+        + [jax.ShapeDtypeStruct((out_m, ext_cols), d) for d in ext_dtypes],
+        compiler_params=params(52),
+        cost_estimate=cost(2 * m * k * (cols + ext_cols), 2 * k * cols + 2 * m * k),
         name="project",
-    )(which, rows, w)
+    )(seq, which, *ins, w, w_ext, *olds)
 
 
 def silu(v):
@@ -149,9 +158,8 @@
 
 
 def ssm_kernel(
-    meta_ref, recv_ref, mine_ref, dt_ref, braw_ref, craw_ref, own_ref, prevx_ref, prevb_ref, prevc_ref,
-    prevo_ref, tapx_ref, tapb_ref, tapc_ref, bias_ref, rate_ref, skip_ref, gain_ref, state_ref,
-    gated_ref, ssq_ref, xw_ref, bconv_ref, sw_ref, xraw_ref, tail_ref,
+    meta_ref, recv_ref, mine_ref, dt_ref, braw_ref, craw_ref, prevx_ref, prevb_ref, prevc_ref, tapx_ref, tapb_ref, tapc_ref, bias_ref, rate_ref, skip_ref, gain_ref, state_ref,
+    gated_ref, ssq_ref, xw_ref, bconv_ref, sw_ref, xraw_ref,
 ):
     rb = recv_ref.shape[0]
     hp = gated_ref.shape[1]
@@ -251,8 +259,6 @@
     row_sum = jnp.broadcast_to(jnp.sum(squares, axis=1, keepdims=True), (rb, LANES))
     ssq_ref[...] = row_sum.T[:8]
 
-    tail_ref[...] = pick_tail(ss, acc, own_ref[...], prevo_ref[...].reshape(own_ref.shape)).astype(BF)
-
 
 def pick_tail(ss, acc, raw, prev):
     rb = raw.shape[0]
@@ -274,7 +280,6 @@
     n, _, rq, hp, width_n = state.shape
     rc = rq * DRAFT
     ob = rb // rc
-    cw = per_row[6].shape[1]
 
     def row_spec(a):
         if a.ndim == 2:
@@ -297,7 +302,6 @@
             flat(LANES),
             flat(LANES),
             flat(hp),
-            flat(cw),
         ],
         out_shape=[
             jax.ShapeDtypeStruct((rows, hp), BF),
@@ -306,7 +310,6 @@
             jax.ShapeDtypeStruct((rows, LANES), BF),
             jax.ShapeDtypeStruct((rows, LANES), F32),
             jax.ShapeDtypeStruct((rows, hp), BF),
-            jax.ShapeDtypeStruct((rows, cw), BF),
         ],
         compiler_params=params(40),
         cost_estimate=cost(2 * rows * hp * 4096, 6 * rows * hp * 16),
@@ -339,6 +342,31 @@
                 o_ref[r // rq, 0, r % rq, cut, :] = new.astype(BF)
 
 
+def tail_kernel(meta_ref, raw_ref, prev_ref, o_ref):
+    rb = raw_ref.shape[0]
+    ss = meta_ref[..., 0:1].reshape(rb, 1)
+    acc = meta_ref[..., 1:2].reshape(rb, 1)
+    o_ref[...] = pick_tail(ss, acc, raw_ref[...], prev_ref[...]).astype(BF)
+
+
+def new_history(rb, meta, raw, prev):
+    rows, cols = raw.shape
+
+    def flat(w):
+        return pl.BlockSpec((rb, w), lambda i: (i, 0))
+
+    return pl.pallas_call(
+        tail_kernel,
+        grid=(rows // rb,),
+        in_specs=[flat(2), flat(cols), flat(cols)],
+        out_specs=flat(cols),
+        out_shape=jax.ShapeDtypeStruct((rows, cols), BF),
+        compiler_params=params(24),
+        cost_estimate=cost(4 * rows * rb * cols, 6 * rows * cols),
+        name="new_history",
+    )(meta, raw, prev)
+
+
 def new_state(chunk, rb, meta, xw, bconv, sw, xraw, prev_x, state, into):
     rows, hp = xw.shape
     n, _, rq, _, width_n = state.shape
@@ -386,9 +414,10 @@
     o_ref[...] = (product * column).astype(o_ref.dtype)
 
 
-def out_project(inc, mine, theirs, w_out, ssq, scale_by, bn=512):
+def out_project(inc, mine, theirs, w_out, ssq, scale_by, part, parts, bn=512):
     rows, hp = mine.shape
-    cols = w_out.shape[1]
+    cols = w_out.shape[1] // parts
+    first = part * (cols // bn)
     return pl.pallas_call(
         functools.partial(out_kernel, scale_by),
         grid_spec=pltpu.PrefetchScalarGridSpec(
@@ -397,8 +426,8 @@
             in_specs=[
                 pl.BlockSpec((rows, hp), lambda j, inc: (0, 0)),
                 pl.BlockSpec((rows, hp), lambda j, inc: (0, 0)),
-                pl.BlockSpec((hp, bn), lambda j, inc: (inc[0], j)),
-                pl.BlockSpec((hp, bn), lambda j, inc: (1 - inc[0], j)),
+                pl.BlockSpec((hp, bn), lambda j, inc: (inc[0], first + j)),
+                pl.BlockSpec((hp, bn), lambda j, inc: (1 - inc[0], first + j)),
                 pl.BlockSpec((8, rows), lambda j, inc: (0, 0)),
             ],
             out_specs=pl.BlockSpec((rows, bn), lambda j, inc: (0, j)),
@@ -422,18 +451,18 @@
     rb = min(128, rows)
     order = list(range(0, n, 2)) + list(range(n - 1, 0, -2))
     place = [order.index(i) for i in range(n)]
-    up = [(order[i], order[(i + 1) % n]) for i in range(n)]
-    down = [(b, a) for a, b in up]
+    ring = [(2 * order[i], 2 * order[(i + 1) % n]) for i in range(n)]
+    ring += [(2 * order[(i + 1) % n] + 1, 2 * order[i] + 1) for i in range(n)]
     swap = [(0, 1), (1, 0)]
     me = lax.axis_index("outc")
     inc = lax.axis_index("inc")
     pos = jnp.array(place, jnp.int32)[me]
-    order_a = jnp.array(order, jnp.int32)
     steps = jnp.arange(n, dtype=jnp.int32)
-    above = order_a[(pos - steps) % n]
-    below = order_a[(pos + steps) % n]
-    owners = jnp.concatenate([above, below])
+    seq = jnp.array(order, jnp.int32)[(pos + (2 * inc - 1) * steps) % n]
     inc1 = inc.astype(jnp.int32).reshape(1)
+
+    def onward(a):
+        return lax.ppermute(a, ("outc", "inc"), ring)
 
     def other(a):
         return lax.ppermute(a, "inc", swap)
@@ -456,7 +485,7 @@
     prev_x = history(conv_x_state)
     prev_b = history(columns(conv_bc_state, group * width_n, width_n))
     prev_c = history(columns(conv_bc_state, (G + group) * width_n, width_n))
-    prev_own = history(columns(conv_bc_state, me * cw, cw))
+    prev_own = history(columns(conv_bc_state, me * cw, cw)).reshape(rows, cw)
     meta = jnp.stack([span_start, accepted], axis=-1).astype(jnp.int32)
     meta = jnp.broadcast_to(meta[:, None, :], (req, DRAFT, 2)).reshape(n, chunks, rc, 2)
 
@@ -473,82 +502,102 @@
         norm_gain.reshape(1, hp),
     ]
     state = ssm_state.reshape(n, chunks, rq, hp, width_n)
-    w = relayout(w_zx)
     scale_by = 1.0 / (HEADS // G * width_p)
 
-    halves = []
-    for c in range(chunks):
-        own = tokens[c * rc : (c + 1) * rc]
-        a, b = own[:, : half_d // 2], own[:, half_d // 2 :]
-        ups, downs = [], []
-        for s in range(n - 1):
-            a = lax.ppermute(a, "outc", up)
-            b = lax.ppermute(b, "outc", down)
-            ups.append(a)
-            downs.append(b)
-        halves.append((own, ups, downs))
-
-    outs, tails_x, tails_bc = [], [], []
-    into = None
-    for c in range(chunks):
-        own, ups, downs = halves[c]
-        rows_all, ext_keep, ext_send = gather_rows(owners, own, w_ext, ups, downs)
-        ext = (ext_keep + other(ext_send).astype(F32)).astype(BF)
-        bc_own = ext[:, :cw]
-        dt = columns(ext[:, cw : cw + 2 * hd], inc * hd, hd)
-        dt = jnp.pad(dt, ((0, 0), (0, LANES - hd)))
-        got = []
-        for k in range(member):
-            pairs = []
-            for g in range(G):
-                width = member // 2
-                sources = [g * width + i for i in range(width)] + [n // 2 + g * width + i for i in range(width)]
-                for i in range(member):
-                    pairs.append((sources[(i + k) % member], g * member + i))
-            got.append(lax.ppermute(bc_own, "outc", pairs))
-        pieces = []
-        for i in range(member):
-            piece = got[0]
-            for k in range(1, member):
-                piece = jnp.where((i - seat) % member == k, got[k], piece)
-            pieces.append(piece)
-        b_raw = jnp.concatenate(pieces[: member // 2], axis=1)
-        c_raw = jnp.concatenate(pieces[member // 2 :], axis=1)
-        theirs = other(project(1 - inc1, rows_all, w, BF))
-        mine = project(inc1, rows_all, w, F32)
-        gated, ssq, xw, bconv, sw, xraw, tail = ssm(
-            c, rb, [meta, theirs, mine, dt, b_raw, c_raw, bc_own, prev_x, prev_b, prev_c, prev_own], tables, state
-        )
-        tails_bc.append(tail)
-        gated_theirs = other(gated)
-        ssq = ssq + other(ssq)
-        d = 1
-        while d < member:
-            ssq = ssq + lax.ppermute(ssq, "outc", [(i, i ^ d) for i in range(n)])
-            d *= 2
-        partial = out_project(inc1, gated, gated_theirs, w_out, ssq, scale_by)
-        half = partial.shape[1] // 2
-
-        def part(i, side):
-            owner = owners[i]
-            return lax.dynamic_slice(partial, (owner * rc, side * half), (rc, half))
-
-        p = part(1, 0).astype(BF)
-        q = part(n + 1, 1).astype(BF)
-        for s in range(n - 1):
-            p = (lax.ppermute(p, "outc", up).astype(F32) + part((s + 2) % n, 0)).astype(BF)
-            q = (lax.ppermute(q, "outc", down).astype(F32) + part(n + (s + 2) % n, 1)).astype(BF)
-        outs.append(jnp.concatenate([p, q], axis=1))
-        into, tail_x = new_state(c, rb, meta, xw, bconv, sw, xraw, prev_x, state, into)
-        tails_x.append(tail_x)
-
-    def tails(parts):
-        a = jnp.stack([x.reshape(n, rq, DRAFT, x.shape[1]) for x in parts], axis=1)
+    pieces = 4
+    w = None
+    piece_rows = rc // STREAMS
+    heads_of = [tokens[i * piece_rows : (i + 1) * piece_rows] for i in range(STREAMS)]
+    blocks = list(heads_of)
+    first = n // 2
+    split = first * STREAMS
+    for s in range(n - 1):
+        heads_of = [onward(a) for a in heads_of]
+        lead = heads_of[0]
+        if s < pieces:
+            w = relayout(s, pieces, w_zx, w)
+            lead, w = lax.optimization_barrier((lead, w))
+        elif s == max(pieces, first):
+            theirs_1, ext_1 = project(seq, 1 - inc1, blocks[:split], w, w_ext, BF, [F32])
+            lead, theirs_1, ext_1 = lax.optimization_barrier((lead, theirs_1, ext_1))
+        elif s == max(pieces, first) + 1:
+            (mine_1,) = project(seq, inc1, blocks[:split], w, w_ext, F32, [])
+            lead, mine_1 = lax.optimization_barrier((lead, mine_1))
+        heads_of[0] = lead
+        blocks += heads_of
+
+    prepared = [meta, prev_x, prev_b, prev_c, tables, prev_own, w_ext]
+    blocks[-1], prepared = lax.optimization_barrier((blocks[-1], prepared))
+    meta, prev_x, prev_b, prev_c, tables, prev_own, w_ext = prepared
+
+    theirs, ext_keep, ext_send = project(
+        seq, 1 - inc1, blocks[split:], w, w_ext, BF, [F32, BF], (theirs_1, ext_1)
+    )
+    ext = (ext_keep + other(ext_send).astype(F32)).astype(BF)
+    bc_own = ext[:, :cw]
+    history_bc = new_history(rb, meta.reshape(rows, 2), bc_own, prev_own)
+    history_bc = history_bc.reshape(req, DRAFT, cw)[:, : KW - 1].reshape(1, req * (KW - 1), cw)
+    dt = columns(ext[:, cw : cw + 2 * hd], inc * hd, hd)
+    dt = jnp.pad(dt, ((0, 0), (0, LANES - hd)))
+    got = []
+    for k in range(member):
+        pairs = []
+        for g in range(G):
+            width = member // 2
+            sources = [g * width + i for i in range(width)] + [n // 2 + g * width + i for i in range(width)]
+            for i in range(member):
+                pairs.append((sources[(i + k) % member], g * member + i))
+        got.append(lax.ppermute(bc_own, "outc", pairs))
+    picked = []
+    for i in range(member):
+        piece = got[0]
+        for k in range(1, member):
+            piece = jnp.where((i - seat) % member == k, got[k], piece)
+        picked.append(piece)
+    b_raw = jnp.concatenate(picked[: member // 2], axis=1)
+    c_raw = jnp.concatenate(picked[member // 2 :], axis=1)
+    theirs = other(theirs)
+    (mine,) = project(seq, inc1, blocks[split:], w, w_ext, F32, [], (mine_1,))
+    gated, ssq, xw, bconv, sw, xraw = ssm(
+        0, rb, [meta, theirs, mine, dt, b_raw, c_raw, prev_x, prev_b, prev_c], tables, state
+    )
+
+    def tails(a):
         return a.reshape(req, DRAFT, a.shape[-1])[:, : KW - 1]
 
-    new_x = tails(tails_x).reshape(req, KW - 1, hd, width_p)
-    new_bc = lax.all_gather(tails(tails_bc), "outc", axis=2, tiled=True)
-    return jnp.concatenate(outs, axis=0), into.reshape(ssm_state.shape), new_x, new_bc
+    gated_theirs = other(gated)
+    ssq = ssq + other(ssq)
+    d = 1
+    while d < member:
+        ssq = ssq + lax.ppermute(ssq, "outc", [(i, i ^ d) for i in range(n)])
+        d *= 2
+    after, tail_x = new_state(0, rb, meta, xw, bconv, sw, xraw, prev_x, state, None)
+    gated_theirs, ssq, after = lax.optimization_barrier((gated_theirs, ssq, after))
+
+    sums, partials = [], []
+
+    def part(i, s):
+        return lax.dynamic_slice_in_dim(partials[i], seq[(s + 1) % n] * rc, rc, 0)
+
+    for i in range(STREAMS):
+        partials.append(out_project(inc1, gated, gated_theirs, w_out, ssq, scale_by, i, STREAMS))
+        sums.append(part(i, 0).astype(BF))
+    width = 1
+    for s in range(n - 1):
+        if width < n:
+            history_bc, sums[0] = lax.optimization_barrier((history_bc, sums[0]))
+            got = lax.ppermute(history_bc, "outc", [(i, i ^ width) for i in range(n)])
+            history_bc = jnp.where(
+                (me & width) != 0,
+                jnp.concatenate([got, history_bc], axis=0),
+                jnp.concatenate([history_bc, got], axis=0),
+            )
+            width *= 2
+        for i in range(STREAMS):
+            sums[i] = (onward(sums[i]).astype(F32) + part(i, s + 1)).astype(BF)
+    new_bc = jnp.swapaxes(history_bc, 0, 1).reshape(req, KW - 1, n * cw)
+    new_x = tails(tail_x).reshape(req, KW - 1, hd, width_p)
+    return jnp.concatenate(sums, axis=1), after.reshape(ssm_state.shape), new_x, new_bc
 
 
 def solution(mesh):
@@ -572,7 +621,7 @@
         P("groups"),
     )
     return jax.shard_map(
-        functools.partial(shards, n, 2),
+        functools.partial(shards, n, 1),
         mesh=mesh,
         in_specs=placed,
         out_specs=(

time: 262 us -> 194 us (0.74)
  starting transfers between devices: 76.2 us -> 39.1 us
  blocking collectives: 27.2 us -> 0 us
  waiting for transfers between devices: 22.6 us -> 40.1 us
  local copies, waits for them, and re-layouts: 40.4 us -> 23.2 us
  other arithmetic: 7.66 us -> 15.7 us
  Pallas kernels: 74.6 us -> 68.9 us
  between operations: 11.7 us -> 6.37 us
    ppermute x56 -> x31, starting transfers between devices: 61.4 us -> 31.6 us  [the longest x28 29.4 us: onward(): return lax.ppermute(a, ('outc', 'inc'), ring)]
    all_gather x1 -> x0, blocking collectives: 27.2 us -> none  [shards(): new_bc = lax.all_gather(tails(tails_bc), 'outc', axis=2, tiled=True)]
    ppermute x56 -> x31, waiting for transfers between devices: 17.4 us -> 39 us  [the longest x28 25.7 us: onward(): return lax.ppermute(a, ('outc', 'inc'), ring)]
    convert_element_type x14, other arithmetic: 0.69 us -> 11.2 us  [shards(): sums[i] = (onward(sums[i]).astype(F32) + part(i, s + 1)).astype(BF)]
    ppermute x4 -> x2, starting transfers between devices: 10.4 us -> 2.16 us  [shards(): got.append(lax.ppermute(bc_own, 'outc', pairs))]
    unnamed x79 -> x55, local copies, waits for them, and re-layouts: 22.7 us -> 14.8 us
    ppermute x4 -> x2, waiting for transfers between devices: 4.63 us -> 0.01 us  [shards(): got.append(lax.ppermute(bc_own, 'outc', pairs))]
    pallas_call x7 -> x9, Pallas kernels: 51.2 us -> 48.2 us  [the longest x4 29.1 us: project(): pl.pallas_call(functools.partial(project_kernel, parts, len(olds)), grid_...]
  transfers between devices with their start and end apart: 70 -> 38, of which waited for: 22 -> 17; matrix products, arithmetic and copies ran while one was open for 11% -> 12% of each run, Pallas kernels for 29% -> 24%
where the time goes in v2:
time: 194 us; the launch traced here: 193 us
  Pallas kernels  68.9 us (36%)
  waiting for transfers between devices  40.1 us (21%)
  starting transfers between devices  39.1 us (20%)
  local copies, waits for them, and re-layouts  23.2 us (12%)
  other arithmetic  15.7 us (8%)
  between operations  6.37 us (3%)
    ppermute x28, starting transfers between devices, onward(): return lax.ppermute(a, ('outc', 'inc'), ring)  29.4 us
    pallas_call x4, Pallas kernels, project(): pl.pallas_call(functools.partial(project_kernel, parts, len(olds)), grid_...  29.1 us
    ppermute x28, waiting for transfers between devices, onward(): return lax.ppermute(a, ('outc', 'inc'), ring)  25.7 us
    pallas_call x4, Pallas kernels, relayout(): pl.pallas_call(kernel, grid=(steps,), in_specs=specs, out_specs=pl.BlockS...  17.9 us
    unnamed x55, local copies, waits for them, and re-layouts  14.8 us
    ppermute x3, waiting for transfers between devices, shards(): got = lax.ppermute(history_bc, 'outc', [(i, i ^ width) for i in range(n)])  13.3 us
    convert_element_type x14, other arithmetic, shards(): sums[i] = (onward(sums[i]).astype(F32) + part(i, s + 1)).astype(BF)  11.2 us
    pallas_call x1, Pallas kernels, ssm(): pl.pallas_call(ssm_kernel, grid=(rows // rb,), in_specs=[row_spec(a) for...  8.1 us
  transfers between devices with their start and end apart: 38, of which 17 were waited for; matrix products, arithmetic and copies ran while one was open for 12% of the time, Pallas kernels for 24%

profile of v2, /device:TPU:0, one launch (start us, length us, event | category | flops | bytes accessed | tf_op | source)
XLA Modules:
  0.0 193.3 jit_solution(4005128450878419694)
XLA Ops:
  1.7 3.1 %collective-permute-start.7 = (bf16[32,4096]{1,0:T(8,128)(2,1)S(1)}, bf16[32,4096]{1,0:T(8,128)(2,1)S(1)}, u32[]{:S(2)}, u32[]{:S(2)}) collective-permute-start(bf16[32,4096]{1,0:T(8,128)(2,1)S(1)} %get-tuple-element.106.refs_0_), channel_id=1, source_target_pairs={{0,4},{4,8},{8,12},{12,14},{14,10},{10,6},{6,2},{2,0},{5,1},{9,5},... | collective-permute-start | bytes 786440 | tf_op jit(solution)/shard_map/ppermute | solution.py:465
  6.4 4.5 %relayout.4._ = bf16[2,4096,1024]{2,1,0:T(8,128)(2,1)} custom-call(bf16[4096,16,128]{2,1,0:T(8,128)(2,1)} %w_ref.7), custom_call_target="tpu_custom_call" | custom-call | flops 1073741824 | bytes 8388608 | tf_op jit(solution)/shard_map/relayout/pallas_call | solution.py:77
  14.5 4.6 %relayout.5._ = bf16[2,4096,1024]{2,1,0:T(8,128)(2,1)} custom-call(bf16[4096,16,128]{2,1,0:T(8,128)(2,1)} %w_ref.7, bf16[2,4096,1024]{2,1,0:T(8,128)(2,1)} %relayout.4._), custom_call_target="tpu_custom_call", output_to_operand_aliasing={{}: (1, {})} | custom-call | flops 1073741824 | bytes 8388608 | tf_op jit(solution)/shard_map/relayout/pallas_call | solution.py:77
  24.7 4.4 %relayout.6._ = bf16[2,4096,1024]{2,1,0:T(8,128)(2,1)} custom-call(bf16[4096,16,128]{2,1,0:T(8,128)(2,1)} %w_ref.7, bf16[2,4096,1024]{2,1,0:T(8,128)(2,1)} %relayout.5._), custom_call_target="tpu_custom_call", output_to_operand_aliasing={{}: (1, {})} | custom-call | flops 1073741824 | bytes 8388608 | tf_op jit(solution)/shard_map/relayout/pallas_call | solution.py:77
  32.7 4.5 %relayout.7.refs_8_ = bf16[2,4096,1024]{2,1,0:T(8,128)(2,1)} custom-call(bf16[4096,16,128]{2,1,0:T(8,128)(2,1)} %w_ref.7, bf16[2,4096,1024]{2,1,0:T(8,128)(2,1)} %relayout.6._), custom_call_target="tpu_custom_call", output_to_operand_aliasing={{}: (1, {})} | custom-call | flops 1073741824 | bytes 8388608 | tf_op jit(solution)/shard_map/relayout/pallas_call | solution.py:77
  40.5 8.5 %project.4 = (bf16[256,1024]{1,0:T(8,128)(2,1)}, f32[256,256]{1,0:T(8,128)S(1)}) custom-call(s32[8]{0:T(128)S(1)} %gather_fusion, s32[1]{0:T(128)S(6)} %sub.19.which_ref, bf16[32,4096]{1,0:T(8,128)(2,1)S(1)} %get-tuple-element.106.refs_0_, bf16[32,4096]{1,0:T(8,128)(2,1)S(1)} %get-tuple-element.107.refs_1_, ...), custom_call_target="tpu_custom_call" | custom-call | flops 2684354560 | bytes 10485760 | tf_op jit(solution)/shard_map/project/pallas_call | solution.py:138
  51.0 6.2 %project.5.refs_10_ = f32[256,1024]{1,0:T(8,128)} custom-call(s32[8]{0:T(128)S(1)} %gather_fusion, s32[1]{0:T(128)} %bitcast.12.which_ref.inc_ref, bf16[32,4096]{1,0:T(8,128)(2,1)S(1)} %get-tuple-element.106.refs_0_, bf16[32,4096]{1,0:T(8,128)(2,1)S(1)} %get-tuple-element.107.refs_1_, bf16[32,4096]{1,0:T(8,128)(2,1)S(1)} %collective-permute-done.7.refs_2_, ...), custom_call_target="tpu_custom_call" | custom-call | flops 2684354560 | bytes 10485760 | tf_op jit(solution)/shard_map/project/pallas_call | solution.py:138
  62.4 4.0 %collective-permute-done.6.refs_7_ = bf16[32,4096]{1,0:T(8,128)(2,1)S(1)} collective-permute-done((bf16[32,4096]{1,0:T(8,128)(2,1)S(1)}, bf16[32,4096]{1,0:T(8,128)(2,1)S(1)}, u32[]{:S(2)}, u32[]{:S(2)}) %collective-permute-start.6) | collective-permute-done | bytes 262176 | tf_op jit(solution)/shard_map/ppermute | solution.py:465
  67.8 7.8 %project.6 = (bf16[512,1024]{1,0:T(8,128)(2,1)}, f32[512,256]{1,0:T(8,128)}, bf16[512,256]{1,0:T(8,128)(2,1)S(1)}) custom-call(s32[8]{0:T(128)S(1)} %gather_fusion, s32[1]{0:T(128)S(6)} %sub.19.which_ref, bf16[32,4096]{1,0:T(8,128)(2,1)S(1)} %collective-permute-done.10.refs_0_, bf16[32,4096]{1,0:T(8,128)(2,1)S(1)} %collective-permute-done.3.refs_1_, ...), custom_call_target="tpu_custom_call" | custom-call | flops 2684354560 | bytes 10485760 | tf_op jit(solution)/shard_map/project/pallas_call | solution.py:138
  81.4 6.6 %project.7.mine_ref = f32[512,1024]{1,0:T(8,128)} custom-call(s32[8]{0:T(128)S(1)} %gather_fusion, s32[1]{0:T(128)} %bitcast.12.which_ref.inc_ref, bf16[32,4096]{1,0:T(8,128)(2,1)S(1)} %collective-permute-done.10.refs_0_, bf16[32,4096]{1,0:T(8,128)(2,1)S(1)} %collective-permute-done.3.refs_1_, bf16[32,4096]{1,0:T(8,128)(2,1)S(1)} %collective-permute-done.11.refs_2_, ...), custom_call_target="tpu_custom_call" | custom-call | flops 2684354560 | bytes 10485760 | tf_op jit(solution)/shard_map/project/pallas_call | solution.py:138
  89.8 8.1 %ssm.1 = (bf16[512,512]{1,0:T(8,128)(2,1)S(1)}, f32[8,512]{1,0:T(8,128)S(1)}, bf16[512,512]{1,0:T(8,128)(2,1)S(1)}, bf16[512,128]{1,0:T(8,128)(2,1)S(1)}, f32[51...) custom-call(s32[8,1,64,2]{3,2,1,0:T(8,128)S(1)} %bitcast.37, bf16[512,1024]{1,0:T(8,128)(2,1)} %collective-permute-done.15.recv_ref, ...), custom_call_target="tpu_custom_call" | custom-call | flops 2147483648 | bytes 25165824 | tf_op jit(solution)/shard_map/ssm/pallas_call | solution.py:292
  106.4 4.3 %collective-permute-start.20 = (f32[8,512]{1,0:T(8,128)S(1)}, f32[8,512]{1,0:T(8,128)S(1)}, u32[]{:S(2)}, u32[]{:S(2)}) collective-permute-start(f32[8,512]{1,0:T(8,128)S(1)} %add.180), channel_id=1, source_target_pairs={{0,2},{2,0},{4,6},{6,4},{8,10},{10,8},{12,14},{14,12},{1,3},{3,1},... | collective-permute-start | bytes 49160 | tf_op jit(solution)/shard_map/ppermute | solution.py:572
  110.7 3.4 %copy-done.1 = bf16[64,8,64,128]{3,2,1,0:T(8,128)(2,1)S(1)} copy-done((bf16[64,8,64,128]{3,2,1,0:T(8,128)(2,1)S(1)}, bf16[64,8,64,128]{3,2,1,0:T(8,128)(2,1)}, u32[]{:S(2)}) %copy-start.1) | copy-done | bytes 8388632
  115.1 5.5 %new_state.1 = (bf16[8,1,8,512,128]{4,3,2,1,0:T(8,128)(2,1)}, bf16[512,512]{1,0:T(8,128)(2,1)S(1)}) custom-call(s32[8,1,64,2]{3,2,1,0:T(8,128)S(1)} %bitcast.39, bf16[512,512]{1,0:T(8,128)(2,1)S(1)} %get-tuple-element.87.xw_ref, bf16[512,128]{1,0:T(8,128)(2,1)S(1)} %get-tuple-element.88.bconv_ref, f32[512,128]{1,0:T(8,128)S(1)} %get-tuple-element.89.sw_ref, ...), custom_call_target="tpu_custom_call" | custom-call | flops 2147483648 | bytes 33554432 | tf_op jit(solution)/shard_map/new_state/pallas_call | solution.py:394
  121.7 3.4 %copy-done = bf16[1024,4096]{1,0:T(8,128)(2,1)S(1)} copy-done((bf16[1024,4096]{1,0:T(8,128)(2,1)S(1)}, bf16[1024,4096]{1,0:T(8,128)(2,1)}, u32[]{:S(2)}) %copy-start) | copy-done | bytes 8388632
  125.1 3.5 %out_project.2 = f32[512,2048]{1,0:T(8,128)S(1)} custom-call(s32[1]{0:T(128)} %bitcast.12.which_ref.inc_ref, bf16[512,512]{1,0:T(8,128)(2,1)S(1)} %get-tuple-element.85.mine_ref, bf16[512,512]{1,0:T(8,128)(2,1)S(1)} %collective-permute-done.18.theirs_ref, bf16[1024,4096]{1,0:T(8,128)(2,1)S(1)} %copy-done, bf16[1024,4096]{1,0:T(8,128)(2,1)S(1)} %copy-done, ...), custom_call_target="tpu_custom_call" | custom-call | flops 2147483648 | bytes 8388608 | tf_op jit(solution)/shard_map/out_project/pallas_call | solution.py:421
  128.6 3.5 %out_project.3 = f32[512,2048]{1,0:T(8,128)S(1)} custom-call(s32[1]{0:T(128)} %bitcast.12.which_ref.inc_ref, bf16[512,512]{1,0:T(8,128)(2,1)S(1)} %get-tuple-element.85.mine_ref, bf16[512,512]{1,0:T(8,128)(2,1)S(1)} %collective-permute-done.18.theirs_ref, bf16[1024,4096]{1,0:T(8,128)(2,1)S(1)} %copy-done, bf16[1024,4096]{1,0:T(8,128)(2,1)S(1)} %copy-done, ...), custom_call_target="tpu_custom_call" | custom-call | flops 2147483648 | bytes 8388608 | tf_op jit(solution)/shard_map/out_project/pallas_call | solution.py:421
  134.4 4.8 %collective-permute-done.21 = bf16[1,192,128]{2,1,0:T(8,128)(2,1)S(1)} collective-permute-done((bf16[1,192,128]{2,1,0:T(8,128)(2,1)S(1)}, bf16[1,192,128]{2,1,0:T(8,128)(2,1)S(1)}, u32[]{:S(2)}, u32[]{:S(2)}) %collective-permute-start.21) | collective-permute-done | bytes 49184 | tf_op jit(solution)/shard_map/ppermute | solution.py:589
  142.9 2.5 %collective-permute-done.23 = bf16[2,192,128]{2,1,0:T(8,128)(2,1)S(1)} collective-permute-done((bf16[2,192,128]{2,1,0:T(8,128)(2,1)S(1)}, bf16[2,192,128]{2,1,0:T(8,128)(2,1)S(1)}, u32[]{:S(2)}, u32[]{:S(2)}) %collective-permute-start.23) | collective-permute-done | bytes 98336 | tf_op jit(solution)/shard_map/ppermute | solution.py:589
  151.1 6.0 %collective-permute-done.37 = bf16[4,192,128]{2,1,0:T(8,128)(2,1)S(1)} collective-permute-done((bf16[4,192,128]{2,1,0:T(8,128)(2,1)S(1)}, bf16[4,192,128]{2,1,0:T(8,128)(2,1)S(1)}, u32[]{:S(2)}, u32[]{:S(2)}) %collective-permute-start.37) | collective-permute-done | bytes 196640 | tf_op jit(solution)/shard_map/ppermute | solution.py:589
  163.0 3.0 %collective-permute-done.26 = bf16[64,2048]{1,0:T(8,128)(2,1)S(1)} collective-permute-done((bf16[64,2048]{1,0:T(8,128)(2,1)S(1)}, bf16[64,2048]{1,0:T(8,128)(2,1)S(1)}, u32[]{:S(2)}, u32[]{:S(2)}) %collective-permute-start.26) | collective-permute-done | bytes 262176 | tf_op jit(solution)/shard_map/ppermute | solution.py:465
  170.5 3.0 %collective-permute-done.27 = bf16[64,2048]{1,0:T(8,128)(2,1)S(1)} collective-permute-done((bf16[64,2048]{1,0:T(8,128)(2,1)S(1)}, bf16[64,2048]{1,0:T(8,128)(2,1)S(1)}, u32[]{:S(2)}, u32[]{:S(2)}) %collective-permute-start.27) | collective-permute-done | bytes 262176 | tf_op jit(solution)/shard_map/ppermute | solution.py:465
  178.1 3.0 %collective-permute-done.28 = bf16[64,2048]{1,0:T(8,128)(2,1)S(1)} collective-permute-done((bf16[64,2048]{1,0:T(8,128)(2,1)S(1)}, bf16[64,2048]{1,0:T(8,128)(2,1)S(1)}, u32[]{:S(2)}, u32[]{:S(2)}) %collective-permute-start.28) | collective-permute-done | bytes 262176 | tf_op jit(solution)/shard_map/ppermute | solution.py:465
  185.6 3.0 %collective-permute-done.29 = bf16[64,2048]{1,0:T(8,128)(2,1)S(1)} collective-permute-done((bf16[64,2048]{1,0:T(8,128)(2,1)S(1)}, bf16[64,2048]{1,0:T(8,128)(2,1)S(1)}, u32[]{:S(2)}, u32[]{:S(2)}) %collective-permute-start.29) | collective-permute-done | bytes 262176 | tf_op jit(solution)/shard_map/ppermute | solution.py:465
  (178 shorter events, 76.0 us)
Async XLA Ops:
  1.7 9.1 %collective-permute-start.7 = (bf16[32,4096]{1,0:T(8,128)(2,1)S(1)}, bf16[32,4096]{1,0:T(8,128)(2,1)S(1)}, u32[]{:S(2)}, u32[]{:S(2)}) collective-permute-start(bf16[32,4096]{1,0:T(8,128)(2,1)S(1)} %get-tuple-element.106.refs_0_), channel_id=1, source_target_pairs={{0,4},{4,8},{8,12},{12,14},{14,10},{10,6},{6,2},{2,0},{5,1},{9,5},... | collective-permute-start | bytes 786440 | tf_op jit(solution)/shard_map/ppermute | solution.py:465
  4.8 7.6 %collective-permute-start = (bf16[32,4096]{1,0:T(8,128)(2,1)S(1)}, bf16[32,4096]{1,0:T(8,128)(2,1)S(1)}, u32[]{:S(2)}, u32[]{:S(2)}) collective-permute-start(bf16[32,4096]{1,0:T(8,128)(2,1)S(1)} %get-tuple-element.107.refs_1_), channel_id=1, source_target_pairs={{0,4},{4,8},{8,12},{12,14},{14,10},{10,6},{6,2},{2,0},{5,1},{9,5},... | collective-permute-start | bytes 786440 | tf_op jit(solution)/shard_map/ppermute | solution.py:465
  10.8 8.3 %collective-permute-start.8 = (bf16[32,4096]{1,0:T(8,128)(2,1)S(1)}, bf16[32,4096]{1,0:T(8,128)(2,1)S(1)}, u32[]{:S(2)}, u32[]{:S(2)}) collective-permute-start(bf16[32,4096]{1,0:T(8,128)(2,1)S(1)} %collective-permute-done.7.refs_2_), channel_id=1, source_target_pairs={{0,4},{4,8},{8,12},{12,14},{14,10},{10,6},{6,2},{2,0},{5,1},{9,5},... | collective-permute-start | bytes 786440 | tf_op jit(solution)/shard_map/ppermute | solution.py:465
  12.4 8.3 %collective-permute-start.1 = (bf16[32,4096]{1,0:T(8,128)(2,1)S(1)}, bf16[32,4096]{1,0:T(8,128)(2,1)S(1)}, u32[]{:S(2)}, u32[]{:S(2)}) collective-permute-start(bf16[32,4096]{1,0:T(8,128)(2,1)S(1)} %collective-permute-done.refs_3_), channel_id=1, source_target_pairs={{0,4},{4,8},{8,12},{12,14},{14,10},{10,6},{6,2},{2,0},{5,1},{9,5},... | collective-permute-start | bytes 786440 | tf_op jit(solution)/shard_map/ppermute | solution.py:465
  19.1 10.0 %collective-permute-start.9 = (bf16[32,4096]{1,0:T(8,128)(2,1)S(1)}, bf16[32,4096]{1,0:T(8,128)(2,1)S(1)}, u32[]{:S(2)}, u32[]{:S(2)}) collective-permute-start(bf16[32,4096]{1,0:T(8,128)(2,1)S(1)} %collective-permute-done.8.refs_4_), channel_id=1, source_target_pairs={{0,4},{4,8},{8,12},{12,14},{14,10},{10,6},{6,2},{2,0},{5,1},{9,5},... | collective-permute-start | bytes 786440 | tf_op jit(solution)/shard_map/ppermute | solution.py:465
  20.7 9.9 %collective-permute-start.2 = (bf16[32,4096]{1,0:T(8,128)(2,1)S(1)}, bf16[32,4096]{1,0:T(8,128)(2,1)S(1)}, u32[]{:S(2)}, u32[]{:S(2)}) collective-permute-start(bf16[32,4096]{1,0:T(8,128)(2,1)S(1)} %collective-permute-done.1.refs_5_), channel_id=1, source_target_pairs={{0,4},{4,8},{8,12},{12,14},{14,10},{10,6},{6,2},{2,0},{5,1},{9,5},... | collective-permute-start | bytes 786440 | tf_op jit(solution)/shard_map/ppermute | solution.py:465
  29.1 8.0 %collective-permute-start.10 = (bf16[32,4096]{1,0:T(8,128)(2,1)S(1)}, bf16[32,4096]{1,0:T(8,128)(2,1)S(1)}, u32[]{:S(2)}, u32[]{:S(2)}) collective-permute-start(bf16[32,4096]{1,0:T(8,128)(2,1)S(1)} %collective-permute-done.9.refs_6_), channel_id=1, source_target_pairs={{0,4},{4,8},{8,12},{12,14},{14,10},{10,6},{6,2},{2,0},{5,1},{9,5},... | collective-permute-start | bytes 786440 | tf_op jit(solution)/shard_map/ppermute | solution.py:465
  30.6 7.7 %collective-permute-start.3 = (bf16[32,4096]{1,0:T(8,128)(2,1)S(1)}, bf16[32,4096]{1,0:T(8,128)(2,1)S(1)}, u32[]{:S(2)}, u32[]{:S(2)}) collective-permute-start(bf16[32,4096]{1,0:T(8,128)(2,1)S(1)} %collective-permute-done.2.refs_7_), channel_id=1, source_target_pairs={{0,4},{4,8},{8,12},{12,14},{14,10},{10,6},{6,2},{2,0},{5,1},{9,5},... | collective-permute-start | bytes 786440 | tf_op jit(solution)/shard_map/ppermute | solution.py:465
  37.1 12.5 %collective-permute-start.11 = (bf16[32,4096]{1,0:T(8,128)(2,1)S(1)}, bf16[32,4096]{1,0:T(8,128)(2,1)S(1)}, u32[]{:S(2)}, u32[]{:S(2)}) collective-permute-start(bf16[32,4096]{1,0:T(8,128)(2,1)S(1)} %collective-permute-done.10.refs_0_), channel_id=1, source_target_pairs={{0,4},{4,8},{8,12},{12,14},{14,10},{10,6},{6,2},{2,0},{5,1},{9,5},... | collective-permute-start | bytes 786440 | tf_op jit(solution)/shard_map/ppermute | solution.py:465
  38.3 11.8 %collective-permute-start.4 = (bf16[32,4096]{1,0:T(8,128)(2,1)S(1)}, bf16[32,4096]{1,0:T(8,128)(2,1)S(1)}, u32[]{:S(2)}, u32[]{:S(2)}) collective-permute-start(bf16[32,4096]{1,0:T(8,128)(2,1)S(1)} %collective-permute-done.3.refs_1_), channel_id=1, source_target_pairs={{0,4},{4,8},{8,12},{12,14},{14,10},{10,6},{6,2},{2,0},{5,1},{9,5},... | collective-permute-start | bytes 786440 | tf_op jit(solution)/shard_map/ppermute | solution.py:465
  49.7 7.5 %collective-permute-start.12 = (bf16[32,4096]{1,0:T(8,128)(2,1)S(1)}, bf16[32,4096]{1,0:T(8,128)(2,1)S(1)}, u32[]{:S(2)}, u32[]{:S(2)}) collective-permute-start(bf16[32,4096]{1,0:T(8,128)(2,1)S(1)} %collective-permute-done.11.refs_2_), channel_id=1, source_target_pairs={{0,4},{4,8},{8,12},{12,14},{14,10},{10,6},{6,2},{2,0},{5,1},{9,5},... | collective-permute-start | bytes 786440 | tf_op jit(solution)/shard_map/ppermute | solution.py:465
  50.1 8.7 %collective-permute-start.5 = (bf16[32,4096]{1,0:T(8,128)(2,1)S(1)}, bf16[32,4096]{1,0:T(8,128)(2,1)S(1)}, u32[]{:S(2)}, u32[]{:S(2)}) collective-permute-start(bf16[32,4096]{1,0:T(8,128)(2,1)S(1)} %collective-permute-done.4.refs_3_), channel_id=1, source_target_pairs={{0,4},{4,8},{8,12},{12,14},{14,10},{10,6},{6,2},{2,0},{5,1},{9,5},... | collective-permute-start | bytes 786440 | tf_op jit(solution)/shard_map/ppermute | solution.py:465
  57.2 9.9 %collective-permute-start.13 = (bf16[32,4096]{1,0:T(8,128)(2,1)S(1)}, bf16[32,4096]{1,0:T(8,128)(2,1)S(1)}, u32[]{:S(2)}, u32[]{:S(2)}) collective-permute-start(bf16[32,4096]{1,0:T(8,128)(2,1)S(1)} %collective-permute-done.12.refs_4_), channel_id=1, source_target_pairs={{0,4},{4,8},{8,12},{12,14},{14,10},{10,6},{6,2},{2,0},{5,1},{9,5},... | collective-permute-start | bytes 786440 | tf_op jit(solution)/shard_map/ppermute | solution.py:465
  75.6 12.6 %collective-permute-start.15 = (bf16[512,1024]{1,0:T(8,128)(2,1)}, bf16[512,1024]{1,0:T(8,128)(2,1)}, u32[]{:S(2)}, u32[]{:S(2)}) collective-permute-start(bf16[512,1024]{1,0:T(8,128)(2,1)} %get-tuple-element.73), channel_id=1, source_target_pairs={{0,1},{1,0},{2,3},{3,2},{4,5},{5,4},{6,7},{7,6},{8,9},{9,8},{10,11... | collective-permute-start | bytes 3145736 | tf_op jit(solution)/shard_map/ppermute | solution.py:468
  78.3 9.9 %collective-permute-start.16 = (bf16[512,128]{1,0:T(8,128)(2,1)S(1)}, bf16[512,128]{1,0:T(8,128)(2,1)S(1)}, u32[]{:S(2)}, u32[]{:S(2)}) collective-permute-start(bf16[512,128]{1,0:T(8,128)(2,1)S(1)} %slice.66.raw_ref), channel_id=1, source_target_pairs={{8,0},{0,2},{10,4},{2,6},{12,8},{4,10},{14,12},{6,14},{9,1},{1,3},... | collective-permute-start | bytes 393224 | tf_op jit(solution)/shard_map/ppermute | solution.py:550
  79.6 8.6 %collective-permute-start.17 = (bf16[512,128]{1,0:T(8,128)(2,1)S(1)}, bf16[512,128]{1,0:T(8,128)(2,1)S(1)}, u32[]{:S(2)}, u32[]{:S(2)}) collective-permute-start(bf16[512,128]{1,0:T(8,128)(2,1)S(1)} %slice.66.raw_ref), channel_id=1, source_target_pairs={{0,0},{8,2},{2,4},{10,6},{4,8},{12,10},{6,12},{14,14},{1,1},{9,3},... | collective-permute-start | bytes 393224 | tf_op jit(solution)/shard_map/ppermute | solution.py:550
  98.7 23.0 %collective-permute-start.18 = (bf16[512,512]{1,0:T(8,128)(2,1)S(1)}, bf16[512,512]{1,0:T(8,128)(2,1)S(1)}, u32[]{:S(2)}, u32[]{:S(2)}) collective-permute-start(bf16[512,512]{1,0:T(8,128)(2,1)S(1)} %get-tuple-element.85.mine_ref), channel_id=1, source_target_pairs={{0,1},{1,0},{2,3},{3,2},{4,5},{5,4},{6,7},{7,6},{8,9},{9,8},{10,11... | collective-permute-start | bytes 1572872 | tf_op jit(solution)/shard_map/ppermute | solution.py:468
  98.7 7.6 %collective-permute-start.19 = (f32[8,512]{1,0:T(8,128)S(1)}, f32[8,512]{1,0:T(8,128)S(1)}, u32[]{:S(2)}, u32[]{:S(2)}) collective-permute-start(f32[8,512]{1,0:T(8,128)S(1)} %get-tuple-element.86), channel_id=1, source_target_pairs={{0,1},{1,0},{2,3},{3,2},{4,5},{5,4},{6,7},{7,6},{8,9},{9,8},{10,11... | collective-permute-start | bytes 49160 | tf_op jit(solution)/shard_map/ppermute | solution.py:468
  106.4 15.3 %collective-permute-start.20 = (f32[8,512]{1,0:T(8,128)S(1)}, f32[8,512]{1,0:T(8,128)S(1)}, u32[]{:S(2)}, u32[]{:S(2)}) collective-permute-start(f32[8,512]{1,0:T(8,128)S(1)} %add.180), channel_id=1, source_target_pairs={{0,2},{2,0},{4,6},{6,4},{8,10},{10,8},{12,14},{14,12},{1,3},{3,1},... | collective-permute-start | bytes 49160 | tf_op jit(solution)/shard_map/ppermute | solution.py:572
  134.3 7.6 %collective-permute-start.30 = (bf16[64,2048]{1,0:T(8,128)(2,1)S(1)}, bf16[64,2048]{1,0:T(8,128)(2,1)S(1)}, u32[]{:S(2)}, u32[]{:S(2)}) collective-permute-start(bf16[64,2048]{1,0:T(8,128)(2,1)S(1)} %dynamic-slice_convert_fusion), channel_id=1, source_target_pairs={{0,4},{4,8},{8,12},{12,14},{14,10},{10,6},{6,2},{2,0},{5,1},{9,5},... | collective-permute-start | bytes 786440 | tf_op jit(solution)/shard_map/ppermute | solution.py:465
  145.7 11.4 %collective-permute-start.37 = (bf16[4,192,128]{2,1,0:T(8,128)(2,1)S(1)}, bf16[4,192,128]{2,1,0:T(8,128)(2,1)S(1)}, u32[]{:S(2)}, u32[]{:S(2)}) collective-permute-start(bf16[4,192,128]{2,1,0:T(8,128)(2,1)S(1)} %maximum_select_fusion.1), channel_id=1, source_target_pairs={{0,8},{2,10},{4,12},{6,14},{8,0},{10,2},{12,4},{14,6},{1,9},{3,11}... | collective-permute-start | bytes 589832 | tf_op jit(solution)/shard_map/ppermute | solution.py:589
  146.3 12.1 %collective-permute-start.25 = (bf16[64,2048]{1,0:T(8,128)(2,1)S(1)}, bf16[64,2048]{1,0:T(8,128)(2,1)S(1)}, u32[]{:S(2)}, u32[]{:S(2)}) collective-permute-start(bf16[64,2048]{1,0:T(8,128)(2,1)S(1)} %add_convert_fusion.12), channel_id=1, source_target_pairs={{0,4},{4,8},{8,12},{12,14},{14,10},{10,6},{6,2},{2,0},{5,1},{9,5},... | collective-permute-start | bytes 786440 | tf_op jit(solution)/shard_map/ppermute | solution.py:465
  148.9 10.7 %collective-permute-start.32 = (bf16[64,2048]{1,0:T(8,128)(2,1)S(1)}, bf16[64,2048]{1,0:T(8,128)(2,1)S(1)}, u32[]{:S(2)}, u32[]{:S(2)}) collective-permute-start(bf16[64,2048]{1,0:T(8,128)(2,1)S(1)} %add_convert_fusion.5), channel_id=1, source_target_pairs={{0,4},{4,8},{8,12},{12,14},{14,10},{10,6},{6,2},{2,0},{5,1},{9,5},... | collective-permute-start | bytes 786440 | tf_op jit(solution)/shard_map/ppermute | solution.py:465
  160.7 8.1 %collective-permute-start.33 = (bf16[64,2048]{1,0:T(8,128)(2,1)S(1)}, bf16[64,2048]{1,0:T(8,128)(2,1)S(1)}, u32[]{:S(2)}, u32[]{:S(2)}) collective-permute-start(bf16[64,2048]{1,0:T(8,128)(2,1)S(1)} %add_convert_fusion.4), channel_id=1, source_target_pairs={{0,4},{4,8},{8,12},{12,14},{14,10},{10,6},{6,2},{2,0},{5,1},{9,5},... | collective-permute-start | bytes 786440 | tf_op jit(solution)/shard_map/ppermute | solution.py:465
  (39 other events, 256.6 us)

commit v3 on v2

--- a/solution.py
+++ b/solution.py
@@ -147,18 +147,60 @@
         ),
         out_shape=[jax.ShapeDtypeStruct((out_m, cols), dtype)]
         + [jax.ShapeDtypeStruct((out_m, ext_cols), d) for d in ext_dtypes],
-        compiler_params=params(52),
+        compiler_params=params(46),
         cost_estimate=cost(2 * m * k * (cols + ext_cols), 2 * k * cols + 2 * m * k),
         name="project",
     )(seq, which, *ins, w, w_ext, *olds)
 
 
+def extra_kernel(parts, seq_ref, *refs):
+    ins, ext_ref, old_ref, o_ref, rows = refs[:parts], *refs[parts:]
+    piece = ins[0].shape[0]
+    blocks = parts // STREAMS
+    rc = piece * STREAMS
+    for i in range(parts):
+        rows[i * piece : (i + 1) * piece, :] = ins[i][...]
+    total = jnp.dot(rows[...], ext_ref[...], preferred_element_type=F32)
+    for i in range(blocks):
+        at = pl.ds(pl.multiple_of(seq_ref[i] * rc, 16), rc)
+        o_ref[at, :] = old_ref[i * rc : (i + 1) * rc, :]
+        at = pl.ds(pl.multiple_of(seq_ref[blocks + i] * rc, 16), rc)
+        o_ref[at, :] = total[i * rc : (i + 1) * rc]
+
+
+def extra(seq, ins, w_ext, old):
+    parts = len(ins)
+    piece, k = ins[0].shape
+    m, cols = old.shape
+    args = [*ins, w_ext, old]
+    return pl.pallas_call(
+        functools.partial(extra_kernel, parts),
+        grid_spec=pltpu.PrefetchScalarGridSpec(
+            num_scalar_prefetch=1,
+            grid=(1,),
+            in_specs=[whole_block(a.shape) for a in args],
+            out_specs=whole_block((2 * m, cols)),
+            scratch_shapes=[pltpu.VMEM((m, k), BF)],
+        ),
+        out_shape=jax.ShapeDtypeStruct((2 * m, cols), F32),
+        compiler_params=params(46),
+        cost_estimate=cost(2 * m * k * cols, 2 * m * k + 2 * k * cols),
+        name="extra",
+    )(seq, *args)
+
+
 def silu(v):
     return v / (1.0 + jnp.exp(-v))
 
 
+def history_rows(state):
+    state = state.astype(F32)
+    return jnp.concatenate([jnp.zeros((state.shape[0], DRAFT - KW + 1, state.shape[2]), F32), state], axis=1)
+
+
 def ssm_kernel(
-    meta_ref, recv_ref, mine_ref, dt_ref, braw_ref, craw_ref, prevx_ref, prevb_ref, prevc_ref, tapx_ref, tapb_ref, tapc_ref, bias_ref, rate_ref, skip_ref, gain_ref, state_ref,
+    group_ref, meta_ref, recv_ref, mine_ref, dt_ref, braw_ref, craw_ref, prevx_ref, prevb_ref, prevc_ref,
+    tapx_ref, tapb_ref, tapc_ref, heads_ref, gain_ref, state_ref,
     gated_ref, ssq_ref, xw_ref, bconv_ref, sw_ref, xraw_ref,
 ):
     rb = recv_ref.shape[0]
@@ -173,10 +215,12 @@
     ]
     t3 = t.reshape(rb // DRAFT, DRAFT, 1)
 
-    def conv(x, prev, taps):
+    def pair(v, j):
+        return jnp.concatenate([v[2 * j : 2 * j + 1, :], v[2 * j + 1 : 2 * j + 2, :]], axis=1)
+
+    def conv(x, p3, taps):
         width = x.shape[1]
         x3 = x.reshape(rb // DRAFT, DRAFT, width)
-        p3 = prev.reshape(rb // DRAFT, DRAFT, width)
         total = x3 * taps[KW - 1 : KW, :].reshape(1, 1, width)
         for d in range(1, KW):
             source = jnp.where(t3 >= d, pltpu.roll(x3, d, 1), pltpu.roll(p3, d, 1))
@@ -190,19 +234,20 @@
         b = zx[:, (2 * j + 1) * LANES : (2 * j + 2) * LANES]
         gates.append(jnp.where(low, a, pltpu.roll(b, LANES // 2, 1)))
         xs.append(jnp.where(low, pltpu.roll(a, LANES // 2, 1), b))
-    prev_x = prevx_ref[...].reshape(rb, hp).astype(F32)
+    prev_x = history_rows(prevx_ref[...])
     convs = []
     for j in range(pairs):
         cut = slice(j * LANES, (j + 1) * LANES)
         xraw_ref[:, cut] = xs[j].astype(BF)
-        convs.append(conv(xs[j], prev_x[:, cut], tapx_ref[:, cut]))
-    b_conv = conv(braw_ref[...].astype(F32), prevb_ref[...].reshape(rb, LANES).astype(F32), tapb_ref[...])
-    c_conv = conv(craw_ref[...].astype(F32), prevc_ref[...].reshape(rb, LANES).astype(F32), tapc_ref[...])
+        taps = jnp.concatenate([pair(tapx_ref[k], j) for k in range(KW)], axis=0)
+        convs.append(conv(xs[j], prev_x[:, :, cut], taps))
+    b_conv = conv(braw_ref[...].astype(F32), history_rows(prevb_ref[...]), tapb_ref[...])
+    c_conv = conv(craw_ref[...].astype(F32), history_rows(prevc_ref[...]), tapc_ref[...])
     bconv_ref[...] = b_conv.astype(BF)
 
-    raw = dt_ref[...].astype(F32) + bias_ref[...]
+    raw = dt_ref[...].astype(F32) + heads_ref[0:1, :]
     step = jnp.maximum(raw, 0.0) + jnp.log1p(jnp.exp(-jnp.abs(raw)))
-    log_a = -step * rate_ref[...]
+    log_a = -step * heads_ref[1:2, :]
     ri = lax.broadcasted_iota(jnp.int32, (rb, rb), 0)
     ci = lax.broadcasted_iota(jnp.int32, (rb, rb), 1)
     same = (ri // DRAFT) == (ci // DRAFT)
@@ -218,7 +263,7 @@
     scores = lax.dot_general(c_conv, b_conv, NT, precision=HIGH, preferred_element_type=F32)
 
     def spread(v, j):
-        return jnp.where(low, v[:, 2 * j : 2 * j + 1], v[:, 2 * j + 1 : 2 * j + 2])
+        return jnp.where(low[: v.shape[0]], v[:, 2 * j : 2 * j + 1], v[:, 2 * j + 1 : 2 * j + 2])
 
     odd = (lax.broadcasted_iota(jnp.int32, (rb, 1), 0) & DRAFT) != 0
     c_pair = jnp.concatenate(
@@ -239,6 +284,7 @@
     counted = (t < acc) & jnp.logical_not((t < ss) & (ss < acc))
     weight = jnp.where(counted, jnp.exp(jnp.where(counted, cum_acc - cum, 0.0)), 0.0) * step
     sw_ref[...] = jnp.where(ss < acc, 0.0, jnp.exp(cum_acc))
+    skip = heads_ref[2:3, :]
     squares = jnp.zeros((rb, LANES), F32)
     for j in range(pairs):
         cut = slice(j * LANES, (j + 1) * LANES)
@@ -251,10 +297,10 @@
             [jnp.where(low, x_conv, 0.0).astype(BF), jnp.where(low, 0.0, x_conv).astype(BF)], axis=0
         )
         intra = jnp.dot(jnp.concatenate(mixes, axis=1), x_pair, preferred_element_type=F32)
-        mixed = spread(kept, j) * carried[:, cut] + intra + skip_ref[:, cut] * x_conv
+        mixed = spread(kept, j) * carried[:, cut] + intra + spread(skip, j) * x_conv
         gated = mixed * silu(gates[j])
         squares = squares + gated * gated
-        gated_ref[:, cut] = (gated * gain_ref[:, cut]).astype(BF)
+        gated_ref[:, cut] = (gated * pair(gain_ref, j)).astype(BF)
         xw_ref[:, cut] = (spread(weight, j) * x_conv).astype(BF)
     row_sum = jnp.broadcast_to(jnp.sum(squares, axis=1, keepdims=True), (rb, LANES))
     ssq_ref[...] = row_sum.T[:8]
@@ -275,34 +321,52 @@
     )
 
 
-def ssm(chunk, rb, per_row, tables, state):
-    rows = per_row[1].shape[0]
-    n, _, rq, hp, width_n = state.shape
-    rc = rq * DRAFT
-    ob = rb // rc
-
-    def row_spec(a):
-        if a.ndim == 2:
-            return pl.BlockSpec((rb, a.shape[1]), lambda i: (i, 0))
-        return pl.BlockSpec((ob, 1, rc, a.shape[3]), lambda i: (i, chunk, 0, 0))
+def ssm(group, rb, meta, recv, mine, dt, b_raw, c_raw, x_state, bc_state, conv_x, conv_bc, heads, gain, state):
+    rows = recv.shape[0]
+    _, _, rq, hp, width_n = state.shape
+    ob = rb // (rq * DRAFT)
+    reqs = rb // DRAFT
 
     def flat(w):
-        return pl.BlockSpec((rb, w), lambda i: (i, 0))
+        return pl.BlockSpec((rb, w), lambda i, group: (i, 0))
+
+    def columns(shape, which):
+        lead = (0,) * (len(shape) - 1)
+        if len(shape) == 3:
+            return pl.BlockSpec(shape, lambda i, group: (i, 0, which * G + group[0]))
+        return pl.BlockSpec(shape, lambda i, group: (*lead, which * G + group[0]))
 
     return pl.pallas_call(
         ssm_kernel,
-        grid=(rows // rb,),
-        in_specs=[row_spec(a) for a in per_row]
-        + [whole_block(a.shape) for a in tables]
-        + [pl.BlockSpec((ob, 1, rq, hp, width_n), lambda i: (i, chunk, 0, 0, 0))],
-        out_specs=[
-            flat(hp),
-            pl.BlockSpec((8, rb), lambda i: (0, i)),
-            flat(hp),
-            flat(LANES),
-            flat(LANES),
-            flat(hp),
-        ],
+        grid_spec=pltpu.PrefetchScalarGridSpec(
+            num_scalar_prefetch=1,
+            grid=(rows // rb,),
+            in_specs=[
+                flat(2),
+                flat(recv.shape[1]),
+                flat(mine.shape[1]),
+                flat(LANES),
+                flat(LANES),
+                flat(LANES),
+                pl.BlockSpec((reqs, KW - 1, hp), lambda i, group: (i, 0, 0)),
+                columns((reqs, KW - 1, LANES), 0),
+                columns((reqs, KW - 1, LANES), 1),
+                whole_block(conv_x.shape),
+                columns((KW, LANES), 0),
+                columns((KW, LANES), 1),
+                whole_block(heads.shape),
+                whole_block(gain.shape),
+                pl.BlockSpec((ob, 1, rq, hp, width_n), lambda i, group: (i, 0, 0, 0, 0)),
+            ],
+            out_specs=[
+                flat(hp),
+                pl.BlockSpec((8, rb), lambda i, group: (0, i)),
+                flat(hp),
+                flat(LANES),
+                flat(LANES),
+                flat(hp),
+            ],
+        ),
         out_shape=[
             jax.ShapeDtypeStruct((rows, hp), BF),
             jax.ShapeDtypeStruct((8, rows), F32),
@@ -311,10 +375,10 @@
             jax.ShapeDtypeStruct((rows, LANES), F32),
             jax.ShapeDtypeStruct((rows, hp), BF),
         ],
-        compiler_params=params(40),
+        compiler_params=params(46),
         cost_estimate=cost(2 * rows * hp * 4096, 6 * rows * hp * 16),
         name="ssm",
-    )(*per_row, *tables, state)
+    )(group, meta, recv, mine, dt, b_raw, c_raw, x_state, bc_state, bc_state, conv_x, conv_bc, conv_bc, heads, gain, state)
 
 
 def state_kernel(meta_ref, xw_ref, bconv_ref, sw_ref, xraw_ref, prevx_ref, state_ref, o_ref, tail_ref):
@@ -322,7 +386,7 @@
     width_p = LANES // 2
     ss = meta_ref[..., 0:1].reshape(rb, 1)
     acc = meta_ref[..., 1:2].reshape(rb, 1)
-    tail_ref[...] = pick_tail(ss, acc, xraw_ref[...], prevx_ref[...].reshape(rb, hp)).astype(BF)
+    tail_ref[...] = pick_tail(ss, acc, xraw_ref[...], history_rows(prevx_ref[...]).reshape(rb, hp)).astype(BF)
     request = lax.broadcasted_iota(jnp.int32, (rb, 1), 0) // DRAFT
     b_conv = bconv_ref[...].astype(F32)
     xw_t = xw_ref[...].astype(F32).T.astype(BF)
@@ -346,7 +410,7 @@
     rb = raw_ref.shape[0]
     ss = meta_ref[..., 0:1].reshape(rb, 1)
     acc = meta_ref[..., 1:2].reshape(rb, 1)
-    o_ref[...] = pick_tail(ss, acc, raw_ref[...], prev_ref[...]).astype(BF)
+    o_ref[...] = pick_tail(ss, acc, raw_ref[...], history_rows(prev_ref[...]).reshape(raw_ref.shape)).astype(BF)
 
 
 def new_history(rb, meta, raw, prev):
@@ -358,7 +422,7 @@
     return pl.pallas_call(
         tail_kernel,
         grid=(rows // rb,),
-        in_specs=[flat(2), flat(cols), flat(cols)],
+        in_specs=[flat(2), flat(cols), pl.BlockSpec((rb // DRAFT, KW - 1, cols), lambda i: (i, 0, 0))],
         out_specs=flat(cols),
         out_shape=jax.ShapeDtypeStruct((rows, cols), BF),
         compiler_params=params(24),
@@ -367,21 +431,27 @@
     )(meta, raw, prev)
 
 
-def new_state(chunk, rb, meta, xw, bconv, sw, xraw, prev_x, state, into):
+def new_state(piece, pieces, rb, meta, xw, bconv, sw, xraw, prev_x, state, into):
     rows, hp = xw.shape
     n, _, rq, _, width_n = state.shape
-    rc = rq * DRAFT
-    ob = rb // rc
-
-    def four(w):
-        return pl.BlockSpec((ob, 1, rc, w), lambda i: (i, chunk, 0, 0))
+    ob = rb // (rq * DRAFT)
+    steps = rows // rb // pieces
+    first = piece * steps
 
     def flat(w):
-        return pl.BlockSpec((rb, w), lambda i: (i, 0))
-
-    states = pl.BlockSpec((ob, 1, rq, hp, width_n), lambda i: (i, chunk, 0, 0, 0))
+        return pl.BlockSpec((rb, w), lambda i: (first + i, 0))
+
+    states = pl.BlockSpec((ob, 1, rq, hp, width_n), lambda i: (first + i, 0, 0, 0, 0))
     args = [meta, xw, bconv, sw, xraw, prev_x, state]
-    specs = [four(2), flat(hp), flat(LANES), flat(LANES), flat(hp), four(hp), states]
+    specs = [
+        flat(2),
+        flat(hp),
+        flat(LANES),
+        flat(LANES),
+        flat(hp),
+        pl.BlockSpec((rb // DRAFT, KW - 1, hp), lambda i: (first + i, 0, 0)),
+        states,
+    ]
     kernel, aliases = state_kernel, {}
     if into is not None:
         args.append(into)
@@ -393,13 +463,13 @@
 
     return pl.pallas_call(
         kernel,
-        grid=(rows // rb,),
+        grid=(steps,),
         in_specs=specs,
-        out_specs=[states, flat(hp)],
-        out_shape=[jax.ShapeDtypeStruct(state.shape, BF), jax.ShapeDtypeStruct((rows, hp), BF)],
+        out_specs=[states, pl.BlockSpec((rb, hp), lambda i: (i, 0))],
+        out_shape=[jax.ShapeDtypeStruct(state.shape, BF), jax.ShapeDtypeStruct((rows // pieces, hp), BF)],
         input_output_aliases=aliases,
         compiler_params=params(40),
-        cost_estimate=cost(2 * rows * hp * 4096, 8 * rows * hp * 16),
+        cost_estimate=cost(2 * rows * hp * 4096 // pieces, 8 * rows * hp * 16 // pieces),
         name="new_state",
     )(*args)
 
@@ -432,7 +502,7 @@
             ],
             out_specs=pl.BlockSpec((rows, bn), lambda j, inc: (0, j)),
         ),
-        out_shape=jax.ShapeDtypeStruct((rows, cols), F32),
+        out_shape=jax.ShapeDtypeStruct((rows, cols), BF),
         compiler_params=params(40),
         cost_estimate=cost(4 * rows * hp * cols, 4 * hp * cols + 4 * rows * cols),
         name="out_project",
@@ -450,15 +520,18 @@
     rows = n * rc
     rb = min(128, rows)
     order = list(range(0, n, 2)) + list(range(n - 1, 0, -2))
-    place = [order.index(i) for i in range(n)]
     ring = [(2 * order[i], 2 * order[(i + 1) % n]) for i in range(n)]
     ring += [(2 * order[(i + 1) % n] + 1, 2 * order[i] + 1) for i in range(n)]
     swap = [(0, 1), (1, 0)]
     me = lax.axis_index("outc")
     inc = lax.axis_index("inc")
-    pos = jnp.array(place, jnp.int32)[me]
-    steps = jnp.arange(n, dtype=jnp.int32)
-    seq = jnp.array(order, jnp.int32)[(pos + (2 * inc - 1) * steps) % n]
+    pos = jnp.where(me % 2 == 0, me // 2, n - 1 - me // 2)
+
+    def owner(step):
+        i = (pos + (2 * inc - 1) * step + n) % n
+        return jnp.where(i < n // 2, 2 * i, 2 * n - 1 - 2 * i)
+
+    seq = owner(jnp.arange(n, dtype=jnp.int32))
     inc1 = inc.astype(jnp.int32).reshape(1)
 
     def onward(a):
@@ -474,33 +547,15 @@
     if w_ext.shape[1] % LANES:
         w_ext = jnp.pad(w_ext, ((0, 0), (0, LANES - w_ext.shape[1] % LANES)))
 
-    def history(a):
-        a = a.reshape(req, KW - 1, -1)
-        a = jnp.pad(a, ((0, 0), (DRAFT - KW + 1, 0), (0, 0)))
-        return a.reshape(n, chunks, rc, a.shape[-1])
-
     def columns(a, start, size):
         return lax.dynamic_slice_in_dim(a, start, size, a.ndim - 1)
 
-    prev_x = history(conv_x_state)
-    prev_b = history(columns(conv_bc_state, group * width_n, width_n))
-    prev_c = history(columns(conv_bc_state, (G + group) * width_n, width_n))
-    prev_own = history(columns(conv_bc_state, me * cw, cw)).reshape(rows, cw)
+    x_state = conv_x_state.reshape(req, KW - 1, hp)
+    own_state = columns(conv_bc_state, me * cw, cw)
     meta = jnp.stack([span_start, accepted], axis=-1).astype(jnp.int32)
-    meta = jnp.broadcast_to(meta[:, None, :], (req, DRAFT, 2)).reshape(n, chunks, rc, 2)
-
-    def lanes(v):
-        return jnp.pad(v, (0, LANES - hd)).reshape(1, LANES)
-
-    tables = [
-        conv_x.reshape(KW, hp),
-        columns(conv_bc, group * width_n, width_n),
-        columns(conv_bc, (G + group) * width_n, width_n),
-        lanes(dt_bias),
-        lanes(decay_rate),
-        jnp.repeat(skip_gain, width_p).reshape(1, hp),
-        norm_gain.reshape(1, hp),
-    ]
+    meta = jnp.broadcast_to(meta[:, None, :], (req, DRAFT, 2)).reshape(rows, 2)
+    heads = jnp.pad(jnp.stack([dt_bias, decay_rate, skip_gain]), ((0, 5), (0, LANES - hd)))
+    group1 = group.astype(jnp.int32).reshape(1)
     state = ssm_state.reshape(n, chunks, rq, hp, width_n)
     scale_by = 1.0 / (HEADS // G * width_p)
 
@@ -526,17 +581,16 @@
         heads_of[0] = lead
         blocks += heads_of
 
-    prepared = [meta, prev_x, prev_b, prev_c, tables, prev_own, w_ext]
+    prepared = [meta, x_state, own_state, heads, w_ext]
     blocks[-1], prepared = lax.optimization_barrier((blocks[-1], prepared))
-    meta, prev_x, prev_b, prev_c, tables, prev_own, w_ext = prepared
-
-    theirs, ext_keep, ext_send = project(
-        seq, 1 - inc1, blocks[split:], w, w_ext, BF, [F32, BF], (theirs_1, ext_1)
-    )
-    ext = (ext_keep + other(ext_send).astype(F32)).astype(BF)
+    meta, x_state, own_state, heads, w_ext = prepared
+
+    ext = extra(seq, blocks[split:], w_ext, ext_1)
+    ext_other = other(ext)
+    (theirs,) = project(seq, 1 - inc1, blocks[split:], w, w_ext, BF, [], (theirs_1,))
+    theirs, ext, ext_other = lax.optimization_barrier((theirs, ext, ext_other))
+    ext = (ext + ext_other).astype(BF)
     bc_own = ext[:, :cw]
-    history_bc = new_history(rb, meta.reshape(rows, 2), bc_own, prev_own)
-    history_bc = history_bc.reshape(req, DRAFT, cw)[:, : KW - 1].reshape(1, req * (KW - 1), cw)
     dt = columns(ext[:, cw : cw + 2 * hd], inc * hd, hd)
     dt = jnp.pad(dt, ((0, 0), (0, LANES - hd)))
     got = []
@@ -557,9 +611,11 @@
     b_raw = jnp.concatenate(picked[: member // 2], axis=1)
     c_raw = jnp.concatenate(picked[member // 2 :], axis=1)
     theirs = other(theirs)
+    late, bc_own, dt = lax.optimization_barrier((blocks[-1], bc_own, dt))
+    blocks[-1] = late
     (mine,) = project(seq, inc1, blocks[split:], w, w_ext, F32, [], (mine_1,))
     gated, ssq, xw, bconv, sw, xraw = ssm(
-        0, rb, [meta, theirs, mine, dt, b_raw, c_raw, prev_x, prev_b, prev_c], tables, state
+        group1, rb, meta, theirs, mine, dt, b_raw, c_raw, x_state, conv_bc_state, conv_x, conv_bc, heads, norm_gain, state
     )
 
     def tails(a):
@@ -567,36 +623,56 @@
 
     gated_theirs = other(gated)
     ssq = ssq + other(ssq)
+    bc_own, gated, ssq = lax.optimization_barrier((bc_own, gated, ssq))
     d = 1
     while d < member:
         ssq = ssq + lax.ppermute(ssq, "outc", [(i, i ^ d) for i in range(n)])
         d *= 2
-    after, tail_x = new_state(0, rb, meta, xw, bconv, sw, xraw, prev_x, state, None)
-    gated_theirs, ssq, after = lax.optimization_barrier((gated_theirs, ssq, after))
+    history_bc = new_history(rb, meta, bc_own, own_state)
+    history_bc = history_bc.reshape(req, DRAFT, cw)[:, : KW - 1].reshape(req * (KW - 1), cw)
+    half_rows = req * (KW - 1) // 2
+    history_bc = lax.dynamic_slice_in_dim(history_bc, inc * half_rows, half_rows, 0)
+    widths = [n >> (i + 1) for i in range(n.bit_length() - 1)]
+
+    def double(a, i):
+        got = lax.ppermute(a, "outc", [(k, k ^ widths[i]) for k in range(n)])
+        return jnp.where((me & widths[i]) != 0, jnp.stack([got, a], i), jnp.stack([a, got], i))
+
+    history_bc = double(history_bc, 0)
+    gated_theirs, ssq, history_bc = lax.optimization_barrier((gated_theirs, ssq, history_bc))
+    history_bc = double(history_bc, 1)
 
     sums, partials = [], []
 
     def part(i, s):
-        return lax.dynamic_slice_in_dim(partials[i], seq[(s + 1) % n] * rc, rc, 0)
+        return lax.dynamic_slice_in_dim(partials[i], owner((s + 1) % n) * rc, rc, 0)
 
     for i in range(STREAMS):
         partials.append(out_project(inc1, gated, gated_theirs, w_out, ssq, scale_by, i, STREAMS))
-        sums.append(part(i, 0).astype(BF))
-    width = 1
+        if i == 0:
+            partials[0], history_bc = lax.optimization_barrier((partials[0], history_bc))
+            for k in range(2, len(widths)):
+                history_bc = double(history_bc, k)
+        sums.append(part(i, 0))
+    history_bc, sums[1] = lax.optimization_barrier((history_bc, sums[1]))
+    history_bc = history_bc.reshape(n, half_rows, cw)
+    history_other = other(history_bc)
+    history_bc = jnp.where(
+        inc != 0,
+        jnp.concatenate([history_other, history_bc], axis=1),
+        jnp.concatenate([history_bc, history_other], axis=1),
+    )
+    tails_x = []
+    after = None
     for s in range(n - 1):
-        if width < n:
-            history_bc, sums[0] = lax.optimization_barrier((history_bc, sums[0]))
-            got = lax.ppermute(history_bc, "outc", [(i, i ^ width) for i in range(n)])
-            history_bc = jnp.where(
-                (me & width) != 0,
-                jnp.concatenate([got, history_bc], axis=0),
-                jnp.concatenate([history_bc, got], axis=0),
-            )
-            width *= 2
+        if s in (1, 2):
+            after, tail = new_state(s - 1, 2, rb, meta, xw, bconv, sw, xraw, x_state, state, after)
+            tails_x.append(tail)
+            after, sums[0] = lax.optimization_barrier((after, sums[0]))
         for i in range(STREAMS):
-            sums[i] = (onward(sums[i]).astype(F32) + part(i, s + 1)).astype(BF)
+            sums[i] = (onward(sums[i]).astype(F32) + part(i, s + 1).astype(F32)).astype(BF)
     new_bc = jnp.swapaxes(history_bc, 0, 1).reshape(req, KW - 1, n * cw)
-    new_x = tails(tail_x).reshape(req, KW - 1, hd, width_p)
+    new_x = tails(jnp.concatenate(tails_x, axis=0)).reshape(req, KW - 1, hd, width_p)
     return jnp.concatenate(sums, axis=1), after.reshape(ssm_state.shape), new_x, new_bc
 
 

time: 194 us -> 187 us (0.964)
  other arithmetic: 15.7 us -> 7.54 us
  starting transfers between devices: 39.1 us -> 46.3 us
  local copies, waits for them, and re-layouts: 23.2 us -> 28.5 us
  waiting for transfers between devices: 40.1 us -> 34.9 us
  between operations: 6.37 us -> 1.74 us
    ppermute x3, waiting for transfers between devices: 13.3 us -> 1.38 us  [double(): got = lax.ppermute(a, 'outc', [(k, k ^ widths[i]) for k in range(n)])]
    convert_element_type x15, other arithmetic: 12.3 us -> 4.77 us  [the longest x14 3.51 us: shards(): (onward(sums[i]).astype(F32) + part(i, s + 1).astype(F32)).astype(BF)]
    ppermute x28, starting transfers between devices: 29.4 us -> 36.7 us  [onward(): return lax.ppermute(a, ('outc', 'inc'), ring)]
    unnamed x55 -> x127, local copies, waits for them, and re-layouts: 14.8 us -> 20.2 us
    pallas_call x4, Pallas kernels: 29.1 us -> 24.2 us  [project(): pl.pallas_call(functools.partial(project_kernel, parts, len(olds)), grid_...]
    ppermute x1, starting transfers between devices: 4.29 us -> 0.01 us  [shards(): ssq = ssq + lax.ppermute(ssq, 'outc', [(i, i ^ d) for i in range(n)])]
    ppermute x28, waiting for transfers between devices: 25.7 us -> 29.8 us  [onward(): return lax.ppermute(a, ('outc', 'inc'), ring)]
    ppermute x3, starting transfers between devices: 2.23 us -> 6.24 us  [double(): got = lax.ppermute(a, 'outc', [(k, k ^ widths[i]) for k in range(n)])]
  transfers between devices with their start and end apart: 38 -> 39, of which waited for: 17 -> 17; matrix products, arithmetic and copies ran while one was open for 12% -> 9% of each run, Pallas kernels for 24% -> 30%
where the time goes in v3:
time: 187 us; the launch traced here: 186 us
  Pallas kernels  67.4 us (36%)
  starting transfers between devices  46.3 us (25%)
  waiting for transfers between devices  34.9 us (19%)
  local copies, waits for them, and re-layouts  28.5 us (15%)
  other arithmetic  7.54 us (4%)
    ppermute x28, starting transfers between devices, onward(): return lax.ppermute(a, ('outc', 'inc'), ring)  36.7 us
    ppermute x28, waiting for transfers between devices, onward(): return lax.ppermute(a, ('outc', 'inc'), ring)  29.8 us
    pallas_call x4, Pallas kernels, project(): pl.pallas_call(functools.partial(project_kernel, parts, len(olds)), grid_...  24.2 us
    unnamed x127, local copies, waits for them, and re-layouts  20.2 us
    pallas_call x4, Pallas kernels, relayout(): pl.pallas_call(kernel, grid=(steps,), in_specs=specs, out_specs=pl.BlockS...  18.1 us
    pallas_call x1, Pallas kernels, ssm(): pl.pallas_call(ssm_kernel, grid_spec=pltpu.PrefetchScalarGridSpec(num_sca...  8.21 us
    pallas_call x2, Pallas kernels, out_project(): pl.pallas_call(functools.partial(out_kernel, scale_by), grid_spec=pltpu.P...  6.76 us
    pallas_call x2, Pallas kernels, new_state(): pl.pallas_call(kernel, grid=(steps,), in_specs=specs, out_specs=[states,...  6.52 us
  transfers between devices with their start and end apart: 39, of which 17 were waited for; matrix products, arithmetic and copies ran while one was open for 9% of the time, Pallas kernels for 30%

profile of v3, /device:TPU:0, one launch (start us, length us, event | category | flops | bytes accessed | tf_op | source)
XLA Modules:
  0.0 186.3 jit_solution(11809662114826831726)
XLA Ops:
  1.7 3.1 %collective-permute-start.7 = (bf16[32,4096]{1,0:T(8,128)(2,1)S(1)}, bf16[32,4096]{1,0:T(8,128)(2,1)S(1)}, u32[]{:S(2)}, u32[]{:S(2)}) collective-permute-start(bf16[32,4096]{1,0:T(8,128)(2,1)S(1)} %get-tuple-element.110.refs_0_), channel_id=1, source_target_pairs={{0,4},{4,8},{8,12},{12,14},{14,10},{10,6},{6,2},{2,0},{5,1},{9,5},... | collective-permute-start | bytes 786440 | tf_op jit(solution)/shard_map/ppermute | solution.py:538
  6.4 4.4 %relayout.4._ = bf16[2,4096,1024]{2,1,0:T(8,128)(2,1)} custom-call(bf16[4096,16,128]{2,1,0:T(8,128)(2,1)} %w_ref.7), custom_call_target="tpu_custom_call" | custom-call | flops 1073741824 | bytes 8388608 | tf_op jit(solution)/shard_map/relayout/pallas_call | solution.py:77
  14.0 4.4 %relayout.5._ = bf16[2,4096,1024]{2,1,0:T(8,128)(2,1)} custom-call(bf16[4096,16,128]{2,1,0:T(8,128)(2,1)} %w_ref.7, bf16[2,4096,1024]{2,1,0:T(8,128)(2,1)} %relayout.4._), custom_call_target="tpu_custom_call", output_to_operand_aliasing={{}: (1, {})} | custom-call | flops 1073741824 | bytes 8388608 | tf_op jit(solution)/shard_map/relayout/pallas_call | solution.py:77
  23.1 4.6 %relayout.6._ = bf16[2,4096,1024]{2,1,0:T(8,128)(2,1)} custom-call(bf16[4096,16,128]{2,1,0:T(8,128)(2,1)} %w_ref.7, bf16[2,4096,1024]{2,1,0:T(8,128)(2,1)} %relayout.5._), custom_call_target="tpu_custom_call", output_to_operand_aliasing={{}: (1, {})} | custom-call | flops 1073741824 | bytes 8388608 | tf_op jit(solution)/shard_map/relayout/pallas_call | solution.py:77
  32.3 4.6 %relayout.7.refs_8_ = bf16[2,4096,1024]{2,1,0:T(8,128)(2,1)} custom-call(bf16[4096,16,128]{2,1,0:T(8,128)(2,1)} %w_ref.7, bf16[2,4096,1024]{2,1,0:T(8,128)(2,1)} %relayout.6._), custom_call_target="tpu_custom_call", output_to_operand_aliasing={{}: (1, {})} | custom-call | flops 1073741824 | bytes 8388608 | tf_op jit(solution)/shard_map/relayout/pallas_call | solution.py:77
  39.7 6.2 %project.4 = (bf16[256,1024]{1,0:T(8,128)(2,1)S(1)}, f32[256,256]{1,0:T(8,128)S(1)}) custom-call(s32[8]{0:T(128)S(1)} %compare_select_fusion.2.seq_ref, s32[1]{0:T(128)S(6)} %sub.38.which_ref, bf16[32,4096]{1,0:T(8,128)(2,1)S(1)} %copy-done.17, bf16[32,4096]{1,0:T(8,128)(2,1)S(1)} %copy-done.19, bf16[32,4096]{1,0:T(8,128)(2,1)S(1)} %copy-done.29, ...), custom_call_target="tpu_custom_call" | custom-call | flops 2684354560 | bytes 10485760 | tf_op jit(solution)/shard_map/project/pallas_call | solution.py:138
  48.4 5.6 %project.5.refs_10_ = f32[256,1024]{1,0:T(8,128)S(1)} custom-call(s32[8]{0:T(128)S(1)} %compare_select_fusion.2.seq_ref, s32[1]{0:T(128)} %bitcast.7.which_ref.inc_ref, bf16[32,4096]{1,0:T(8,128)(2,1)S(1)} %copy-done.17, bf16[32,4096]{1,0:T(8,128)(2,1)S(1)} %copy-done.19, bf16[32,4096]{1,0:T(8,128)(2,1)S(1)} %copy-done.29, bf16[32,4096]{1,0:T(8,128)(2,1)S(1)} %copy-done.31, ...), custom_call_target="tpu_custom_call" | custom-call | flops 2684354560 | bytes 10485760 | tf_op jit(solution)/shard_map/project/pallas_call | solution.py:138
  59.6 4.9 %collective-permute-done.6.refs_7_ = bf16[32,4096]{1,0:T(8,128)(2,1)} collective-permute-done((bf16[32,4096]{1,0:T(8,128)(2,1)}, bf16[32,4096]{1,0:T(8,128)(2,1)}, u32[]{:S(2)}, u32[]{:S(2)}) %collective-permute-start.6) | collective-permute-done | bytes 262176 | tf_op jit(solution)/shard_map/ppermute | solution.py:538
  69.9 6.5 %project.6 = bf16[512,1024]{1,0:T(8,128)(2,1)} custom-call(s32[8]{0:T(128)S(1)} %compare_select_fusion.2.seq_ref, s32[1]{0:T(128)S(6)} %sub.38.which_ref, bf16[32,4096]{1,0:T(8,128)(2,1)S(1)} %collective-permute-done.10.refs_0_, bf16[32,4096]{1,0:T(8,128)(2,1)S(1)} %collective-permute-done.3.refs_1_, bf16[32,4096]{1,0:T(8,128)(2,1)S(1)} %copy-done.10, ...), custom_call_target="tpu_custom_call" | custom-call | flops 2684354560 | bytes 10485760 | tf_op jit(solution)/shard_map/project/pallas_call | solution.py:138
  84.8 5.9 %project.7.mine_ref = f32[512,1024]{1,0:T(8,128)S(1)} custom-call(s32[8]{0:T(128)S(1)} %compare_select_fusion.2.seq_ref, s32[1]{0:T(128)} %bitcast.7.which_ref.inc_ref, bf16[32,4096]{1,0:T(8,128)(2,1)S(1)} %collective-permute-done.10.refs_0_, bf16[32,4096]{1,0:T(8,128)(2,1)S(1)} %copy-done.7, bf16[32,4096]{1,0:T(8,128)(2,1)S(1)} %copy-done.11, ...), custom_call_target="tpu_custom_call" | custom-call | flops 2684354560 | bytes 10485760 | tf_op jit(solution)/shard_map/project/pallas_call | solution.py:138
  90.7 8.2 %ssm.1 = (bf16[512,512]{1,0:T(8,128)(2,1)S(1)}, f32[8,512]{1,0:T(8,128)S(1)}, bf16[512,512]{1,0:T(8,128)(2,1)S(1)}, bf16[512,128]{1,0:T(8,128)(2,1)S(1)}, f32[51...) custom-call(s32[1]{0:T(128)} %bitcast.6.group_ref, s32[512,2]{1,0:T(8,128)S(1)} %broadcast_bitcast_fusion.meta_ref.refs_0_, ...), custom_call_target="tpu_custom_call" | custom-call | flops 2147483648 | bytes 25165824 | tf_op jit(solution)/shard_map/ssm/pallas_call | solution.py:339
  100.2 3.4 %copy-done.1 = bf16[64,8,64,128]{3,2,1,0:T(8,128)(2,1)S(1)} copy-done((bf16[64,8,64,128]{3,2,1,0:T(8,128)(2,1)S(1)}, bf16[64,8,64,128]{3,2,1,0:T(8,128)(2,1)}, u32[]{:S(2)}) %copy-start.1) | copy-done | bytes 8388632
  103.6 3.2 %new_state.2 = (bf16[8,1,8,512,128]{4,3,2,1,0:T(8,128)(2,1)}, bf16[256,512]{1,0:T(8,128)(2,1)S(1)}) custom-call(s32[512,2]{1,0:T(8,128)S(1)} %broadcast_bitcast_fusion.meta_ref.refs_0_, bf16[512,512]{1,0:T(8,128)(2,1)S(1)} %get-tuple-element.80.xw_ref.refs_1_, bf16[512,128]{1,0:T(8,128)(2,1)S(1)} %get-tuple-element.81.bconv_ref.refs_2_, ...), custom_call_target="tpu_custom_call" | custom-call | flops 1073741824 | bytes 16777216 | tf_op jit(solution)/shard_map/new_state/pallas_call | solution.py:464
  108.2 5.2 %collective-permute-start.21 = (bf16[96,128]{1,0:T(8,128)(2,1)S(1)}, bf16[96,128]{1,0:T(8,128)(2,1)S(1)}, u32[]{:S(2)}, u32[]{:S(2)}) collective-permute-start(bf16[96,128]{1,0:T(8,128)(2,1)S(1)} %constant_dynamic-slice_fusion.2), channel_id=1, source_target_pairs={{0,8},{2,10},{4,12},{6,14},{8,0},{10,2},{12,4},{14,6},{1,9},{3,11}... | collective-permute-start | bytes 73736 | tf_op jit(solution)/shard_map/ppermute | solution.py:638
  113.5 3.7 %collective-permute-done.20 = f32[8,512]{1,0:T(8,128)S(1)} collective-permute-done((f32[8,512]{1,0:T(8,128)S(1)}, f32[8,512]{1,0:T(8,128)S(1)}, u32[]{:S(2)}, u32[]{:S(2)}) %collective-permute-start.20) | collective-permute-done | bytes 16416 | tf_op jit(solution)/shard_map/ppermute | solution.py:629
  117.3 3.4 %copy-done = bf16[1024,4096]{1,0:T(8,128)(2,1)S(1)} copy-done((bf16[1024,4096]{1,0:T(8,128)(2,1)S(1)}, bf16[1024,4096]{1,0:T(8,128)(2,1)}, u32[]{:S(2)}) %copy-start) | copy-done | bytes 8388632
  121.8 3.4 %out_project.3 = bf16[512,2048]{1,0:T(8,128)(2,1)S(1)} custom-call(s32[1]{0:T(128)} %bitcast.7.which_ref.inc_ref, bf16[512,512]{1,0:T(8,128)(2,1)S(1)} %copy-done.25, bf16[512,512]{1,0:T(8,128)(2,1)S(1)} %collective-permute-done.19.theirs_ref, bf16[1024,4096]{1,0:T(8,128)(2,1)S(1)} %copy-done, bf16[1024,4096]{1,0:T(8,128)(2,1)S(1)} %copy-done, ...), custom_call_target="tpu_custom_call" | custom-call | flops 2147483648 | bytes 8388608 | tf_op jit(solution)/shard_map/out_project/pallas_call | solution.py:491
  125.2 3.4 %out_project.2 = bf16[512,2048]{1,0:T(8,128)(2,1)S(1)} custom-call(s32[1]{0:T(128)} %bitcast.7.which_ref.inc_ref, bf16[512,512]{1,0:T(8,128)(2,1)S(1)} %copy-done.26, bf16[512,512]{1,0:T(8,128)(2,1)S(1)} %collective-permute-done.19.theirs_ref, bf16[1024,4096]{1,0:T(8,128)(2,1)S(1)} %copy-done, bf16[1024,4096]{1,0:T(8,128)(2,1)S(1)} %copy-done, ...), custom_call_target="tpu_custom_call" | custom-call | flops 2147483648 | bytes 8388608 | tf_op jit(solution)/shard_map/out_project/pallas_call | solution.py:491
  136.9 3.3 %new_state.3 = (bf16[8,1,8,512,128]{4,3,2,1,0:T(8,128)(2,1)}, bf16[256,512]{1,0:T(8,128)(2,1)S(1)}) custom-call(s32[512,2]{1,0:T(8,128)S(1)} %broadcast_bitcast_fusion.meta_ref.refs_0_, bf16[512,512]{1,0:T(8,128)(2,1)S(1)} %copy-done.21, bf16[512,128]{1,0:T(8,128)(2,1)S(1)} %get-tuple-element.81.bconv_ref.refs_2_, ...), custom_call_target="tpu_custom_call", output_to_operand_aliasing={{0}: (7, {})} | custom-call | flops 1073741824 | bytes 16777216 | tf_op jit(solution)/shard_map/new_state/pallas_call | solution.py:464
  150.3 2.6 %collective-permute-done.32 = bf16[64,2048]{1,0:T(8,128)(2,1)S(1)} collective-permute-done((bf16[64,2048]{1,0:T(8,128)(2,1)S(1)}, bf16[64,2048]{1,0:T(8,128)(2,1)S(1)}, u32[]{:S(2)}, u32[]{:S(2)}) %collective-permute-start.32) | collective-permute-done | bytes 262176 | tf_op jit(solution)/shard_map/ppermute | solution.py:538
  157.0 2.4 %collective-permute-done.33 = bf16[64,2048]{1,0:T(8,128)(2,1)S(1)} collective-permute-done((bf16[64,2048]{1,0:T(8,128)(2,1)S(1)}, bf16[64,2048]{1,0:T(8,128)(2,1)S(1)}, u32[]{:S(2)}, u32[]{:S(2)}) %collective-permute-start.33) | collective-permute-done | bytes 262176 | tf_op jit(solution)/shard_map/ppermute | solution.py:538
  163.4 2.4 %collective-permute-done.34 = bf16[64,2048]{1,0:T(8,128)(2,1)S(1)} collective-permute-done((bf16[64,2048]{1,0:T(8,128)(2,1)S(1)}, bf16[64,2048]{1,0:T(8,128)(2,1)S(1)}, u32[]{:S(2)}, u32[]{:S(2)}) %collective-permute-start.34) | collective-permute-done | bytes 262176 | tf_op jit(solution)/shard_map/ppermute | solution.py:538
  169.9 2.4 %collective-permute-done.35 = bf16[64,2048]{1,0:T(8,128)(2,1)S(1)} collective-permute-done((bf16[64,2048]{1,0:T(8,128)(2,1)S(1)}, bf16[64,2048]{1,0:T(8,128)(2,1)S(1)}, u32[]{:S(2)}, u32[]{:S(2)}) %collective-permute-start.35) | collective-permute-done | bytes 262176 | tf_op jit(solution)/shard_map/ppermute | solution.py:538
  181.8 3.6 %collective-permute-done.37 = bf16[64,2048]{1,0:T(8,128)(2,1)S(1)} collective-permute-done((bf16[64,2048]{1,0:T(8,128)(2,1)S(1)}, bf16[64,2048]{1,0:T(8,128)(2,1)S(1)}, u32[]{:S(2)}, u32[]{:S(2)}) %collective-permute-start.37) | collective-permute-done | bytes 262176 | tf_op jit(solution)/shard_map/ppermute | solution.py:538
  (249 shorter events, 83.5 us)
Async XLA Ops:
  1.7 9.1 %collective-permute-start.7 = (bf16[32,4096]{1,0:T(8,128)(2,1)S(1)}, bf16[32,4096]{1,0:T(8,128)(2,1)S(1)}, u32[]{:S(2)}, u32[]{:S(2)}) collective-permute-start(bf16[32,4096]{1,0:T(8,128)(2,1)S(1)} %get-tuple-element.110.refs_0_), channel_id=1, source_target_pairs={{0,4},{4,8},{8,12},{12,14},{14,10},{10,6},{6,2},{2,0},{5,1},{9,5},... | collective-permute-start | bytes 786440 | tf_op jit(solution)/shard_map/ppermute | solution.py:538
  4.8 7.7 %collective-permute-start = (bf16[32,4096]{1,0:T(8,128)(2,1)S(1)}, bf16[32,4096]{1,0:T(8,128)(2,1)S(1)}, u32[]{:S(2)}, u32[]{:S(2)}) collective-permute-start(bf16[32,4096]{1,0:T(8,128)(2,1)S(1)} %get-tuple-element.111.refs_1_), channel_id=1, source_target_pairs={{0,4},{4,8},{8,12},{12,14},{14,10},{10,6},{6,2},{2,0},{5,1},{9,5},... | collective-permute-start | bytes 786440 | tf_op jit(solution)/shard_map/ppermute | solution.py:538
  10.8 7.6 %collective-permute-start.8 = (bf16[32,4096]{1,0:T(8,128)(2,1)S(1)}, bf16[32,4096]{1,0:T(8,128)(2,1)S(1)}, u32[]{:S(2)}, u32[]{:S(2)}) collective-permute-start(bf16[32,4096]{1,0:T(8,128)(2,1)S(1)} %collective-permute-done.7.refs_2_), channel_id=1, source_target_pairs={{0,4},{4,8},{8,12},{12,14},{14,10},{10,6},{6,2},{2,0},{5,1},{9,5},... | collective-permute-start | bytes 786440 | tf_op jit(solution)/shard_map/ppermute | solution.py:538
  12.5 7.6 %collective-permute-start.1 = (bf16[32,4096]{1,0:T(8,128)(2,1)S(1)}, bf16[32,4096]{1,0:T(8,128)(2,1)S(1)}, u32[]{:S(2)}, u32[]{:S(2)}) collective-permute-start(bf16[32,4096]{1,0:T(8,128)(2,1)S(1)} %collective-permute-done.refs_3_), channel_id=1, source_target_pairs={{0,4},{4,8},{8,12},{12,14},{14,10},{10,6},{6,2},{2,0},{5,1},{9,5},... | collective-permute-start | bytes 786440 | tf_op jit(solution)/shard_map/ppermute | solution.py:538
  18.5 9.2 %collective-permute-start.9 = (bf16[32,4096]{1,0:T(8,128)(2,1)S(1)}, bf16[32,4096]{1,0:T(8,128)(2,1)}, u32[]{:S(2)}, u32[]{:S(2)}) collective-permute-start(bf16[32,4096]{1,0:T(8,128)(2,1)S(1)} %collective-permute-done.8.refs_4_), channel_id=1, source_target_pairs={{0,4},{4,8},{8,12},{12,14},{14,10},{10,6},{6,2},{2,0},{5,1},{9,5},... | collective-permute-start | bytes 786440 | tf_op jit(solution)/shard_map/ppermute | solution.py:538
  20.1 9.2 %collective-permute-start.2 = (bf16[32,4096]{1,0:T(8,128)(2,1)S(1)}, bf16[32,4096]{1,0:T(8,128)(2,1)}, u32[]{:S(2)}, u32[]{:S(2)}) collective-permute-start(bf16[32,4096]{1,0:T(8,128)(2,1)S(1)} %collective-permute-done.1.refs_5_), channel_id=1, source_target_pairs={{0,4},{4,8},{8,12},{12,14},{14,10},{10,6},{6,2},{2,0},{5,1},{9,5},... | collective-permute-start | bytes 786440 | tf_op jit(solution)/shard_map/ppermute | solution.py:538
  27.7 9.1 %collective-permute-start.10 = (bf16[32,4096]{1,0:T(8,128)(2,1)}, bf16[32,4096]{1,0:T(8,128)(2,1)S(1)}, u32[]{:S(2)}, u32[]{:S(2)}) collective-permute-start(bf16[32,4096]{1,0:T(8,128)(2,1)} %collective-permute-done.9.refs_6_), channel_id=1, source_target_pairs={{0,4},{4,8},{8,12},{12,14},{14,10},{10,6},{6,2},{2,0},{5,1},{9,5},... | collective-permute-start | bytes 786440 | tf_op jit(solution)/shard_map/ppermute | solution.py:538
  29.3 9.0 %collective-permute-start.3 = (bf16[32,4096]{1,0:T(8,128)(2,1)}, bf16[32,4096]{1,0:T(8,128)(2,1)S(1)}, u32[]{:S(2)}, u32[]{:S(2)}) collective-permute-start(bf16[32,4096]{1,0:T(8,128)(2,1)} %collective-permute-done.2.refs_7_), channel_id=1, source_target_pairs={{0,4},{4,8},{8,12},{12,14},{14,10},{10,6},{6,2},{2,0},{5,1},{9,5},... | collective-permute-start | bytes 786440 | tf_op jit(solution)/shard_map/ppermute | solution.py:538
  36.8 10.6 %collective-permute-start.11 = (bf16[32,4096]{1,0:T(8,128)(2,1)S(1)}, bf16[32,4096]{1,0:T(8,128)(2,1)S(1)}, u32[]{:S(2)}, u32[]{:S(2)}) collective-permute-start(bf16[32,4096]{1,0:T(8,128)(2,1)S(1)} %collective-permute-done.10.refs_0_), channel_id=1, source_target_pairs={{0,4},{4,8},{8,12},{12,14},{14,10},{10,6},{6,2},{2,0},{5,1},{9,5},... | collective-permute-start | bytes 786440 | tf_op jit(solution)/shard_map/ppermute | solution.py:538
  38.2 9.6 %collective-permute-start.4 = (bf16[32,4096]{1,0:T(8,128)(2,1)S(1)}, bf16[32,4096]{1,0:T(8,128)(2,1)S(1)}, u32[]{:S(2)}, u32[]{:S(2)}) collective-permute-start(bf16[32,4096]{1,0:T(8,128)(2,1)S(1)} %collective-permute-done.3.refs_1_), channel_id=1, source_target_pairs={{0,4},{4,8},{8,12},{12,14},{14,10},{10,6},{6,2},{2,0},{5,1},{9,5},... | collective-permute-start | bytes 786440 | tf_op jit(solution)/shard_map/ppermute | solution.py:538
  47.4 7.6 %collective-permute-start.12 = (bf16[32,4096]{1,0:T(8,128)(2,1)S(1)}, bf16[32,4096]{1,0:T(8,128)(2,1)}, u32[]{:S(2)}, u32[]{:S(2)}) collective-permute-start(bf16[32,4096]{1,0:T(8,128)(2,1)S(1)} %collective-permute-done.11.refs_2_), channel_id=1, source_target_pairs={{0,4},{4,8},{8,12},{12,14},{14,10},{10,6},{6,2},{2,0},{5,1},{9,5},... | collective-permute-start | bytes 786440 | tf_op jit(solution)/shard_map/ppermute | solution.py:538
  47.9 8.8 %collective-permute-start.5 = (bf16[32,4096]{1,0:T(8,128)(2,1)S(1)}, bf16[32,4096]{1,0:T(8,128)(2,1)}, u32[]{:S(2)}, u32[]{:S(2)}) collective-permute-start(bf16[32,4096]{1,0:T(8,128)(2,1)S(1)} %collective-permute-done.4.refs_3_), channel_id=1, source_target_pairs={{0,4},{4,8},{8,12},{12,14},{14,10},{10,6},{6,2},{2,0},{5,1},{9,5},... | collective-permute-start | bytes 786440 | tf_op jit(solution)/shard_map/ppermute | solution.py:538
  55.0 9.5 %collective-permute-start.13 = (bf16[32,4096]{1,0:T(8,128)(2,1)}, bf16[32,4096]{1,0:T(8,128)(2,1)}, u32[]{:S(2)}, u32[]{:S(2)}) collective-permute-start(bf16[32,4096]{1,0:T(8,128)(2,1)} %collective-permute-done.12.refs_4_), channel_id=1, source_target_pairs={{0,4},{4,8},{8,12},{12,14},{14,10},{10,6},{6,2},{2,0},{5,1},{9,5},... | collective-permute-start | bytes 786440 | tf_op jit(solution)/shard_map/ppermute | solution.py:538
  56.7 7.8 %collective-permute-start.6 = (bf16[32,4096]{1,0:T(8,128)(2,1)}, bf16[32,4096]{1,0:T(8,128)(2,1)}, u32[]{:S(2)}, u32[]{:S(2)}) collective-permute-start(bf16[32,4096]{1,0:T(8,128)(2,1)} %collective-permute-done.5.refs_5_), channel_id=1, source_target_pairs={{0,4},{4,8},{8,12},{12,14},{14,10},{10,6},{6,2},{2,0},{5,1},{9,5},... | collective-permute-start | bytes 786440 | tf_op jit(solution)/shard_map/ppermute | solution.py:538
  77.2 13.5 %collective-permute-start.15 = (bf16[512,1024]{1,0:T(8,128)(2,1)}, bf16[512,1024]{1,0:T(8,128)(2,1)}, u32[]{:S(2)}, u32[]{:S(2)}) collective-permute-start(bf16[512,1024]{1,0:T(8,128)(2,1)} %project.6), channel_id=1, source_target_pairs={{0,1},{1,0},{2,3},{3,2},{4,5},{5,4},{6,7},{7,6},{8,9},{9,8},{10,11... | collective-permute-start | bytes 3145736 | tf_op jit(solution)/shard_map/ppermute | solution.py:541
  80.2 10.4 %collective-permute-start.16 = (bf16[512,128]{1,0:T(8,128)(2,1)S(1)}, bf16[512,128]{1,0:T(8,128)(2,1)S(1)}, u32[]{:S(2)}, u32[]{:S(2)}) collective-permute-start(bf16[512,128]{1,0:T(8,128)(2,1)S(1)} %slice.24.raw_ref), channel_id=1, source_target_pairs={{8,0},{0,2},{10,4},{2,6},{12,8},{4,10},{14,12},{6,14},{9,1},{1,3},... | collective-permute-start | bytes 393224 | tf_op jit(solution)/shard_map/ppermute | solution.py:604
  81.8 8.9 %collective-permute-start.17 = (bf16[512,128]{1,0:T(8,128)(2,1)S(1)}, bf16[512,128]{1,0:T(8,128)(2,1)S(1)}, u32[]{:S(2)}, u32[]{:S(2)}) collective-permute-start(bf16[512,128]{1,0:T(8,128)(2,1)S(1)} %slice.24.raw_ref), channel_id=1, source_target_pairs={{0,0},{8,2},{2,4},{10,6},{4,8},{12,10},{6,12},{14,14},{1,1},{9,3},... | collective-permute-start | bytes 393224 | tf_op jit(solution)/shard_map/ppermute | solution.py:604
  99.6 17.7 %collective-permute-start.19 = (bf16[512,512]{1,0:T(8,128)(2,1)S(1)}, bf16[512,512]{1,0:T(8,128)(2,1)S(1)}, u32[]{:S(2)}, u32[]{:S(2)}) collective-permute-start(bf16[512,512]{1,0:T(8,128)(2,1)S(1)} %get-tuple-element.88.mine_ref), channel_id=1, source_target_pairs={{0,1},{1,0},{2,3},{3,2},{4,5},{5,4},{6,7},{7,6},{8,9},{9,8},{10,11... | collective-permute-start | bytes 1572872 | tf_op jit(solution)/shard_map/ppermute | solution.py:541
  99.9 7.0 %collective-permute-start.18 = (f32[8,512]{1,0:T(8,128)}, f32[8,512]{1,0:T(8,128)S(1)}, u32[]{:S(2)}, u32[]{:S(2)}) collective-permute-start(f32[8,512]{1,0:T(8,128)} %copy-done.47), channel_id=1, source_target_pairs={{0,1},{1,0},{2,3},{3,2},{4,5},{5,4},{6,7},{7,6},{8,9},{9,8},{10,11... | collective-permute-start | bytes 49160 | tf_op jit(solution)/shard_map/ppermute | solution.py:541
  108.2 9.0 %collective-permute-start.21 = (bf16[96,128]{1,0:T(8,128)(2,1)S(1)}, bf16[96,128]{1,0:T(8,128)(2,1)S(1)}, u32[]{:S(2)}, u32[]{:S(2)}) collective-permute-start(bf16[96,128]{1,0:T(8,128)(2,1)S(1)} %constant_dynamic-slice_fusion.2), channel_id=1, source_target_pairs={{0,8},{2,10},{4,12},{6,14},{8,0},{10,2},{12,4},{14,6},{1,9},{3,11}... | collective-permute-start | bytes 73736 | tf_op jit(solution)/shard_map/ppermute | solution.py:638
  117.3 11.4 %collective-permute-start.22 = (bf16[2,96,128]{2,1,0:T(8,128)(2,1)S(1)}, bf16[2,96,128]{2,1,0:T(8,128)(2,1)S(1)}, u32[]{:S(2)}, u32[]{:S(2)}) collective-permute-start(bf16[2,96,128]{2,1,0:T(8,128)(2,1)S(1)} %maximum_select_fusion.3), channel_id=1, source_target_pairs={{0,4},{2,6},{4,0},{6,2},{8,12},{10,14},{12,8},{14,10},{1,5},{3,7},... | collective-permute-start | bytes 147464 | tf_op jit(solution)/shard_map/ppermute | solution.py:638
  134.0 8.8 %collective-permute-start.38 = (bf16[8,96,128]{2,1,0:T(8,128)(2,1)}, bf16[8,96,128]{2,1,0:T(8,128)(2,1)}, u32[]{:S(2)}, u32[]{:S(2)}) collective-permute-start(bf16[8,96,128]{2,1,0:T(8,128)(2,1)} %bitcast.18), channel_id=1, source_target_pairs={{0,1},{1,0},{2,3},{3,2},{4,5},{5,4},{6,7},{7,6},{8,9},{9,8},{10,11... | collective-permute-start | bytes 589832 | tf_op jit(solution)/shard_map/ppermute | solution.py:541
  134.0 11.4 %collective-permute-start.31 = (bf16[64,2048]{1,0:T(8,128)(2,1)}, bf16[64,2048]{1,0:T(8,128)(2,1)}, u32[]{:S(2)}, u32[]{:S(2)}) collective-permute-start(bf16[64,2048]{1,0:T(8,128)(2,1)} %constant_dynamic-slice_fusion), channel_id=1, source_target_pairs={{0,4},{4,8},{8,12},{12,14},{14,10},{10,6},{6,2},{2,0},{5,1},{9,5},... | collective-permute-start | bytes 786440 | tf_op jit(solution)/shard_map/ppermute | solution.py:538
  148.7 7.0 %collective-permute-start.25 = (bf16[64,2048]{1,0:T(8,128)(2,1)S(1)}, bf16[64,2048]{1,0:T(8,128)(2,1)S(1)}, u32[]{:S(2)}, u32[]{:S(2)}) collective-permute-start(bf16[64,2048]{1,0:T(8,128)(2,1)S(1)} %add_convert_fusion.12), channel_id=1, source_target_pairs={{0,4},{4,8},{8,12},{12,14},{14,10},{10,6},{6,2},{2,0},{5,1},{9,5},... | collective-permute-start | bytes 786440 | tf_op jit(solution)/shard_map/ppermute | solution.py:538
  (77 other events, 493.2 us)

commit v4 on v3

--- a/solution.py
+++ b/solution.py
@@ -145,8 +145,8 @@
             + [whole_block((out_m, ext_cols)) for _ in ext_dtypes],
             scratch_shapes=[pltpu.VMEM((m, k), BF)],
         ),
-        out_shape=[jax.ShapeDtypeStruct((out_m, cols), dtype)]
-        + [jax.ShapeDtypeStruct((out_m, ext_cols), d) for d in ext_dtypes],
+        out_shape=[pltpu.HBM((out_m, cols), dtype)]
+        + [pltpu.HBM((out_m, ext_cols), d) for d in ext_dtypes],
         compiler_params=params(46),
         cost_estimate=cost(2 * m * k * (cols + ext_cols), 2 * k * cols + 2 * m * k),
         name="project",
@@ -195,7 +195,8 @@
 
 def history_rows(state):
     state = state.astype(F32)
-    return jnp.concatenate([jnp.zeros((state.shape[0], DRAFT - KW + 1, state.shape[2]), F32), state], axis=1)
+    empty = jnp.zeros((state.shape[1], DRAFT - KW + 1, state.shape[2]), F32)
+    return jnp.concatenate([empty, *[state[j][:, None, :] for j in range(KW - 1)]], axis=1)
 
 
 def ssm_kernel(
@@ -333,7 +334,7 @@
     def columns(shape, which):
         lead = (0,) * (len(shape) - 1)
         if len(shape) == 3:
-            return pl.BlockSpec(shape, lambda i, group: (i, 0, which * G + group[0]))
+            return pl.BlockSpec(shape, lambda i, group: (0, i, which * G + group[0]))
         return pl.BlockSpec(shape, lambda i, group: (*lead, which * G + group[0]))
 
     return pl.pallas_call(
@@ -348,9 +349,9 @@
                 flat(LANES),
                 flat(LANES),
                 flat(LANES),
-                pl.BlockSpec((reqs, KW - 1, hp), lambda i, group: (i, 0, 0)),
-                columns((reqs, KW - 1, LANES), 0),
-                columns((reqs, KW - 1, LANES), 1),
+                pl.BlockSpec((KW - 1, reqs, hp), lambda i, group: (0, i, 0)),
+                columns((KW - 1, reqs, LANES), 0),
+                columns((KW - 1, reqs, LANES), 1),
                 whole_block(conv_x.shape),
                 columns((KW, LANES), 0),
                 columns((KW, LANES), 1),
@@ -370,10 +371,10 @@
         out_shape=[
             jax.ShapeDtypeStruct((rows, hp), BF),
             jax.ShapeDtypeStruct((8, rows), F32),
-            jax.ShapeDtypeStruct((rows, hp), BF),
-            jax.ShapeDtypeStruct((rows, LANES), BF),
-            jax.ShapeDtypeStruct((rows, LANES), F32),
-            jax.ShapeDtypeStruct((rows, hp), BF),
+            pltpu.HBM((rows, hp), BF),
+            pltpu.HBM((rows, LANES), BF),
+            pltpu.HBM((rows, LANES), F32),
+            pltpu.HBM((rows, hp), BF),
         ],
         compiler_params=params(46),
         cost_estimate=cost(2 * rows * hp * 4096, 6 * rows * hp * 16),
@@ -422,7 +423,7 @@
     return pl.pallas_call(
         tail_kernel,
         grid=(rows // rb,),
-        in_specs=[flat(2), flat(cols), pl.BlockSpec((rb // DRAFT, KW - 1, cols), lambda i: (i, 0, 0))],
+        in_specs=[flat(2), flat(cols), pl.BlockSpec((KW - 1, rb // DRAFT, cols), lambda i: (0, i, 0))],
         out_specs=flat(cols),
         out_shape=jax.ShapeDtypeStruct((rows, cols), BF),
         compiler_params=params(24),
@@ -449,7 +450,7 @@
         flat(LANES),
         flat(LANES),
         flat(hp),
-        pl.BlockSpec((rb // DRAFT, KW - 1, hp), lambda i: (first + i, 0, 0)),
+        pl.BlockSpec((KW - 1, rb // DRAFT, hp), lambda i: (0, first + i, 0)),
         states,
     ]
     kernel, aliases = state_kernel, {}
@@ -550,8 +551,9 @@
     def columns(a, start, size):
         return lax.dynamic_slice_in_dim(a, start, size, a.ndim - 1)
 
-    x_state = conv_x_state.reshape(req, KW - 1, hp)
-    own_state = columns(conv_bc_state, me * cw, cw)
+    x_state = jnp.swapaxes(conv_x_state.reshape(req, KW - 1, hp), 0, 1)
+    bc_state = jnp.swapaxes(conv_bc_state, 0, 1)
+    own_state = columns(bc_state, me * cw, cw)
     meta = jnp.stack([span_start, accepted], axis=-1).astype(jnp.int32)
     meta = jnp.broadcast_to(meta[:, None, :], (req, DRAFT, 2)).reshape(rows, 2)
     heads = jnp.pad(jnp.stack([dt_bias, decay_rate, skip_gain]), ((0, 5), (0, LANES - hd)))
@@ -615,7 +617,7 @@
     blocks[-1] = late
     (mine,) = project(seq, inc1, blocks[split:], w, w_ext, F32, [], (mine_1,))
     gated, ssq, xw, bconv, sw, xraw = ssm(
-        group1, rb, meta, theirs, mine, dt, b_raw, c_raw, x_state, conv_bc_state, conv_x, conv_bc, heads, norm_gain, state
+        group1, rb, meta, theirs, mine, dt, b_raw, c_raw, x_state, bc_state, conv_x, conv_bc, heads, norm_gain, state
     )
 
     def tails(a):
@@ -654,21 +656,28 @@
             for k in range(2, len(widths)):
                 history_bc = double(history_bc, k)
         sums.append(part(i, 0))
-    history_bc, sums[1] = lax.optimization_barrier((history_bc, sums[1]))
-    history_bc = history_bc.reshape(n, half_rows, cw)
-    history_other = other(history_bc)
-    history_bc = jnp.where(
-        inc != 0,
-        jnp.concatenate([history_other, history_bc], axis=1),
-        jnp.concatenate([history_bc, history_other], axis=1),
-    )
     tails_x = []
     after = None
     for s in range(n - 1):
-        if s in (1, 2):
-            after, tail = new_state(s - 1, 2, rb, meta, xw, bconv, sw, xraw, x_state, state, after)
+        if s in (0, 2):
+            xw, sums[0] = lax.optimization_barrier((xw, sums[0]))
+            piece = len(tails_x)
+            after, tail = new_state(piece, 2, rb, meta, xw, bconv, sw, xraw, x_state, state, after)
             tails_x.append(tail)
             after, sums[0] = lax.optimization_barrier((after, sums[0]))
+        if s == 3:
+            history_bc, sums[0] = lax.optimization_barrier((history_bc, sums[0]))
+            history_bc = history_bc.reshape(n, half_rows, cw)
+            history_other = other(history_bc)
+        if s == 4:
+            history_other, sums[0] = lax.optimization_barrier((history_other, sums[0]))
+            history_bc = jnp.where(
+                inc != 0,
+                jnp.concatenate([history_other, history_bc], axis=1),
+                jnp.concatenate([history_bc, history_other], axis=1),
+            )
+        if s == 5:
+            history_bc, tails_x, sums[1] = lax.optimization_barrier((history_bc, tails_x, sums[1]))
         for i in range(STREAMS):
             sums[i] = (onward(sums[i]).astype(F32) + part(i, s + 1).astype(F32)).astype(BF)
     new_bc = jnp.swapaxes(history_bc, 0, 1).reshape(req, KW - 1, n * cw)

time: 187 us -> 177 us (0.947)
  local copies, waits for them, and re-layouts: 28.5 us -> 14.9 us
  waiting for transfers between devices: 34.9 us -> 41.3 us
  starting transfers between devices: 46.3 us -> 40.5 us
  Pallas kernels: 67.4 us -> 70.3 us
    unnamed x127 -> x102, local copies, waits for them, and re-layouts: 20.2 us -> 8.42 us
    ppermute x28, starting transfers between devices: 36.7 us -> 31.3 us  [onward(): return lax.ppermute(a, ('outc', 'inc'), ring)]
    ppermute x28, waiting for transfers between devices: 29.8 us -> 34.9 us  [onward(): return lax.ppermute(a, ('outc', 'inc'), ring)]
    pallas_call x4, Pallas kernels: 24.2 us -> 26.1 us  [project(): pl.pallas_call(functools.partial(project_kernel, parts, len(olds)), grid_...]
    optimization_barrier x2 -> x1, local copies, waits for them, and re-layouts: 1.89 us -> 0.01 us  [shards(): history_bc, sums[0] = lax.optimization_barrier((history_bc, sums[0]))]
  transfers between devices with their start and end apart: 39 -> 39, of which waited for: 17 -> 17; matrix products, arithmetic and copies ran while one was open for 9% -> 8% of each run, Pallas kernels for 30% -> 33%
where the time goes in v4:
time: 177 us
  Pallas kernels  70.3 us (40%)
  waiting for transfers between devices  41.3 us (23%)
  starting transfers between devices  40.5 us (23%)
  local copies, waits for them, and re-layouts  14.9 us (8%)
  other arithmetic  8.13 us (5%)
    ppermute x28, waiting for transfers between devices, onward(): return lax.ppermute(a, ('outc', 'inc'), ring)  34.9 us
    ppermute x28, starting transfers between devices, onward(): return lax.ppermute(a, ('outc', 'inc'), ring)  31.3 us
    pallas_call x4, Pallas kernels, project(): pl.pallas_call(functools.partial(project_kernel, parts, len(olds)), grid_...  26.1 us
    pallas_call x4, Pallas kernels, relayout(): pl.pallas_call(kernel, grid=(steps,), in_specs=specs, out_specs=pl.BlockS...  18.1 us
    pallas_call x1, Pallas kernels, ssm(): pl.pallas_call(ssm_kernel, grid_spec=pltpu.PrefetchScalarGridSpec(num_sca...  9.07 us
    unnamed x102, local copies, waits for them, and re-layouts  8.42 us
    pallas_call x2, Pallas kernels, out_project(): pl.pallas_call(functools.partial(out_kernel, scale_by), grid_spec=pltpu.P...  6.77 us
    pallas_call x2, Pallas kernels, new_state(): pl.pallas_call(kernel, grid=(steps,), in_specs=specs, out_specs=[states,...  6.58 us
  transfers between devices with their start and end apart: 39, of which 17 were waited for; matrix products, arithmetic and copies ran while one was open for 8% of the time, Pallas kernels for 33%

profile of v4, /device:TPU:0, one launch (start us, length us, event | category | flops | bytes accessed | tf_op | source)
XLA Modules:
  0.0 176.6 jit_solution(18191661722467216945)
XLA Ops:
  1.7 3.1 %collective-permute-start.7 = (bf16[32,4096]{1,0:T(8,128)(2,1)S(1)}, bf16[32,4096]{1,0:T(8,128)(2,1)S(1)}, u32[]{:S(2)}, u32[]{:S(2)}) collective-permute-start(bf16[32,4096]{1,0:T(8,128)(2,1)S(1)} %get-tuple-element.130.refs_0_), channel_id=1, source_target_pairs={{0,4},{4,8},{8,12},{12,14},{14,10},{10,6},{6,2},{2,0},{5,1},{9,5},... | collective-permute-start | bytes 786440 | tf_op jit(solution)/shard_map/ppermute | solution.py:539
  6.4 4.5 %relayout.4._ = bf16[2,4096,1024]{2,1,0:T(8,128)(2,1)} custom-call(bf16[4096,16,128]{2,1,0:T(8,128)(2,1)} %w_ref.7), custom_call_target="tpu_custom_call" | custom-call | flops 1073741824 | bytes 8388608 | tf_op jit(solution)/shard_map/relayout/pallas_call | solution.py:77
  14.0 4.5 %relayout.5._ = bf16[2,4096,1024]{2,1,0:T(8,128)(2,1)} custom-call(bf16[4096,16,128]{2,1,0:T(8,128)(2,1)} %w_ref.7, bf16[2,4096,1024]{2,1,0:T(8,128)(2,1)} %relayout.4._), custom_call_target="tpu_custom_call", output_to_operand_aliasing={{}: (1, {})} | custom-call | flops 1073741824 | bytes 8388608 | tf_op jit(solution)/shard_map/relayout/pallas_call | solution.py:77
  23.1 4.6 %relayout.6._ = bf16[2,4096,1024]{2,1,0:T(8,128)(2,1)} custom-call(bf16[4096,16,128]{2,1,0:T(8,128)(2,1)} %w_ref.7, bf16[2,4096,1024]{2,1,0:T(8,128)(2,1)} %relayout.5._), custom_call_target="tpu_custom_call", output_to_operand_aliasing={{}: (1, {})} | custom-call | flops 1073741824 | bytes 8388608 | tf_op jit(solution)/shard_map/relayout/pallas_call | solution.py:77
  31.7 4.6 %relayout.7.refs_8_ = bf16[2,4096,1024]{2,1,0:T(8,128)(2,1)} custom-call(bf16[4096,16,128]{2,1,0:T(8,128)(2,1)} %w_ref.7, bf16[2,4096,1024]{2,1,0:T(8,128)(2,1)} %relayout.6._), custom_call_target="tpu_custom_call", output_to_operand_aliasing={{}: (1, {})} | custom-call | flops 1073741824 | bytes 8388608 | tf_op jit(solution)/shard_map/relayout/pallas_call | solution.py:77
  39.1 6.8 %project.4 = (bf16[256,1024]{1,0:T(8,128)(2,1)}, f32[256,256]{1,0:T(8,128)}) custom-call(s32[8]{0:T(128)S(1)} %compare_select_fusion.2.seq_ref, s32[1]{0:T(128)S(6)} %sub.38.which_ref, bf16[32,4096]{1,0:T(8,128)(2,1)S(1)} %get-tuple-element.130.refs_0_, bf16[32,4096]{1,0:T(8,128)(2,1)S(1)} %copy-done.15, bf16[32,4096]{1,0:T(8,128)(2,1)S(1)} %copy-done.21, ...), custom_call_target="tpu_custom_call" | custom-call | flops 2684354560 | bytes 10485760 | tf_op jit(solution)/shard_map/project/pallas_call | solution.py:138
  47.2 6.2 %project.5.refs_10_ = f32[256,1024]{1,0:T(8,128)} custom-call(s32[8]{0:T(128)S(1)} %compare_select_fusion.2.seq_ref, s32[1]{0:T(128)} %bitcast.which_ref.inc_ref, bf16[32,4096]{1,0:T(8,128)(2,1)S(1)} %get-tuple-element.130.refs_0_, bf16[32,4096]{1,0:T(8,128)(2,1)S(1)} %copy-done.15, bf16[32,4096]{1,0:T(8,128)(2,1)S(1)} %copy-done.21, ...), custom_call_target="tpu_custom_call" | custom-call | flops 2684354560 | bytes 10485760 | tf_op jit(solution)/shard_map/project/pallas_call | solution.py:138
  57.8 5.1 %collective-permute-done.6.refs_7_ = bf16[32,4096]{1,0:T(8,128)(2,1)} collective-permute-done((bf16[32,4096]{1,0:T(8,128)(2,1)}, bf16[32,4096]{1,0:T(8,128)(2,1)}, u32[]{:S(2)}, u32[]{:S(2)}) %collective-permute-start.6) | collective-permute-done | bytes 262176 | tf_op jit(solution)/shard_map/ppermute | solution.py:539
  66.5 6.5 %project.6 = bf16[512,1024]{1,0:T(8,128)(2,1)} custom-call(s32[8]{0:T(128)S(1)} %compare_select_fusion.2.seq_ref, s32[1]{0:T(128)S(6)} %sub.38.which_ref, bf16[32,4096]{1,0:T(8,128)(2,1)S(1)} %collective-permute-done.10.refs_0_, bf16[32,4096]{1,0:T(8,128)(2,1)S(1)} %collective-permute-done.3.refs_1_, bf16[32,4096]{1,0:T(8,128)(2,1)S(1)} %collective-permute-done.11.refs_2_, ...), custom_call_target="tpu_custom_call" | custom-call | flops 2684354560 | bytes 10485760 | tf_op jit(solution)/shard_map/project/pallas_call | solution.py:138
  77.3 6.7 %project.7.mine_ref = f32[512,1024]{1,0:T(8,128)} custom-call(s32[8]{0:T(128)S(1)} %compare_select_fusion.2.seq_ref, s32[1]{0:T(128)} %bitcast.which_ref.inc_ref, bf16[32,4096]{1,0:T(8,128)(2,1)S(1)} %copy-done.7, bf16[32,4096]{1,0:T(8,128)(2,1)S(1)} %copy-done.9, bf16[32,4096]{1,0:T(8,128)(2,1)S(1)} %copy-done.11, bf16[32,4096]{1,0:T(8,128)(2,1)S(1)} %copy-done.13, ...), custom_call_target="tpu_custom_call" | custom-call | flops 2684354560 | bytes 10485760 | tf_op jit(solution)/shard_map/project/pallas_call | solution.py:138
  85.7 9.1 %ssm.1 = (bf16[512,512]{1,0:T(8,128)(2,1)S(1)}, f32[8,512]{1,0:T(8,128)S(1)}, bf16[512,512]{1,0:T(8,128)(2,1)}, bf16[512,128]{1,0:T(8,128)(2,1)}, f32[512,128]{1,0:T(8,128)}, /*index=5*/bf16[512,512]{1,0:T(8,128)(2,1)}) custom-call(s32[1]{0:T(128)} %bitcast.9.group_ref, s32[512,2]{1,0:T(8,128)S(1)} %broadcast_bitcast_fusion.meta_ref.refs_0_, ...), custom_call_target="tpu_custom_call" | custom-call | flops 2147483648 | bytes 25165824 | tf_op jit(solution)/shard_map/ssm/pallas_call | solution.py:340
  98.1 5.2 %collective-permute-start.21 = (bf16[96,128]{1,0:T(8,128)(2,1)S(1)}, bf16[96,128]{1,0:T(8,128)(2,1)S(1)}, u32[]{:S(2)}, u32[]{:S(2)}) collective-permute-start(bf16[96,128]{1,0:T(8,128)(2,1)S(1)} %constant_dynamic-slice_fusion.2), channel_id=1, source_target_pairs={{0,8},{2,10},{4,12},{6,14},{8,0},{10,2},{12,4},{14,6},{1,9},{3,11}... | collective-permute-start | bytes 73736 | tf_op jit(solution)/shard_map/ppermute | solution.py:640
  103.3 3.7 %collective-permute-done.20 = f32[8,512]{1,0:T(8,128)S(1)} collective-permute-done((f32[8,512]{1,0:T(8,128)S(1)}, f32[8,512]{1,0:T(8,128)S(1)}, u32[]{:S(2)}, u32[]{:S(2)}) %collective-permute-start.20) | collective-permute-done | bytes 16416 | tf_op jit(solution)/shard_map/ppermute | solution.py:631
  107.5 3.4 %copy-done = bf16[1024,4096]{1,0:T(8,128)(2,1)S(1)} copy-done((bf16[1024,4096]{1,0:T(8,128)(2,1)S(1)}, bf16[1024,4096]{1,0:T(8,128)(2,1)}, u32[]{:S(2)}) %copy-start) | copy-done | bytes 8388632
  110.8 3.4 %out_project.3 = bf16[512,2048]{1,0:T(8,128)(2,1)S(1)} custom-call(s32[1]{0:T(128)} %bitcast.which_ref.inc_ref, bf16[512,512]{1,0:T(8,128)(2,1)S(1)} %get-tuple-element.93.mine_ref, bf16[512,512]{1,0:T(8,128)(2,1)S(1)} %collective-permute-done.19.theirs_ref, bf16[1024,4096]{1,0:T(8,128)(2,1)S(1)} %copy-done, bf16[1024,4096]{1,0:T(8,128)(2,1)S(1)} %copy-done, ...), custom_call_target="tpu_custom_call" | custom-call | flops 2147483648 | bytes 8388608 | tf_op jit(solution)/shard_map/out_project/pallas_call | solution.py:492
  114.3 3.4 %out_project.2 = bf16[512,2048]{1,0:T(8,128)(2,1)S(1)} custom-call(s32[1]{0:T(128)} %bitcast.which_ref.inc_ref, bf16[512,512]{1,0:T(8,128)(2,1)S(1)} %get-tuple-element.93.mine_ref, bf16[512,512]{1,0:T(8,128)(2,1)S(1)} %collective-permute-done.19.theirs_ref, bf16[1024,4096]{1,0:T(8,128)(2,1)S(1)} %copy-done, bf16[1024,4096]{1,0:T(8,128)(2,1)S(1)} %copy-done, ...), custom_call_target="tpu_custom_call" | custom-call | flops 2147483648 | bytes 8388608 | tf_op jit(solution)/shard_map/out_project/pallas_call | solution.py:492
  120.0 3.3 %new_state.2 = (bf16[8,1,8,512,128]{4,3,2,1,0:T(8,128)(2,1)}, bf16[256,512]{1,0:T(8,128)(2,1)S(1)}) custom-call(s32[512,2]{1,0:T(8,128)S(1)} %broadcast_bitcast_fusion.meta_ref.refs_0_, bf16[512,512]{1,0:T(8,128)(2,1)S(1)} %copy-done.16, bf16[512,128]{1,0:T(8,128)(2,1)S(1)} %copy-done.33, f32[512,128]{1,0:T(8,128)S(1)} %copy-done.32, ...), custom_call_target="tpu_custom_call" | custom-call | flops 1073741824 | bytes 16777216 | tf_op jit(solution)/shard_map/new_state/pallas_call | solution.py:465
  126.1 3.6 %collective-permute-done.24 = bf16[64,2048]{1,0:T(8,128)(2,1)S(1)} collective-permute-done((bf16[64,2048]{1,0:T(8,128)(2,1)S(1)}, bf16[64,2048]{1,0:T(8,128)(2,1)S(1)}, u32[]{:S(2)}, u32[]{:S(2)}) %collective-permute-start.24) | collective-permute-done | bytes 262176 | tf_op jit(solution)/shard_map/ppermute | solution.py:539
  133.4 2.8 %collective-permute-done.25 = bf16[64,2048]{1,0:T(8,128)(2,1)S(1)} collective-permute-done((bf16[64,2048]{1,0:T(8,128)(2,1)S(1)}, bf16[64,2048]{1,0:T(8,128)(2,1)S(1)}, u32[]{:S(2)}, u32[]{:S(2)}) %collective-permute-start.25) | collective-permute-done | bytes 262176 | tf_op jit(solution)/shard_map/ppermute | solution.py:539
  136.2 3.3 %new_state.3 = (bf16[8,1,8,512,128]{4,3,2,1,0:T(8,128)(2,1)}, bf16[256,512]{1,0:T(8,128)(2,1)S(1)}) custom-call(s32[512,2]{1,0:T(8,128)S(1)} %broadcast_bitcast_fusion.meta_ref.refs_0_, bf16[512,512]{1,0:T(8,128)(2,1)S(1)} %copy-done.16, bf16[512,128]{1,0:T(8,128)(2,1)S(1)} %copy-done.33, ...), custom_call_target="tpu_custom_call", output_to_operand_aliasing={{0}: (7, {})} | custom-call | flops 1073741824 | bytes 16777216 | tf_op jit(solution)/shard_map/new_state/pallas_call | solution.py:465
  141.7 4.2 %collective-permute-done.26 = bf16[64,2048]{1,0:T(8,128)(2,1)S(1)} collective-permute-done((bf16[64,2048]{1,0:T(8,128)(2,1)S(1)}, bf16[64,2048]{1,0:T(8,128)(2,1)S(1)}, u32[]{:S(2)}, u32[]{:S(2)}) %collective-permute-start.26) | collective-permute-done | bytes 262176 | tf_op jit(solution)/shard_map/ppermute | solution.py:539
  149.6 2.8 %collective-permute-done.28 = bf16[64,2048]{1,0:T(8,128)(2,1)S(1)} collective-permute-done((bf16[64,2048]{1,0:T(8,128)(2,1)S(1)}, bf16[64,2048]{1,0:T(8,128)(2,1)S(1)}, u32[]{:S(2)}, u32[]{:S(2)}) %collective-permute-start.28) | collective-permute-done | bytes 262176 | tf_op jit(solution)/shard_map/ppermute | solution.py:539
  164.6 2.8 %collective-permute-done.30 = bf16[64,2048]{1,0:T(8,128)(2,1)S(1)} collective-permute-done((bf16[64,2048]{1,0:T(8,128)(2,1)S(1)}, bf16[64,2048]{1,0:T(8,128)(2,1)S(1)}, u32[]{:S(2)}, u32[]{:S(2)}) %collective-permute-start.30) | collective-permute-done | bytes 262176 | tf_op jit(solution)/shard_map/ppermute | solution.py:539
  170.2 4.6 %collective-permute-done.31 = bf16[64,2048]{1,0:T(8,128)(2,1)S(1)} collective-permute-done((bf16[64,2048]{1,0:T(8,128)(2,1)S(1)}, bf16[64,2048]{1,0:T(8,128)(2,1)S(1)}, u32[]{:S(2)}, u32[]{:S(2)}) %collective-permute-start.31) | collective-permute-done | bytes 262176 | tf_op jit(solution)/shard_map/ppermute | solution.py:539
  (223 shorter events, 67.3 us)
Async XLA Ops:
  1.7 9.1 %collective-permute-start.7 = (bf16[32,4096]{1,0:T(8,128)(2,1)S(1)}, bf16[32,4096]{1,0:T(8,128)(2,1)S(1)}, u32[]{:S(2)}, u32[]{:S(2)}) collective-permute-start(bf16[32,4096]{1,0:T(8,128)(2,1)S(1)} %get-tuple-element.130.refs_0_), channel_id=1, source_target_pairs={{0,4},{4,8},{8,12},{12,14},{14,10},{10,6},{6,2},{2,0},{5,1},{9,5},... | collective-permute-start | bytes 786440 | tf_op jit(solution)/shard_map/ppermute | solution.py:539
  4.8 7.7 %collective-permute-start = (bf16[32,4096]{1,0:T(8,128)(2,1)S(1)}, bf16[32,4096]{1,0:T(8,128)(2,1)S(1)}, u32[]{:S(2)}, u32[]{:S(2)}) collective-permute-start(bf16[32,4096]{1,0:T(8,128)(2,1)S(1)} %get-tuple-element.131.refs_1_), channel_id=1, source_target_pairs={{0,4},{4,8},{8,12},{12,14},{14,10},{10,6},{6,2},{2,0},{5,1},{9,5},... | collective-permute-start | bytes 786440 | tf_op jit(solution)/shard_map/ppermute | solution.py:539
  10.8 7.7 %collective-permute-start.8 = (bf16[32,4096]{1,0:T(8,128)(2,1)S(1)}, bf16[32,4096]{1,0:T(8,128)(2,1)S(1)}, u32[]{:S(2)}, u32[]{:S(2)}) collective-permute-start(bf16[32,4096]{1,0:T(8,128)(2,1)S(1)} %collective-permute-done.7.refs_2_), channel_id=1, source_target_pairs={{0,4},{4,8},{8,12},{12,14},{14,10},{10,6},{6,2},{2,0},{5,1},{9,5},... | collective-permute-start | bytes 786440 | tf_op jit(solution)/shard_map/ppermute | solution.py:539
  12.5 7.6 %collective-permute-start.1 = (bf16[32,4096]{1,0:T(8,128)(2,1)S(1)}, bf16[32,4096]{1,0:T(8,128)(2,1)S(1)}, u32[]{:S(2)}, u32[]{:S(2)}) collective-permute-start(bf16[32,4096]{1,0:T(8,128)(2,1)S(1)} %collective-permute-done.refs_3_), channel_id=1, source_target_pairs={{0,4},{4,8},{8,12},{12,14},{14,10},{10,6},{6,2},{2,0},{5,1},{9,5},... | collective-permute-start | bytes 786440 | tf_op jit(solution)/shard_map/ppermute | solution.py:539
  18.5 9.2 %collective-permute-start.9 = (bf16[32,4096]{1,0:T(8,128)(2,1)S(1)}, bf16[32,4096]{1,0:T(8,128)(2,1)S(1)}, u32[]{:S(2)}, u32[]{:S(2)}) collective-permute-start(bf16[32,4096]{1,0:T(8,128)(2,1)S(1)} %collective-permute-done.8.refs_4_), channel_id=1, source_target_pairs={{0,4},{4,8},{8,12},{12,14},{14,10},{10,6},{6,2},{2,0},{5,1},{9,5},... | collective-permute-start | bytes 786440 | tf_op jit(solution)/shard_map/ppermute | solution.py:539
  20.1 9.2 %collective-permute-start.2 = (bf16[32,4096]{1,0:T(8,128)(2,1)S(1)}, bf16[32,4096]{1,0:T(8,128)(2,1)S(1)}, u32[]{:S(2)}, u32[]{:S(2)}) collective-permute-start(bf16[32,4096]{1,0:T(8,128)(2,1)S(1)} %collective-permute-done.1.refs_5_), channel_id=1, source_target_pairs={{0,4},{4,8},{8,12},{12,14},{14,10},{10,6},{6,2},{2,0},{5,1},{9,5},... | collective-permute-start | bytes 786440 | tf_op jit(solution)/shard_map/ppermute | solution.py:539
  27.7 8.6 %collective-permute-start.10 = (bf16[32,4096]{1,0:T(8,128)(2,1)S(1)}, bf16[32,4096]{1,0:T(8,128)(2,1)S(1)}, u32[]{:S(2)}, u32[]{:S(2)}) collective-permute-start(bf16[32,4096]{1,0:T(8,128)(2,1)S(1)} %collective-permute-done.9.refs_6_), channel_id=1, source_target_pairs={{0,4},{4,8},{8,12},{12,14},{14,10},{10,6},{6,2},{2,0},{5,1},{9,5},... | collective-permute-start | bytes 786440 | tf_op jit(solution)/shard_map/ppermute | solution.py:539
  29.3 8.4 %collective-permute-start.3 = (bf16[32,4096]{1,0:T(8,128)(2,1)S(1)}, bf16[32,4096]{1,0:T(8,128)(2,1)S(1)}, u32[]{:S(2)}, u32[]{:S(2)}) collective-permute-start(bf16[32,4096]{1,0:T(8,128)(2,1)S(1)} %collective-permute-done.2.refs_7_), channel_id=1, source_target_pairs={{0,4},{4,8},{8,12},{12,14},{14,10},{10,6},{6,2},{2,0},{5,1},{9,5},... | collective-permute-start | bytes 786440 | tf_op jit(solution)/shard_map/ppermute | solution.py:539
  36.3 9.5 %collective-permute-start.11 = (bf16[32,4096]{1,0:T(8,128)(2,1)S(1)}, bf16[32,4096]{1,0:T(8,128)(2,1)S(1)}, u32[]{:S(2)}, u32[]{:S(2)}) collective-permute-start(bf16[32,4096]{1,0:T(8,128)(2,1)S(1)} %collective-permute-done.10.refs_0_), channel_id=1, source_target_pairs={{0,4},{4,8},{8,12},{12,14},{14,10},{10,6},{6,2},{2,0},{5,1},{9,5},... | collective-permute-start | bytes 786440 | tf_op jit(solution)/shard_map/ppermute | solution.py:539
  37.7 8.6 %collective-permute-start.4 = (bf16[32,4096]{1,0:T(8,128)(2,1)S(1)}, bf16[32,4096]{1,0:T(8,128)(2,1)S(1)}, u32[]{:S(2)}, u32[]{:S(2)}) collective-permute-start(bf16[32,4096]{1,0:T(8,128)(2,1)S(1)} %collective-permute-done.3.refs_1_), channel_id=1, source_target_pairs={{0,4},{4,8},{8,12},{12,14},{14,10},{10,6},{6,2},{2,0},{5,1},{9,5},... | collective-permute-start | bytes 786440 | tf_op jit(solution)/shard_map/ppermute | solution.py:539
  45.9 7.5 %collective-permute-start.12 = (bf16[32,4096]{1,0:T(8,128)(2,1)S(1)}, bf16[32,4096]{1,0:T(8,128)(2,1)}, u32[]{:S(2)}, u32[]{:S(2)}) collective-permute-start(bf16[32,4096]{1,0:T(8,128)(2,1)S(1)} %collective-permute-done.11.refs_2_), channel_id=1, source_target_pairs={{0,4},{4,8},{8,12},{12,14},{14,10},{10,6},{6,2},{2,0},{5,1},{9,5},... | collective-permute-start | bytes 786440 | tf_op jit(solution)/shard_map/ppermute | solution.py:539
  46.3 8.8 %collective-permute-start.5 = (bf16[32,4096]{1,0:T(8,128)(2,1)S(1)}, bf16[32,4096]{1,0:T(8,128)(2,1)}, u32[]{:S(2)}, u32[]{:S(2)}) collective-permute-start(bf16[32,4096]{1,0:T(8,128)(2,1)S(1)} %collective-permute-done.4.refs_3_), channel_id=1, source_target_pairs={{0,4},{4,8},{8,12},{12,14},{14,10},{10,6},{6,2},{2,0},{5,1},{9,5},... | collective-permute-start | bytes 786440 | tf_op jit(solution)/shard_map/ppermute | solution.py:539
  53.4 9.5 %collective-permute-start.13 = (bf16[32,4096]{1,0:T(8,128)(2,1)}, bf16[32,4096]{1,0:T(8,128)(2,1)}, u32[]{:S(2)}, u32[]{:S(2)}) collective-permute-start(bf16[32,4096]{1,0:T(8,128)(2,1)} %collective-permute-done.12.refs_4_), channel_id=1, source_target_pairs={{0,4},{4,8},{8,12},{12,14},{14,10},{10,6},{6,2},{2,0},{5,1},{9,5},... | collective-permute-start | bytes 786440 | tf_op jit(solution)/shard_map/ppermute | solution.py:539
  55.1 7.8 %collective-permute-start.6 = (bf16[32,4096]{1,0:T(8,128)(2,1)}, bf16[32,4096]{1,0:T(8,128)(2,1)}, u32[]{:S(2)}, u32[]{:S(2)}) collective-permute-start(bf16[32,4096]{1,0:T(8,128)(2,1)} %collective-permute-done.5.refs_5_), channel_id=1, source_target_pairs={{0,4},{4,8},{8,12},{12,14},{14,10},{10,6},{6,2},{2,0},{5,1},{9,5},... | collective-permute-start | bytes 786440 | tf_op jit(solution)/shard_map/ppermute | solution.py:539
  73.0 11.0 %collective-permute-start.15 = (bf16[512,1024]{1,0:T(8,128)(2,1)}, bf16[512,1024]{1,0:T(8,128)(2,1)}, u32[]{:S(2)}, u32[]{:S(2)}) collective-permute-start(bf16[512,1024]{1,0:T(8,128)(2,1)} %project.6), channel_id=1, source_target_pairs={{0,1},{1,0},{2,3},{3,2},{4,5},{5,4},{6,7},{7,6},{8,9},{9,8},{10,11... | collective-permute-start | bytes 3145736 | tf_op jit(solution)/shard_map/ppermute | solution.py:542
  74.9 9.0 %collective-permute-start.16 = (bf16[512,128]{1,0:T(8,128)(2,1)S(1)}, bf16[512,128]{1,0:T(8,128)(2,1)S(1)}, u32[]{:S(2)}, u32[]{:S(2)}) collective-permute-start(bf16[512,128]{1,0:T(8,128)(2,1)S(1)} %slice.24.raw_ref), channel_id=1, source_target_pairs={{8,0},{0,2},{10,4},{2,6},{12,8},{4,10},{14,12},{6,14},{9,1},{1,3},... | collective-permute-start | bytes 393224 | tf_op jit(solution)/shard_map/ppermute | solution.py:606
  76.2 7.8 %collective-permute-start.17 = (bf16[512,128]{1,0:T(8,128)(2,1)S(1)}, bf16[512,128]{1,0:T(8,128)(2,1)S(1)}, u32[]{:S(2)}, u32[]{:S(2)}) collective-permute-start(bf16[512,128]{1,0:T(8,128)(2,1)S(1)} %slice.24.raw_ref), channel_id=1, source_target_pairs={{0,0},{8,2},{2,4},{10,6},{4,8},{12,10},{6,12},{14,14},{1,1},{9,3},... | collective-permute-start | bytes 393224 | tf_op jit(solution)/shard_map/ppermute | solution.py:606
  94.7 12.4 %collective-permute-start.19 = (bf16[512,512]{1,0:T(8,128)(2,1)S(1)}, bf16[512,512]{1,0:T(8,128)(2,1)S(1)}, u32[]{:S(2)}, u32[]{:S(2)}) collective-permute-start(bf16[512,512]{1,0:T(8,128)(2,1)S(1)} %get-tuple-element.93.mine_ref), channel_id=1, source_target_pairs={{0,1},{1,0},{2,3},{3,2},{4,5},{5,4},{6,7},{7,6},{8,9},{9,8},{10,11... | collective-permute-start | bytes 1572872 | tf_op jit(solution)/shard_map/ppermute | solution.py:542
  98.1 9.0 %collective-permute-start.21 = (bf16[96,128]{1,0:T(8,128)(2,1)S(1)}, bf16[96,128]{1,0:T(8,128)(2,1)S(1)}, u32[]{:S(2)}, u32[]{:S(2)}) collective-permute-start(bf16[96,128]{1,0:T(8,128)(2,1)S(1)} %constant_dynamic-slice_fusion.2), channel_id=1, source_target_pairs={{0,8},{2,10},{4,12},{6,14},{8,0},{10,2},{12,4},{14,6},{1,9},{3,11}... | collective-permute-start | bytes 73736 | tf_op jit(solution)/shard_map/ppermute | solution.py:640
  107.1 12.4 %collective-permute-start.22 = (bf16[2,96,128]{2,1,0:T(8,128)(2,1)S(1)}, bf16[2,96,128]{2,1,0:T(8,128)(2,1)S(1)}, u32[]{:S(2)}, u32[]{:S(2)}) collective-permute-start(bf16[2,96,128]{2,1,0:T(8,128)(2,1)S(1)} %maximum_select_fusion.3), channel_id=1, source_target_pairs={{0,4},{2,6},{4,0},{6,2},{8,12},{10,14},{12,8},{14,10},{1,5},{3,7},... | collective-permute-start | bytes 147464 | tf_op jit(solution)/shard_map/ppermute | solution.py:640
  117.7 7.5 %collective-permute-start.32 = (bf16[64,2048]{1,0:T(8,128)(2,1)S(1)}, bf16[64,2048]{1,0:T(8,128)(2,1)S(1)}, u32[]{:S(2)}, u32[]{:S(2)}) collective-permute-start(bf16[64,2048]{1,0:T(8,128)(2,1)S(1)} %constant_dynamic-slice_fusion), channel_id=1, source_target_pairs={{0,4},{4,8},{8,12},{12,14},{14,10},{10,6},{6,2},{2,0},{5,1},{9,5},... | collective-permute-start | bytes 786440 | tf_op jit(solution)/shard_map/ppermute | solution.py:539
  125.3 7.1 %collective-permute-start.33 = (bf16[64,2048]{1,0:T(8,128)(2,1)S(1)}, bf16[64,2048]{1,0:T(8,128)(2,1)S(1)}, u32[]{:S(2)}, u32[]{:S(2)}) collective-permute-start(bf16[64,2048]{1,0:T(8,128)(2,1)S(1)} %add_convert_fusion.6), channel_id=1, source_target_pairs={{0,4},{4,8},{8,12},{12,14},{14,10},{10,6},{6,2},{2,0},{5,1},{9,5},... | collective-permute-start | bytes 786440 | tf_op jit(solution)/shard_map/ppermute | solution.py:539
  132.5 7.8 %collective-permute-start.34 = (bf16[64,2048]{1,0:T(8,128)(2,1)S(1)}, bf16[64,2048]{1,0:T(8,128)(2,1)S(1)}, u32[]{:S(2)}, u32[]{:S(2)}) collective-permute-start(bf16[64,2048]{1,0:T(8,128)(2,1)S(1)} %add_convert_fusion.5), channel_id=1, source_target_pairs={{0,4},{4,8},{8,12},{12,14},{14,10},{10,6},{6,2},{2,0},{5,1},{9,5},... | collective-permute-start | bytes 786440 | tf_op jit(solution)/shard_map/ppermute | solution.py:539
  140.4 8.3 %collective-permute-start.35 = (bf16[64,2048]{1,0:T(8,128)(2,1)S(1)}, bf16[64,2048]{1,0:T(8,128)(2,1)S(1)}, u32[]{:S(2)}, u32[]{:S(2)}) collective-permute-start(bf16[64,2048]{1,0:T(8,128)(2,1)S(1)} %add_convert_fusion.4), channel_id=1, source_target_pairs={{0,4},{4,8},{8,12},{12,14},{14,10},{10,6},{6,2},{2,0},{5,1},{9,5},... | collective-permute-start | bytes 786440 | tf_op jit(solution)/shard_map/ppermute | solution.py:539
  (65 other events, 502.3 us)

commit v5 on v4

--- a/solution.py
+++ b/solution.py
@@ -120,7 +120,7 @@
     put(o_ref, total, olds[0] if old else None)
 
 
-def project(seq, which, ins, w, w_ext, dtype, ext_dtypes, olds=(), bn=512):
+def project(seq, which, ins, w, w_ext, dtype, ext_dtypes, olds=(), bn=512, shape=pltpu.HBM):
     parts = len(ins)
     rc, k = ins[0].shape
     m = rc * parts
@@ -145,8 +145,8 @@
             + [whole_block((out_m, ext_cols)) for _ in ext_dtypes],
             scratch_shapes=[pltpu.VMEM((m, k), BF)],
         ),
-        out_shape=[pltpu.HBM((out_m, cols), dtype)]
-        + [pltpu.HBM((out_m, ext_cols), d) for d in ext_dtypes],
+        out_shape=[shape((out_m, cols), dtype)]
+        + [shape((out_m, ext_cols), d) for d in ext_dtypes],
         compiler_params=params(46),
         cost_estimate=cost(2 * m * k * (cols + ext_cols), 2 * k * cols + 2 * m * k),
         name="project",
@@ -615,7 +615,7 @@
     theirs = other(theirs)
     late, bc_own, dt = lax.optimization_barrier((blocks[-1], bc_own, dt))
     blocks[-1] = late
-    (mine,) = project(seq, inc1, blocks[split:], w, w_ext, F32, [], (mine_1,))
+    (mine,) = project(seq, inc1, blocks[split:], w, w_ext, F32, [], (mine_1,), shape=jax.ShapeDtypeStruct)
     gated, ssq, xw, bconv, sw, xraw = ssm(
         group1, rb, meta, theirs, mine, dt, b_raw, c_raw, x_state, bc_state, conv_x, conv_bc, heads, norm_gain, state
     )

time: 177 us -> 175 us (0.989)
    unnamed x102 -> x100, local copies, waits for them, and re-layouts: 8.42 us -> 6.83 us
where the time goes in v5:
time: 175 us; the launch traced here: 174 us
  Pallas kernels  69.6 us (40%)
  waiting for transfers between devices  41.2 us (24%)
  starting transfers between devices  40.7 us (23%)
  local copies, waits for them, and re-layouts  13.3 us (8%)
  other arithmetic  8.14 us (5%)
    ppermute x28, waiting for transfers between devices, onward(): return lax.ppermute(a, ('outc', 'inc'), ring)  34.8 us
    ppermute x28, starting transfers between devices, onward(): return lax.ppermute(a, ('outc', 'inc'), ring)  31.4 us
    pallas_call x4, Pallas kernels, project(): pl.pallas_call(functools.partial(project_kernel, parts, len(olds)), grid_...  25.3 us
    pallas_call x4, Pallas kernels, relayout(): pl.pallas_call(kernel, grid=(steps,), in_specs=specs, out_specs=pl.BlockS...  18.1 us
    pallas_call x1, Pallas kernels, ssm(): pl.pallas_call(ssm_kernel, grid_spec=pltpu.PrefetchScalarGridSpec(num_sca...  9.1 us
    unnamed x100, local copies, waits for them, and re-layouts  6.83 us
    pallas_call x2, Pallas kernels, out_project(): pl.pallas_call(functools.partial(out_kernel, scale_by), grid_spec=pltpu.P...  6.77 us
    pallas_call x2, Pallas kernels, new_state(): pl.pallas_call(kernel, grid=(steps,), in_specs=specs, out_specs=[states,...  6.58 us
  transfers between devices with their start and end apart: 39, of which 17 were waited for; matrix products, arithmetic and copies ran while one was open for 8% of the time, Pallas kernels for 33%

profile of v5, /device:TPU:0, one launch (start us, length us, event | category | flops | bytes accessed | tf_op | source)
XLA Modules:
  0.0 174.3 jit_solution(5023938654880813968)
XLA Ops:
  1.7 3.1 %collective-permute-start.7 = (bf16[32,4096]{1,0:T(8,128)(2,1)S(1)}, bf16[32,4096]{1,0:T(8,128)(2,1)S(1)}, u32[]{:S(2)}, u32[]{:S(2)}) collective-permute-start(bf16[32,4096]{1,0:T(8,128)(2,1)S(1)} %get-tuple-element.130.refs_0_), channel_id=1, source_target_pairs={{0,4},{4,8},{8,12},{12,14},{14,10},{10,6},{6,2},{2,0},{5,1},{9,5},... | collective-permute-start | bytes 786440 | tf_op jit(solution)/shard_map/ppermute | solution.py:539
  6.4 4.4 %relayout.4._ = bf16[2,4096,1024]{2,1,0:T(8,128)(2,1)} custom-call(bf16[4096,16,128]{2,1,0:T(8,128)(2,1)} %w_ref.7), custom_call_target="tpu_custom_call" | custom-call | flops 1073741824 | bytes 8388608 | tf_op jit(solution)/shard_map/relayout/pallas_call | solution.py:77
  14.0 4.5 %relayout.5._ = bf16[2,4096,1024]{2,1,0:T(8,128)(2,1)} custom-call(bf16[4096,16,128]{2,1,0:T(8,128)(2,1)} %w_ref.7, bf16[2,4096,1024]{2,1,0:T(8,128)(2,1)} %relayout.4._), custom_call_target="tpu_custom_call", output_to_operand_aliasing={{}: (1, {})} | custom-call | flops 1073741824 | bytes 8388608 | tf_op jit(solution)/shard_map/relayout/pallas_call | solution.py:77
  23.1 4.6 %relayout.6._ = bf16[2,4096,1024]{2,1,0:T(8,128)(2,1)} custom-call(bf16[4096,16,128]{2,1,0:T(8,128)(2,1)} %w_ref.7, bf16[2,4096,1024]{2,1,0:T(8,128)(2,1)} %relayout.5._), custom_call_target="tpu_custom_call", output_to_operand_aliasing={{}: (1, {})} | custom-call | flops 1073741824 | bytes 8388608 | tf_op jit(solution)/shard_map/relayout/pallas_call | solution.py:77
  31.8 4.6 %relayout.7.refs_8_ = bf16[2,4096,1024]{2,1,0:T(8,128)(2,1)} custom-call(bf16[4096,16,128]{2,1,0:T(8,128)(2,1)} %w_ref.7, bf16[2,4096,1024]{2,1,0:T(8,128)(2,1)} %relayout.6._), custom_call_target="tpu_custom_call", output_to_operand_aliasing={{}: (1, {})} | custom-call | flops 1073741824 | bytes 8388608 | tf_op jit(solution)/shard_map/relayout/pallas_call | solution.py:77
  39.1 6.8 %project.4 = (bf16[256,1024]{1,0:T(8,128)(2,1)}, f32[256,256]{1,0:T(8,128)}) custom-call(s32[8]{0:T(128)S(1)} %compare_select_fusion.2.seq_ref, s32[1]{0:T(128)S(6)} %sub.38.which_ref, bf16[32,4096]{1,0:T(8,128)(2,1)S(1)} %get-tuple-element.130.refs_0_, bf16[32,4096]{1,0:T(8,128)(2,1)S(1)} %copy-done.14, bf16[32,4096]{1,0:T(8,128)(2,1)S(1)} %copy-done.20, ...), custom_call_target="tpu_custom_call" | custom-call | flops 2684354560 | bytes 10485760 | tf_op jit(solution)/shard_map/project/pallas_call | solution.py:138
  47.2 6.2 %project.5.refs_10_ = f32[256,1024]{1,0:T(8,128)} custom-call(s32[8]{0:T(128)S(1)} %compare_select_fusion.2.seq_ref, s32[1]{0:T(128)} %bitcast.which_ref.inc_ref, bf16[32,4096]{1,0:T(8,128)(2,1)S(1)} %get-tuple-element.130.refs_0_, bf16[32,4096]{1,0:T(8,128)(2,1)S(1)} %copy-done.14, bf16[32,4096]{1,0:T(8,128)(2,1)S(1)} %copy-done.20, ...), custom_call_target="tpu_custom_call" | custom-call | flops 2684354560 | bytes 10485760 | tf_op jit(solution)/shard_map/project/pallas_call | solution.py:138
  57.8 5.1 %collective-permute-done.6.refs_7_ = bf16[32,4096]{1,0:T(8,128)(2,1)} collective-permute-done((bf16[32,4096]{1,0:T(8,128)(2,1)}, bf16[32,4096]{1,0:T(8,128)(2,1)}, u32[]{:S(2)}, u32[]{:S(2)}) %collective-permute-start.6) | collective-permute-done | bytes 262176 | tf_op jit(solution)/shard_map/ppermute | solution.py:539
  66.5 6.5 %project.6 = bf16[512,1024]{1,0:T(8,128)(2,1)} custom-call(s32[8]{0:T(128)S(1)} %compare_select_fusion.2.seq_ref, s32[1]{0:T(128)S(6)} %sub.38.which_ref, bf16[32,4096]{1,0:T(8,128)(2,1)S(1)} %collective-permute-done.10.refs_0_, bf16[32,4096]{1,0:T(8,128)(2,1)S(1)} %collective-permute-done.3.refs_1_, bf16[32,4096]{1,0:T(8,128)(2,1)S(1)} %collective-permute-done.11.refs_2_, ...), custom_call_target="tpu_custom_call" | custom-call | flops 2684354560 | bytes 10485760 | tf_op jit(solution)/shard_map/project/pallas_call | solution.py:138
  77.3 5.8 %project.7.mine_ref = f32[512,1024]{1,0:T(8,128)S(1)} custom-call(s32[8]{0:T(128)S(1)} %compare_select_fusion.2.seq_ref, s32[1]{0:T(128)} %bitcast.which_ref.inc_ref, bf16[32,4096]{1,0:T(8,128)(2,1)S(1)} %copy-done.6, bf16[32,4096]{1,0:T(8,128)(2,1)S(1)} %copy-done.8, bf16[32,4096]{1,0:T(8,128)(2,1)S(1)} %copy-done.10, bf16[32,4096]{1,0:T(8,128)(2,1)S(1)} %copy-done.12, ...), custom_call_target="tpu_custom_call" | custom-call | flops 2684354560 | bytes 10485760 | tf_op jit(solution)/shard_map/project/pallas_call | solution.py:138
  83.3 9.1 %ssm.1 = (bf16[512,512]{1,0:T(8,128)(2,1)S(1)}, f32[8,512]{1,0:T(8,128)S(1)}, bf16[512,512]{1,0:T(8,128)(2,1)}, bf16[512,128]{1,0:T(8,128)(2,1)}, f32[512,128]{1,0:T(8,128)}, /*index=5*/bf16[512,512]{1,0:T(8,128)(2,1)}) custom-call(s32[1]{0:T(128)} %bitcast.9.group_ref, s32[512,2]{1,0:T(8,128)S(1)} %broadcast_bitcast_fusion.meta_ref.refs_0_, ...), custom_call_target="tpu_custom_call" | custom-call | flops 2147483648 | bytes 25165824 | tf_op jit(solution)/shard_map/ssm/pallas_call | solution.py:340
  95.7 5.2 %collective-permute-start.21 = (bf16[96,128]{1,0:T(8,128)(2,1)S(1)}, bf16[96,128]{1,0:T(8,128)(2,1)S(1)}, u32[]{:S(2)}, u32[]{:S(2)}) collective-permute-start(bf16[96,128]{1,0:T(8,128)(2,1)S(1)} %constant_dynamic-slice_fusion.2), channel_id=1, source_target_pairs={{0,8},{2,10},{4,12},{6,14},{8,0},{10,2},{12,4},{14,6},{1,9},{3,11}... | collective-permute-start | bytes 73736 | tf_op jit(solution)/shard_map/ppermute | solution.py:640
  101.0 3.7 %collective-permute-done.20 = f32[8,512]{1,0:T(8,128)S(1)} collective-permute-done((f32[8,512]{1,0:T(8,128)S(1)}, f32[8,512]{1,0:T(8,128)S(1)}, u32[]{:S(2)}, u32[]{:S(2)}) %collective-permute-start.20) | collective-permute-done | bytes 16416 | tf_op jit(solution)/shard_map/ppermute | solution.py:631
  105.1 3.4 %copy-done = bf16[1024,4096]{1,0:T(8,128)(2,1)S(1)} copy-done((bf16[1024,4096]{1,0:T(8,128)(2,1)S(1)}, bf16[1024,4096]{1,0:T(8,128)(2,1)}, u32[]{:S(2)}) %copy-start) | copy-done | bytes 8388632
  108.5 3.4 %out_project.3 = bf16[512,2048]{1,0:T(8,128)(2,1)S(1)} custom-call(s32[1]{0:T(128)} %bitcast.which_ref.inc_ref, bf16[512,512]{1,0:T(8,128)(2,1)S(1)} %get-tuple-element.93.mine_ref, bf16[512,512]{1,0:T(8,128)(2,1)S(1)} %collective-permute-done.19.theirs_ref, bf16[1024,4096]{1,0:T(8,128)(2,1)S(1)} %copy-done, bf16[1024,4096]{1,0:T(8,128)(2,1)S(1)} %copy-done, ...), custom_call_target="tpu_custom_call" | custom-call | flops 2147483648 | bytes 8388608 | tf_op jit(solution)/shard_map/out_project/pallas_call | solution.py:492
  112.0 3.4 %out_project.2 = bf16[512,2048]{1,0:T(8,128)(2,1)S(1)} custom-call(s32[1]{0:T(128)} %bitcast.which_ref.inc_ref, bf16[512,512]{1,0:T(8,128)(2,1)S(1)} %get-tuple-element.93.mine_ref, bf16[512,512]{1,0:T(8,128)(2,1)S(1)} %collective-permute-done.19.theirs_ref, bf16[1024,4096]{1,0:T(8,128)(2,1)S(1)} %copy-done, bf16[1024,4096]{1,0:T(8,128)(2,1)S(1)} %copy-done, ...), custom_call_target="tpu_custom_call" | custom-call | flops 2147483648 | bytes 8388608 | tf_op jit(solution)/shard_map/out_project/pallas_call | solution.py:492
  117.6 3.3 %new_state.2 = (bf16[8,1,8,512,128]{4,3,2,1,0:T(8,128)(2,1)}, bf16[256,512]{1,0:T(8,128)(2,1)S(1)}) custom-call(s32[512,2]{1,0:T(8,128)S(1)} %broadcast_bitcast_fusion.meta_ref.refs_0_, bf16[512,512]{1,0:T(8,128)(2,1)S(1)} %copy-done.15, bf16[512,128]{1,0:T(8,128)(2,1)S(1)} %copy-done.32, f32[512,128]{1,0:T(8,128)S(1)} %copy-done.31, ...), custom_call_target="tpu_custom_call" | custom-call | flops 1073741824 | bytes 16777216 | tf_op jit(solution)/shard_map/new_state/pallas_call | solution.py:465
  123.7 3.6 %collective-permute-done.24 = bf16[64,2048]{1,0:T(8,128)(2,1)S(1)} collective-permute-done((bf16[64,2048]{1,0:T(8,128)(2,1)S(1)}, bf16[64,2048]{1,0:T(8,128)(2,1)S(1)}, u32[]{:S(2)}, u32[]{:S(2)}) %collective-permute-start.24) | collective-permute-done | bytes 262176 | tf_op jit(solution)/shard_map/ppermute | solution.py:539
  131.0 2.8 %collective-permute-done.25 = bf16[64,2048]{1,0:T(8,128)(2,1)S(1)} collective-permute-done((bf16[64,2048]{1,0:T(8,128)(2,1)S(1)}, bf16[64,2048]{1,0:T(8,128)(2,1)S(1)}, u32[]{:S(2)}, u32[]{:S(2)}) %collective-permute-start.25) | collective-permute-done | bytes 262176 | tf_op jit(solution)/shard_map/ppermute | solution.py:539
  133.9 3.3 %new_state.3 = (bf16[8,1,8,512,128]{4,3,2,1,0:T(8,128)(2,1)}, bf16[256,512]{1,0:T(8,128)(2,1)S(1)}) custom-call(s32[512,2]{1,0:T(8,128)S(1)} %broadcast_bitcast_fusion.meta_ref.refs_0_, bf16[512,512]{1,0:T(8,128)(2,1)S(1)} %copy-done.15, bf16[512,128]{1,0:T(8,128)(2,1)S(1)} %copy-done.32, ...), custom_call_target="tpu_custom_call", output_to_operand_aliasing={{0}: (7, {})} | custom-call | flops 1073741824 | bytes 16777216 | tf_op jit(solution)/shard_map/new_state/pallas_call | solution.py:465
  139.3 4.2 %collective-permute-done.26 = bf16[64,2048]{1,0:T(8,128)(2,1)S(1)} collective-permute-done((bf16[64,2048]{1,0:T(8,128)(2,1)S(1)}, bf16[64,2048]{1,0:T(8,128)(2,1)S(1)}, u32[]{:S(2)}, u32[]{:S(2)}) %collective-permute-start.26) | collective-permute-done | bytes 262176 | tf_op jit(solution)/shard_map/ppermute | solution.py:539
  147.3 2.8 %collective-permute-done.28 = bf16[64,2048]{1,0:T(8,128)(2,1)S(1)} collective-permute-done((bf16[64,2048]{1,0:T(8,128)(2,1)S(1)}, bf16[64,2048]{1,0:T(8,128)(2,1)S(1)}, u32[]{:S(2)}, u32[]{:S(2)}) %collective-permute-start.28) | collective-permute-done | bytes 262176 | tf_op jit(solution)/shard_map/ppermute | solution.py:539
  162.2 2.8 %collective-permute-done.30 = bf16[64,2048]{1,0:T(8,128)(2,1)S(1)} collective-permute-done((bf16[64,2048]{1,0:T(8,128)(2,1)S(1)}, bf16[64,2048]{1,0:T(8,128)(2,1)S(1)}, u32[]{:S(2)}, u32[]{:S(2)}) %collective-permute-start.30) | collective-permute-done | bytes 262176 | tf_op jit(solution)/shard_map/ppermute | solution.py:539
  167.9 4.6 %collective-permute-done.31 = bf16[64,2048]{1,0:T(8,128)(2,1)S(1)} collective-permute-done((bf16[64,2048]{1,0:T(8,128)(2,1)S(1)}, bf16[64,2048]{1,0:T(8,128)(2,1)S(1)}, u32[]{:S(2)}, u32[]{:S(2)}) %collective-permute-start.31) | collective-permute-done | bytes 262176 | tf_op jit(solution)/shard_map/ppermute | solution.py:539
  (221 shorter events, 65.7 us)
Async XLA Ops:
  1.7 9.1 %collective-permute-start.7 = (bf16[32,4096]{1,0:T(8,128)(2,1)S(1)}, bf16[32,4096]{1,0:T(8,128)(2,1)S(1)}, u32[]{:S(2)}, u32[]{:S(2)}) collective-permute-start(bf16[32,4096]{1,0:T(8,128)(2,1)S(1)} %get-tuple-element.130.refs_0_), channel_id=1, source_target_pairs={{0,4},{4,8},{8,12},{12,14},{14,10},{10,6},{6,2},{2,0},{5,1},{9,5},... | collective-permute-start | bytes 786440 | tf_op jit(solution)/shard_map/ppermute | solution.py:539
  4.8 7.7 %collective-permute-start = (bf16[32,4096]{1,0:T(8,128)(2,1)S(1)}, bf16[32,4096]{1,0:T(8,128)(2,1)S(1)}, u32[]{:S(2)}, u32[]{:S(2)}) collective-permute-start(bf16[32,4096]{1,0:T(8,128)(2,1)S(1)} %get-tuple-element.131.refs_1_), channel_id=1, source_target_pairs={{0,4},{4,8},{8,12},{12,14},{14,10},{10,6},{6,2},{2,0},{5,1},{9,5},... | collective-permute-start | bytes 786440 | tf_op jit(solution)/shard_map/ppermute | solution.py:539
  10.8 7.7 %collective-permute-start.8 = (bf16[32,4096]{1,0:T(8,128)(2,1)S(1)}, bf16[32,4096]{1,0:T(8,128)(2,1)S(1)}, u32[]{:S(2)}, u32[]{:S(2)}) collective-permute-start(bf16[32,4096]{1,0:T(8,128)(2,1)S(1)} %collective-permute-done.7.refs_2_), channel_id=1, source_target_pairs={{0,4},{4,8},{8,12},{12,14},{14,10},{10,6},{6,2},{2,0},{5,1},{9,5},... | collective-permute-start | bytes 786440 | tf_op jit(solution)/shard_map/ppermute | solution.py:539
  12.5 7.7 %collective-permute-start.1 = (bf16[32,4096]{1,0:T(8,128)(2,1)S(1)}, bf16[32,4096]{1,0:T(8,128)(2,1)S(1)}, u32[]{:S(2)}, u32[]{:S(2)}) collective-permute-start(bf16[32,4096]{1,0:T(8,128)(2,1)S(1)} %collective-permute-done.refs_3_), channel_id=1, source_target_pairs={{0,4},{4,8},{8,12},{12,14},{14,10},{10,6},{6,2},{2,0},{5,1},{9,5},... | collective-permute-start | bytes 786440 | tf_op jit(solution)/shard_map/ppermute | solution.py:539
  18.5 9.2 %collective-permute-start.9 = (bf16[32,4096]{1,0:T(8,128)(2,1)S(1)}, bf16[32,4096]{1,0:T(8,128)(2,1)S(1)}, u32[]{:S(2)}, u32[]{:S(2)}) collective-permute-start(bf16[32,4096]{1,0:T(8,128)(2,1)S(1)} %collective-permute-done.8.refs_4_), channel_id=1, source_target_pairs={{0,4},{4,8},{8,12},{12,14},{14,10},{10,6},{6,2},{2,0},{5,1},{9,5},... | collective-permute-start | bytes 786440 | tf_op jit(solution)/shard_map/ppermute | solution.py:539
  20.1 9.2 %collective-permute-start.2 = (bf16[32,4096]{1,0:T(8,128)(2,1)S(1)}, bf16[32,4096]{1,0:T(8,128)(2,1)S(1)}, u32[]{:S(2)}, u32[]{:S(2)}) collective-permute-start(bf16[32,4096]{1,0:T(8,128)(2,1)S(1)} %collective-permute-done.1.refs_5_), channel_id=1, source_target_pairs={{0,4},{4,8},{8,12},{12,14},{14,10},{10,6},{6,2},{2,0},{5,1},{9,5},... | collective-permute-start | bytes 786440 | tf_op jit(solution)/shard_map/ppermute | solution.py:539
  27.7 8.6 %collective-permute-start.10 = (bf16[32,4096]{1,0:T(8,128)(2,1)S(1)}, bf16[32,4096]{1,0:T(8,128)(2,1)S(1)}, u32[]{:S(2)}, u32[]{:S(2)}) collective-permute-start(bf16[32,4096]{1,0:T(8,128)(2,1)S(1)} %collective-permute-done.9.refs_6_), channel_id=1, source_target_pairs={{0,4},{4,8},{8,12},{12,14},{14,10},{10,6},{6,2},{2,0},{5,1},{9,5},... | collective-permute-start | bytes 786440 | tf_op jit(solution)/shard_map/ppermute | solution.py:539
  29.3 8.4 %collective-permute-start.3 = (bf16[32,4096]{1,0:T(8,128)(2,1)S(1)}, bf16[32,4096]{1,0:T(8,128)(2,1)S(1)}, u32[]{:S(2)}, u32[]{:S(2)}) collective-permute-start(bf16[32,4096]{1,0:T(8,128)(2,1)S(1)} %collective-permute-done.2.refs_7_), channel_id=1, source_target_pairs={{0,4},{4,8},{8,12},{12,14},{14,10},{10,6},{6,2},{2,0},{5,1},{9,5},... | collective-permute-start | bytes 786440 | tf_op jit(solution)/shard_map/ppermute | solution.py:539
  36.4 9.5 %collective-permute-start.11 = (bf16[32,4096]{1,0:T(8,128)(2,1)S(1)}, bf16[32,4096]{1,0:T(8,128)(2,1)S(1)}, u32[]{:S(2)}, u32[]{:S(2)}) collective-permute-start(bf16[32,4096]{1,0:T(8,128)(2,1)S(1)} %collective-permute-done.10.refs_0_), channel_id=1, source_target_pairs={{0,4},{4,8},{8,12},{12,14},{14,10},{10,6},{6,2},{2,0},{5,1},{9,5},... | collective-permute-start | bytes 786440 | tf_op jit(solution)/shard_map/ppermute | solution.py:539
  37.7 8.6 %collective-permute-start.4 = (bf16[32,4096]{1,0:T(8,128)(2,1)S(1)}, bf16[32,4096]{1,0:T(8,128)(2,1)S(1)}, u32[]{:S(2)}, u32[]{:S(2)}) collective-permute-start(bf16[32,4096]{1,0:T(8,128)(2,1)S(1)} %collective-permute-done.3.refs_1_), channel_id=1, source_target_pairs={{0,4},{4,8},{8,12},{12,14},{14,10},{10,6},{6,2},{2,0},{5,1},{9,5},... | collective-permute-start | bytes 786440 | tf_op jit(solution)/shard_map/ppermute | solution.py:539
  45.9 7.6 %collective-permute-start.12 = (bf16[32,4096]{1,0:T(8,128)(2,1)S(1)}, bf16[32,4096]{1,0:T(8,128)(2,1)}, u32[]{:S(2)}, u32[]{:S(2)}) collective-permute-start(bf16[32,4096]{1,0:T(8,128)(2,1)S(1)} %collective-permute-done.11.refs_2_), channel_id=1, source_target_pairs={{0,4},{4,8},{8,12},{12,14},{14,10},{10,6},{6,2},{2,0},{5,1},{9,5},... | collective-permute-start | bytes 786440 | tf_op jit(solution)/shard_map/ppermute | solution.py:539
  46.3 8.8 %collective-permute-start.5 = (bf16[32,4096]{1,0:T(8,128)(2,1)S(1)}, bf16[32,4096]{1,0:T(8,128)(2,1)}, u32[]{:S(2)}, u32[]{:S(2)}) collective-permute-start(bf16[32,4096]{1,0:T(8,128)(2,1)S(1)} %collective-permute-done.4.refs_3_), channel_id=1, source_target_pairs={{0,4},{4,8},{8,12},{12,14},{14,10},{10,6},{6,2},{2,0},{5,1},{9,5},... | collective-permute-start | bytes 786440 | tf_op jit(solution)/shard_map/ppermute | solution.py:539
  53.4 9.5 %collective-permute-start.13 = (bf16[32,4096]{1,0:T(8,128)(2,1)}, bf16[32,4096]{1,0:T(8,128)(2,1)}, u32[]{:S(2)}, u32[]{:S(2)}) collective-permute-start(bf16[32,4096]{1,0:T(8,128)(2,1)} %collective-permute-done.12.refs_4_), channel_id=1, source_target_pairs={{0,4},{4,8},{8,12},{12,14},{14,10},{10,6},{6,2},{2,0},{5,1},{9,5},... | collective-permute-start | bytes 786440 | tf_op jit(solution)/shard_map/ppermute | solution.py:539
  55.2 7.8 %collective-permute-start.6 = (bf16[32,4096]{1,0:T(8,128)(2,1)}, bf16[32,4096]{1,0:T(8,128)(2,1)}, u32[]{:S(2)}, u32[]{:S(2)}) collective-permute-start(bf16[32,4096]{1,0:T(8,128)(2,1)} %collective-permute-done.5.refs_5_), channel_id=1, source_target_pairs={{0,4},{4,8},{8,12},{12,14},{14,10},{10,6},{6,2},{2,0},{5,1},{9,5},... | collective-permute-start | bytes 786440 | tf_op jit(solution)/shard_map/ppermute | solution.py:539
  73.0 10.2 %collective-permute-start.15 = (bf16[512,1024]{1,0:T(8,128)(2,1)}, bf16[512,1024]{1,0:T(8,128)(2,1)}, u32[]{:S(2)}, u32[]{:S(2)}) collective-permute-start(bf16[512,1024]{1,0:T(8,128)(2,1)} %project.6), channel_id=1, source_target_pairs={{0,1},{1,0},{2,3},{3,2},{4,5},{5,4},{6,7},{7,6},{8,9},{9,8},{10,11... | collective-permute-start | bytes 3145736 | tf_op jit(solution)/shard_map/ppermute | solution.py:542
  74.9 8.2 %collective-permute-start.16 = (bf16[512,128]{1,0:T(8,128)(2,1)S(1)}, bf16[512,128]{1,0:T(8,128)(2,1)S(1)}, u32[]{:S(2)}, u32[]{:S(2)}) collective-permute-start(bf16[512,128]{1,0:T(8,128)(2,1)S(1)} %slice.24.raw_ref), channel_id=1, source_target_pairs={{8,0},{0,2},{10,4},{2,6},{12,8},{4,10},{14,12},{6,14},{9,1},{1,3},... | collective-permute-start | bytes 393224 | tf_op jit(solution)/shard_map/ppermute | solution.py:606
  76.2 7.0 %collective-permute-start.17 = (bf16[512,128]{1,0:T(8,128)(2,1)S(1)}, bf16[512,128]{1,0:T(8,128)(2,1)S(1)}, u32[]{:S(2)}, u32[]{:S(2)}) collective-permute-start(bf16[512,128]{1,0:T(8,128)(2,1)S(1)} %slice.24.raw_ref), channel_id=1, source_target_pairs={{0,0},{8,2},{2,4},{10,6},{4,8},{12,10},{6,12},{14,14},{1,1},{9,3},... | collective-permute-start | bytes 393224 | tf_op jit(solution)/shard_map/ppermute | solution.py:606
  92.4 12.4 %collective-permute-start.19 = (bf16[512,512]{1,0:T(8,128)(2,1)S(1)}, bf16[512,512]{1,0:T(8,128)(2,1)S(1)}, u32[]{:S(2)}, u32[]{:S(2)}) collective-permute-start(bf16[512,512]{1,0:T(8,128)(2,1)S(1)} %get-tuple-element.93.mine_ref), channel_id=1, source_target_pairs={{0,1},{1,0},{2,3},{3,2},{4,5},{5,4},{6,7},{7,6},{8,9},{9,8},{10,11... | collective-permute-start | bytes 1572872 | tf_op jit(solution)/shard_map/ppermute | solution.py:542
  95.7 9.0 %collective-permute-start.21 = (bf16[96,128]{1,0:T(8,128)(2,1)S(1)}, bf16[96,128]{1,0:T(8,128)(2,1)S(1)}, u32[]{:S(2)}, u32[]{:S(2)}) collective-permute-start(bf16[96,128]{1,0:T(8,128)(2,1)S(1)} %constant_dynamic-slice_fusion.2), channel_id=1, source_target_pairs={{0,8},{2,10},{4,12},{6,14},{8,0},{10,2},{12,4},{14,6},{1,9},{3,11}... | collective-permute-start | bytes 73736 | tf_op jit(solution)/shard_map/ppermute | solution.py:640
  104.8 12.4 %collective-permute-start.22 = (bf16[2,96,128]{2,1,0:T(8,128)(2,1)S(1)}, bf16[2,96,128]{2,1,0:T(8,128)(2,1)S(1)}, u32[]{:S(2)}, u32[]{:S(2)}) collective-permute-start(bf16[2,96,128]{2,1,0:T(8,128)(2,1)S(1)} %maximum_select_fusion.3), channel_id=1, source_target_pairs={{0,4},{2,6},{4,0},{6,2},{8,12},{10,14},{12,8},{14,10},{1,5},{3,7},... | collective-permute-start | bytes 147464 | tf_op jit(solution)/shard_map/ppermute | solution.py:640
  115.4 7.5 %collective-permute-start.32 = (bf16[64,2048]{1,0:T(8,128)(2,1)S(1)}, bf16[64,2048]{1,0:T(8,128)(2,1)S(1)}, u32[]{:S(2)}, u32[]{:S(2)}) collective-permute-start(bf16[64,2048]{1,0:T(8,128)(2,1)S(1)} %constant_dynamic-slice_fusion), channel_id=1, source_target_pairs={{0,4},{4,8},{8,12},{12,14},{14,10},{10,6},{6,2},{2,0},{5,1},{9,5},... | collective-permute-start | bytes 786440 | tf_op jit(solution)/shard_map/ppermute | solution.py:539
  123.0 7.1 %collective-permute-start.33 = (bf16[64,2048]{1,0:T(8,128)(2,1)S(1)}, bf16[64,2048]{1,0:T(8,128)(2,1)S(1)}, u32[]{:S(2)}, u32[]{:S(2)}) collective-permute-start(bf16[64,2048]{1,0:T(8,128)(2,1)S(1)} %add_convert_fusion.6), channel_id=1, source_target_pairs={{0,4},{4,8},{8,12},{12,14},{14,10},{10,6},{6,2},{2,0},{5,1},{9,5},... | collective-permute-start | bytes 786440 | tf_op jit(solution)/shard_map/ppermute | solution.py:539
  130.2 7.8 %collective-permute-start.34 = (bf16[64,2048]{1,0:T(8,128)(2,1)S(1)}, bf16[64,2048]{1,0:T(8,128)(2,1)S(1)}, u32[]{:S(2)}, u32[]{:S(2)}) collective-permute-start(bf16[64,2048]{1,0:T(8,128)(2,1)S(1)} %add_convert_fusion.5), channel_id=1, source_target_pairs={{0,4},{4,8},{8,12},{12,14},{14,10},{10,6},{6,2},{2,0},{5,1},{9,5},... | collective-permute-start | bytes 786440 | tf_op jit(solution)/shard_map/ppermute | solution.py:539
  138.0 8.3 %collective-permute-start.35 = (bf16[64,2048]{1,0:T(8,128)(2,1)S(1)}, bf16[64,2048]{1,0:T(8,128)(2,1)S(1)}, u32[]{:S(2)}, u32[]{:S(2)}) collective-permute-start(bf16[64,2048]{1,0:T(8,128)(2,1)S(1)} %add_convert_fusion.4), channel_id=1, source_target_pairs={{0,4},{4,8},{8,12},{12,14},{14,10},{10,6},{6,2},{2,0},{5,1},{9,5},... | collective-permute-start | bytes 786440 | tf_op jit(solution)/shard_map/ppermute | solution.py:539
  (64 other events, 496.9 us)

commit v6 on v5

--- a/solution.py
+++ b/solution.py
@@ -485,7 +485,7 @@
     o_ref[...] = (product * column).astype(o_ref.dtype)
 
 
-def out_project(inc, mine, theirs, w_out, ssq, scale_by, part, parts, bn=512):
+def out_project(inc, mine, theirs, w_out, ssq, scale_by, part, parts, bn=1024):
     rows, hp = mine.shape
     cols = w_out.shape[1] // parts
     first = part * (cols // bn)

time: 175 us -> 174 us (level)
  no operation moved by 1% of the time
where the time goes in v6:
time: 174 us
  Pallas kernels  68.8 us (40%)
  waiting for transfers between devices  41.2 us (24%)
  starting transfers between devices  40.6 us (23%)
  local copies, waits for them, and re-layouts  13.3 us (8%)
  other arithmetic  8.14 us (5%)
    ppermute x28, waiting for transfers between devices, onward(): return lax.ppermute(a, ('outc', 'inc'), ring)  34.9 us
    ppermute x28, starting transfers between devices, onward(): return lax.ppermute(a, ('outc', 'inc'), ring)  31.4 us
    pallas_call x4, Pallas kernels, project(): pl.pallas_call(functools.partial(project_kernel, parts, len(olds)), grid_...  25.3 us
    pallas_call x4, Pallas kernels, relayout(): pl.pallas_call(kernel, grid=(steps,), in_specs=specs, out_specs=pl.BlockS...  18.1 us
    pallas_call x1, Pallas kernels, ssm(): pl.pallas_call(ssm_kernel, grid_spec=pltpu.PrefetchScalarGridSpec(num_sca...  9.1 us
    unnamed x100, local copies, waits for them, and re-layouts  6.83 us
    pallas_call x2, Pallas kernels, new_state(): pl.pallas_call(kernel, grid=(steps,), in_specs=specs, out_specs=[states,...  6.58 us
    pallas_call x2, Pallas kernels, out_project(): pl.pallas_call(functools.partial(out_kernel, scale_by), grid_spec=pltpu.P...  5.97 us
  transfers between devices with their start and end apart: 39, of which 17 were waited for; matrix products, arithmetic and copies ran while one was open for 8% of the time, Pallas kernels for 33%

profile of v6, /device:TPU:0, one launch (start us, length us, event | category | flops | bytes accessed | tf_op | source)
XLA Modules:
  0.0 173.5 jit_solution(11069701043674778895)
XLA Ops:
  1.7 3.1 %collective-permute-start.7 = (bf16[32,4096]{1,0:T(8,128)(2,1)S(1)}, bf16[32,4096]{1,0:T(8,128)(2,1)S(1)}, u32[]{:S(2)}, u32[]{:S(2)}) collective-permute-start(bf16[32,4096]{1,0:T(8,128)(2,1)S(1)} %get-tuple-element.130.refs_0_), channel_id=1, source_target_pairs={{0,4},{4,8},{8,12},{12,14},{14,10},{10,6},{6,2},{2,0},{5,1},{9,5},... | collective-permute-start | bytes 786440 | tf_op jit(solution)/shard_map/ppermute | solution.py:539
  6.4 4.4 %relayout.4._ = bf16[2,4096,1024]{2,1,0:T(8,128)(2,1)} custom-call(bf16[4096,16,128]{2,1,0:T(8,128)(2,1)} %w_ref.7), custom_call_target="tpu_custom_call" | custom-call | flops 1073741824 | bytes 8388608 | tf_op jit(solution)/shard_map/relayout/pallas_call | solution.py:77
  14.0 4.5 %relayout.5._ = bf16[2,4096,1024]{2,1,0:T(8,128)(2,1)} custom-call(bf16[4096,16,128]{2,1,0:T(8,128)(2,1)} %w_ref.7, bf16[2,4096,1024]{2,1,0:T(8,128)(2,1)} %relayout.4._), custom_call_target="tpu_custom_call", output_to_operand_aliasing={{}: (1, {})} | custom-call | flops 1073741824 | bytes 8388608 | tf_op jit(solution)/shard_map/relayout/pallas_call | solution.py:77
  23.1 4.6 %relayout.6._ = bf16[2,4096,1024]{2,1,0:T(8,128)(2,1)} custom-call(bf16[4096,16,128]{2,1,0:T(8,128)(2,1)} %w_ref.7, bf16[2,4096,1024]{2,1,0:T(8,128)(2,1)} %relayout.5._), custom_call_target="tpu_custom_call", output_to_operand_aliasing={{}: (1, {})} | custom-call | flops 1073741824 | bytes 8388608 | tf_op jit(solution)/shard_map/relayout/pallas_call | solution.py:77
  31.8 4.6 %relayout.7.refs_8_ = bf16[2,4096,1024]{2,1,0:T(8,128)(2,1)} custom-call(bf16[4096,16,128]{2,1,0:T(8,128)(2,1)} %w_ref.7, bf16[2,4096,1024]{2,1,0:T(8,128)(2,1)} %relayout.6._), custom_call_target="tpu_custom_call", output_to_operand_aliasing={{}: (1, {})} | custom-call | flops 1073741824 | bytes 8388608 | tf_op jit(solution)/shard_map/relayout/pallas_call | solution.py:77
  39.1 6.8 %project.4 = (bf16[256,1024]{1,0:T(8,128)(2,1)}, f32[256,256]{1,0:T(8,128)}) custom-call(s32[8]{0:T(128)S(1)} %compare_select_fusion.2.seq_ref, s32[1]{0:T(128)S(6)} %sub.38.which_ref, bf16[32,4096]{1,0:T(8,128)(2,1)S(1)} %get-tuple-element.130.refs_0_, bf16[32,4096]{1,0:T(8,128)(2,1)S(1)} %copy-done.14, bf16[32,4096]{1,0:T(8,128)(2,1)S(1)} %copy-done.20, ...), custom_call_target="tpu_custom_call" | custom-call | flops 2684354560 | bytes 10485760 | tf_op jit(solution)/shard_map/project/pallas_call | solution.py:138
  47.2 6.2 %project.5.refs_10_ = f32[256,1024]{1,0:T(8,128)} custom-call(s32[8]{0:T(128)S(1)} %compare_select_fusion.2.seq_ref, s32[1]{0:T(128)} %bitcast.which_ref.inc_ref, bf16[32,4096]{1,0:T(8,128)(2,1)S(1)} %get-tuple-element.130.refs_0_, bf16[32,4096]{1,0:T(8,128)(2,1)S(1)} %copy-done.14, bf16[32,4096]{1,0:T(8,128)(2,1)S(1)} %copy-done.20, ...), custom_call_target="tpu_custom_call" | custom-call | flops 2684354560 | bytes 10485760 | tf_op jit(solution)/shard_map/project/pallas_call | solution.py:138
  57.8 5.1 %collective-permute-done.6.refs_7_ = bf16[32,4096]{1,0:T(8,128)(2,1)} collective-permute-done((bf16[32,4096]{1,0:T(8,128)(2,1)}, bf16[32,4096]{1,0:T(8,128)(2,1)}, u32[]{:S(2)}, u32[]{:S(2)}) %collective-permute-start.6) | collective-permute-done | bytes 262176 | tf_op jit(solution)/shard_map/ppermute | solution.py:539
  66.5 6.5 %project.6 = bf16[512,1024]{1,0:T(8,128)(2,1)} custom-call(s32[8]{0:T(128)S(1)} %compare_select_fusion.2.seq_ref, s32[1]{0:T(128)S(6)} %sub.38.which_ref, bf16[32,4096]{1,0:T(8,128)(2,1)S(1)} %collective-permute-done.10.refs_0_, bf16[32,4096]{1,0:T(8,128)(2,1)S(1)} %collective-permute-done.3.refs_1_, bf16[32,4096]{1,0:T(8,128)(2,1)S(1)} %collective-permute-done.11.refs_2_, ...), custom_call_target="tpu_custom_call" | custom-call | flops 2684354560 | bytes 10485760 | tf_op jit(solution)/shard_map/project/pallas_call | solution.py:138
  77.3 5.8 %project.7.mine_ref = f32[512,1024]{1,0:T(8,128)S(1)} custom-call(s32[8]{0:T(128)S(1)} %compare_select_fusion.2.seq_ref, s32[1]{0:T(128)} %bitcast.which_ref.inc_ref, bf16[32,4096]{1,0:T(8,128)(2,1)S(1)} %copy-done.6, bf16[32,4096]{1,0:T(8,128)(2,1)S(1)} %copy-done.8, bf16[32,4096]{1,0:T(8,128)(2,1)S(1)} %copy-done.10, bf16[32,4096]{1,0:T(8,128)(2,1)S(1)} %copy-done.12, ...), custom_call_target="tpu_custom_call" | custom-call | flops 2684354560 | bytes 10485760 | tf_op jit(solution)/shard_map/project/pallas_call | solution.py:138
  83.3 9.1 %ssm.1 = (bf16[512,512]{1,0:T(8,128)(2,1)S(1)}, f32[8,512]{1,0:T(8,128)S(1)}, bf16[512,512]{1,0:T(8,128)(2,1)}, bf16[512,128]{1,0:T(8,128)(2,1)}, f32[512,128]{1,0:T(8,128)}, /*index=5*/bf16[512,512]{1,0:T(8,128)(2,1)}) custom-call(s32[1]{0:T(128)} %bitcast.9.group_ref, s32[512,2]{1,0:T(8,128)S(1)} %broadcast_bitcast_fusion.meta_ref.refs_0_, ...), custom_call_target="tpu_custom_call" | custom-call | flops 2147483648 | bytes 25165824 | tf_op jit(solution)/shard_map/ssm/pallas_call | solution.py:340
  95.7 5.2 %collective-permute-start.21 = (bf16[96,128]{1,0:T(8,128)(2,1)S(1)}, bf16[96,128]{1,0:T(8,128)(2,1)S(1)}, u32[]{:S(2)}, u32[]{:S(2)}) collective-permute-start(bf16[96,128]{1,0:T(8,128)(2,1)S(1)} %constant_dynamic-slice_fusion.2), channel_id=1, source_target_pairs={{0,8},{2,10},{4,12},{6,14},{8,0},{10,2},{12,4},{14,6},{1,9},{3,11}... | collective-permute-start | bytes 73736 | tf_op jit(solution)/shard_map/ppermute | solution.py:640
  101.0 3.7 %collective-permute-done.20 = f32[8,512]{1,0:T(8,128)S(1)} collective-permute-done((f32[8,512]{1,0:T(8,128)S(1)}, f32[8,512]{1,0:T(8,128)S(1)}, u32[]{:S(2)}, u32[]{:S(2)}) %collective-permute-start.20) | collective-permute-done | bytes 16416 | tf_op jit(solution)/shard_map/ppermute | solution.py:631
  105.1 3.4 %copy-done = bf16[1024,4096]{1,0:T(8,128)(2,1)S(1)} copy-done((bf16[1024,4096]{1,0:T(8,128)(2,1)S(1)}, bf16[1024,4096]{1,0:T(8,128)(2,1)}, u32[]{:S(2)}) %copy-start) | copy-done | bytes 8388632
  108.5 3.0 %out_project.3 = bf16[512,2048]{1,0:T(8,128)(2,1)S(1)} custom-call(s32[1]{0:T(128)} %bitcast.which_ref.inc_ref, bf16[512,512]{1,0:T(8,128)(2,1)S(1)} %get-tuple-element.93.mine_ref, bf16[512,512]{1,0:T(8,128)(2,1)S(1)} %collective-permute-done.19.theirs_ref, bf16[1024,4096]{1,0:T(8,128)(2,1)S(1)} %copy-done, bf16[1024,4096]{1,0:T(8,128)(2,1)S(1)} %copy-done, ...), custom_call_target="tpu_custom_call" | custom-call | flops 2147483648 | bytes 8388608 | tf_op jit(solution)/shard_map/out_project/pallas_call | solution.py:492
  111.6 3.0 %out_project.2 = bf16[512,2048]{1,0:T(8,128)(2,1)S(1)} custom-call(s32[1]{0:T(128)} %bitcast.which_ref.inc_ref, bf16[512,512]{1,0:T(8,128)(2,1)S(1)} %get-tuple-element.93.mine_ref, bf16[512,512]{1,0:T(8,128)(2,1)S(1)} %collective-permute-done.19.theirs_ref, bf16[1024,4096]{1,0:T(8,128)(2,1)S(1)} %copy-done, bf16[1024,4096]{1,0:T(8,128)(2,1)S(1)} %copy-done, ...), custom_call_target="tpu_custom_call" | custom-call | flops 2147483648 | bytes 8388608 | tf_op jit(solution)/shard_map/out_project/pallas_call | solution.py:492
  116.8 3.3 %new_state.2 = (bf16[8,1,8,512,128]{4,3,2,1,0:T(8,128)(2,1)}, bf16[256,512]{1,0:T(8,128)(2,1)S(1)}) custom-call(s32[512,2]{1,0:T(8,128)S(1)} %broadcast_bitcast_fusion.meta_ref.refs_0_, bf16[512,512]{1,0:T(8,128)(2,1)S(1)} %copy-done.15, bf16[512,128]{1,0:T(8,128)(2,1)S(1)} %copy-done.32, f32[512,128]{1,0:T(8,128)S(1)} %copy-done.31, ...), custom_call_target="tpu_custom_call" | custom-call | flops 1073741824 | bytes 16777216 | tf_op jit(solution)/shard_map/new_state/pallas_call | solution.py:465
  122.9 3.6 %collective-permute-done.24 = bf16[64,2048]{1,0:T(8,128)(2,1)S(1)} collective-permute-done((bf16[64,2048]{1,0:T(8,128)(2,1)S(1)}, bf16[64,2048]{1,0:T(8,128)(2,1)S(1)}, u32[]{:S(2)}, u32[]{:S(2)}) %collective-permute-start.24) | collective-permute-done | bytes 262176 | tf_op jit(solution)/shard_map/ppermute | solution.py:539
  130.2 2.8 %collective-permute-done.25 = bf16[64,2048]{1,0:T(8,128)(2,1)S(1)} collective-permute-done((bf16[64,2048]{1,0:T(8,128)(2,1)S(1)}, bf16[64,2048]{1,0:T(8,128)(2,1)S(1)}, u32[]{:S(2)}, u32[]{:S(2)}) %collective-permute-start.25) | collective-permute-done | bytes 262176 | tf_op jit(solution)/shard_map/ppermute | solution.py:539
  133.1 3.3 %new_state.3 = (bf16[8,1,8,512,128]{4,3,2,1,0:T(8,128)(2,1)}, bf16[256,512]{1,0:T(8,128)(2,1)S(1)}) custom-call(s32[512,2]{1,0:T(8,128)S(1)} %broadcast_bitcast_fusion.meta_ref.refs_0_, bf16[512,512]{1,0:T(8,128)(2,1)S(1)} %copy-done.15, bf16[512,128]{1,0:T(8,128)(2,1)S(1)} %copy-done.32, ...), custom_call_target="tpu_custom_call", output_to_operand_aliasing={{0}: (7, {})} | custom-call | flops 1073741824 | bytes 16777216 | tf_op jit(solution)/shard_map/new_state/pallas_call | solution.py:465
  138.5 4.2 %collective-permute-done.26 = bf16[64,2048]{1,0:T(8,128)(2,1)S(1)} collective-permute-done((bf16[64,2048]{1,0:T(8,128)(2,1)S(1)}, bf16[64,2048]{1,0:T(8,128)(2,1)S(1)}, u32[]{:S(2)}, u32[]{:S(2)}) %collective-permute-start.26) | collective-permute-done | bytes 262176 | tf_op jit(solution)/shard_map/ppermute | solution.py:539
  146.5 2.8 %collective-permute-done.28 = bf16[64,2048]{1,0:T(8,128)(2,1)S(1)} collective-permute-done((bf16[64,2048]{1,0:T(8,128)(2,1)S(1)}, bf16[64,2048]{1,0:T(8,128)(2,1)S(1)}, u32[]{:S(2)}, u32[]{:S(2)}) %collective-permute-start.28) | collective-permute-done | bytes 262176 | tf_op jit(solution)/shard_map/ppermute | solution.py:539
  161.5 2.8 %collective-permute-done.30 = bf16[64,2048]{1,0:T(8,128)(2,1)S(1)} collective-permute-done((bf16[64,2048]{1,0:T(8,128)(2,1)S(1)}, bf16[64,2048]{1,0:T(8,128)(2,1)S(1)}, u32[]{:S(2)}, u32[]{:S(2)}) %collective-permute-start.30) | collective-permute-done | bytes 262176 | tf_op jit(solution)/shard_map/ppermute | solution.py:539
  167.1 4.6 %collective-permute-done.31 = bf16[64,2048]{1,0:T(8,128)(2,1)S(1)} collective-permute-done((bf16[64,2048]{1,0:T(8,128)(2,1)S(1)}, bf16[64,2048]{1,0:T(8,128)(2,1)S(1)}, u32[]{:S(2)}, u32[]{:S(2)}) %collective-permute-start.31) | collective-permute-done | bytes 262176 | tf_op jit(solution)/shard_map/ppermute | solution.py:539
  (221 shorter events, 65.7 us)
Async XLA Ops:
  1.7 9.1 %collective-permute-start.7 = (bf16[32,4096]{1,0:T(8,128)(2,1)S(1)}, bf16[32,4096]{1,0:T(8,128)(2,1)S(1)}, u32[]{:S(2)}, u32[]{:S(2)}) collective-permute-start(bf16[32,4096]{1,0:T(8,128)(2,1)S(1)} %get-tuple-element.130.refs_0_), channel_id=1, source_target_pairs={{0,4},{4,8},{8,12},{12,14},{14,10},{10,6},{6,2},{2,0},{5,1},{9,5},... | collective-permute-start | bytes 786440 | tf_op jit(solution)/shard_map/ppermute | solution.py:539
  4.8 7.7 %collective-permute-start = (bf16[32,4096]{1,0:T(8,128)(2,1)S(1)}, bf16[32,4096]{1,0:T(8,128)(2,1)S(1)}, u32[]{:S(2)}, u32[]{:S(2)}) collective-permute-start(bf16[32,4096]{1,0:T(8,128)(2,1)S(1)} %get-tuple-element.131.refs_1_), channel_id=1, source_target_pairs={{0,4},{4,8},{8,12},{12,14},{14,10},{10,6},{6,2},{2,0},{5,1},{9,5},... | collective-permute-start | bytes 786440 | tf_op jit(solution)/shard_map/ppermute | solution.py:539
  10.8 7.7 %collective-permute-start.8 = (bf16[32,4096]{1,0:T(8,128)(2,1)S(1)}, bf16[32,4096]{1,0:T(8,128)(2,1)S(1)}, u32[]{:S(2)}, u32[]{:S(2)}) collective-permute-start(bf16[32,4096]{1,0:T(8,128)(2,1)S(1)} %collective-permute-done.7.refs_2_), channel_id=1, source_target_pairs={{0,4},{4,8},{8,12},{12,14},{14,10},{10,6},{6,2},{2,0},{5,1},{9,5},... | collective-permute-start | bytes 786440 | tf_op jit(solution)/shard_map/ppermute | solution.py:539
  12.5 7.7 %collective-permute-start.1 = (bf16[32,4096]{1,0:T(8,128)(2,1)S(1)}, bf16[32,4096]{1,0:T(8,128)(2,1)S(1)}, u32[]{:S(2)}, u32[]{:S(2)}) collective-permute-start(bf16[32,4096]{1,0:T(8,128)(2,1)S(1)} %collective-permute-done.refs_3_), channel_id=1, source_target_pairs={{0,4},{4,8},{8,12},{12,14},{14,10},{10,6},{6,2},{2,0},{5,1},{9,5},... | collective-permute-start | bytes 786440 | tf_op jit(solution)/shard_map/ppermute | solution.py:539
  18.5 9.2 %collective-permute-start.9 = (bf16[32,4096]{1,0:T(8,128)(2,1)S(1)}, bf16[32,4096]{1,0:T(8,128)(2,1)S(1)}, u32[]{:S(2)}, u32[]{:S(2)}) collective-permute-start(bf16[32,4096]{1,0:T(8,128)(2,1)S(1)} %collective-permute-done.8.refs_4_), channel_id=1, source_target_pairs={{0,4},{4,8},{8,12},{12,14},{14,10},{10,6},{6,2},{2,0},{5,1},{9,5},... | collective-permute-start | bytes 786440 | tf_op jit(solution)/shard_map/ppermute | solution.py:539
  20.1 9.2 %collective-permute-start.2 = (bf16[32,4096]{1,0:T(8,128)(2,1)S(1)}, bf16[32,4096]{1,0:T(8,128)(2,1)S(1)}, u32[]{:S(2)}, u32[]{:S(2)}) collective-permute-start(bf16[32,4096]{1,0:T(8,128)(2,1)S(1)} %collective-permute-done.1.refs_5_), channel_id=1, source_target_pairs={{0,4},{4,8},{8,12},{12,14},{14,10},{10,6},{6,2},{2,0},{5,1},{9,5},... | collective-permute-start | bytes 786440 | tf_op jit(solution)/shard_map/ppermute | solution.py:539
  27.7 8.6 %collective-permute-start.10 = (bf16[32,4096]{1,0:T(8,128)(2,1)S(1)}, bf16[32,4096]{1,0:T(8,128)(2,1)S(1)}, u32[]{:S(2)}, u32[]{:S(2)}) collective-permute-start(bf16[32,4096]{1,0:T(8,128)(2,1)S(1)} %collective-permute-done.9.refs_6_), channel_id=1, source_target_pairs={{0,4},{4,8},{8,12},{12,14},{14,10},{10,6},{6,2},{2,0},{5,1},{9,5},... | collective-permute-start | bytes 786440 | tf_op jit(solution)/shard_map/ppermute | solution.py:539
  29.3 8.4 %collective-permute-start.3 = (bf16[32,4096]{1,0:T(8,128)(2,1)S(1)}, bf16[32,4096]{1,0:T(8,128)(2,1)S(1)}, u32[]{:S(2)}, u32[]{:S(2)}) collective-permute-start(bf16[32,4096]{1,0:T(8,128)(2,1)S(1)} %collective-permute-done.2.refs_7_), channel_id=1, source_target_pairs={{0,4},{4,8},{8,12},{12,14},{14,10},{10,6},{6,2},{2,0},{5,1},{9,5},... | collective-permute-start | bytes 786440 | tf_op jit(solution)/shard_map/ppermute | solution.py:539
  36.4 9.5 %collective-permute-start.11 = (bf16[32,4096]{1,0:T(8,128)(2,1)S(1)}, bf16[32,4096]{1,0:T(8,128)(2,1)S(1)}, u32[]{:S(2)}, u32[]{:S(2)}) collective-permute-start(bf16[32,4096]{1,0:T(8,128)(2,1)S(1)} %collective-permute-done.10.refs_0_), channel_id=1, source_target_pairs={{0,4},{4,8},{8,12},{12,14},{14,10},{10,6},{6,2},{2,0},{5,1},{9,5},... | collective-permute-start | bytes 786440 | tf_op jit(solution)/shard_map/ppermute | solution.py:539
  37.7 8.6 %collective-permute-start.4 = (bf16[32,4096]{1,0:T(8,128)(2,1)S(1)}, bf16[32,4096]{1,0:T(8,128)(2,1)S(1)}, u32[]{:S(2)}, u32[]{:S(2)}) collective-permute-start(bf16[32,4096]{1,0:T(8,128)(2,1)S(1)} %collective-permute-done.3.refs_1_), channel_id=1, source_target_pairs={{0,4},{4,8},{8,12},{12,14},{14,10},{10,6},{6,2},{2,0},{5,1},{9,5},... | collective-permute-start | bytes 786440 | tf_op jit(solution)/shard_map/ppermute | solution.py:539
  45.9 7.6 %collective-permute-start.12 = (bf16[32,4096]{1,0:T(8,128)(2,1)S(1)}, bf16[32,4096]{1,0:T(8,128)(2,1)}, u32[]{:S(2)}, u32[]{:S(2)}) collective-permute-start(bf16[32,4096]{1,0:T(8,128)(2,1)S(1)} %collective-permute-done.11.refs_2_), channel_id=1, source_target_pairs={{0,4},{4,8},{8,12},{12,14},{14,10},{10,6},{6,2},{2,0},{5,1},{9,5},... | collective-permute-start | bytes 786440 | tf_op jit(solution)/shard_map/ppermute | solution.py:539
  46.3 8.8 %collective-permute-start.5 = (bf16[32,4096]{1,0:T(8,128)(2,1)S(1)}, bf16[32,4096]{1,0:T(8,128)(2,1)}, u32[]{:S(2)}, u32[]{:S(2)}) collective-permute-start(bf16[32,4096]{1,0:T(8,128)(2,1)S(1)} %collective-permute-done.4.refs_3_), channel_id=1, source_target_pairs={{0,4},{4,8},{8,12},{12,14},{14,10},{10,6},{6,2},{2,0},{5,1},{9,5},... | collective-permute-start | bytes 786440 | tf_op jit(solution)/shard_map/ppermute | solution.py:539
  53.4 9.5 %collective-permute-start.13 = (bf16[32,4096]{1,0:T(8,128)(2,1)}, bf16[32,4096]{1,0:T(8,128)(2,1)}, u32[]{:S(2)}, u32[]{:S(2)}) collective-permute-start(bf16[32,4096]{1,0:T(8,128)(2,1)} %collective-permute-done.12.refs_4_), channel_id=1, source_target_pairs={{0,4},{4,8},{8,12},{12,14},{14,10},{10,6},{6,2},{2,0},{5,1},{9,5},... | collective-permute-start | bytes 786440 | tf_op jit(solution)/shard_map/ppermute | solution.py:539
  55.2 7.8 %collective-permute-start.6 = (bf16[32,4096]{1,0:T(8,128)(2,1)}, bf16[32,4096]{1,0:T(8,128)(2,1)}, u32[]{:S(2)}, u32[]{:S(2)}) collective-permute-start(bf16[32,4096]{1,0:T(8,128)(2,1)} %collective-permute-done.5.refs_5_), channel_id=1, source_target_pairs={{0,4},{4,8},{8,12},{12,14},{14,10},{10,6},{6,2},{2,0},{5,1},{9,5},... | collective-permute-start | bytes 786440 | tf_op jit(solution)/shard_map/ppermute | solution.py:539
  73.0 10.2 %collective-permute-start.15 = (bf16[512,1024]{1,0:T(8,128)(2,1)}, bf16[512,1024]{1,0:T(8,128)(2,1)}, u32[]{:S(2)}, u32[]{:S(2)}) collective-permute-start(bf16[512,1024]{1,0:T(8,128)(2,1)} %project.6), channel_id=1, source_target_pairs={{0,1},{1,0},{2,3},{3,2},{4,5},{5,4},{6,7},{7,6},{8,9},{9,8},{10,11... | collective-permute-start | bytes 3145736 | tf_op jit(solution)/shard_map/ppermute | solution.py:542
  74.9 8.2 %collective-permute-start.16 = (bf16[512,128]{1,0:T(8,128)(2,1)S(1)}, bf16[512,128]{1,0:T(8,128)(2,1)S(1)}, u32[]{:S(2)}, u32[]{:S(2)}) collective-permute-start(bf16[512,128]{1,0:T(8,128)(2,1)S(1)} %slice.24.raw_ref), channel_id=1, source_target_pairs={{8,0},{0,2},{10,4},{2,6},{12,8},{4,10},{14,12},{6,14},{9,1},{1,3},... | collective-permute-start | bytes 393224 | tf_op jit(solution)/shard_map/ppermute | solution.py:606
  76.2 7.0 %collective-permute-start.17 = (bf16[512,128]{1,0:T(8,128)(2,1)S(1)}, bf16[512,128]{1,0:T(8,128)(2,1)S(1)}, u32[]{:S(2)}, u32[]{:S(2)}) collective-permute-start(bf16[512,128]{1,0:T(8,128)(2,1)S(1)} %slice.24.raw_ref), channel_id=1, source_target_pairs={{0,0},{8,2},{2,4},{10,6},{4,8},{12,10},{6,12},{14,14},{1,1},{9,3},... | collective-permute-start | bytes 393224 | tf_op jit(solution)/shard_map/ppermute | solution.py:606
  92.4 12.4 %collective-permute-start.19 = (bf16[512,512]{1,0:T(8,128)(2,1)S(1)}, bf16[512,512]{1,0:T(8,128)(2,1)S(1)}, u32[]{:S(2)}, u32[]{:S(2)}) collective-permute-start(bf16[512,512]{1,0:T(8,128)(2,1)S(1)} %get-tuple-element.93.mine_ref), channel_id=1, source_target_pairs={{0,1},{1,0},{2,3},{3,2},{4,5},{5,4},{6,7},{7,6},{8,9},{9,8},{10,11... | collective-permute-start | bytes 1572872 | tf_op jit(solution)/shard_map/ppermute | solution.py:542
  95.7 9.0 %collective-permute-start.21 = (bf16[96,128]{1,0:T(8,128)(2,1)S(1)}, bf16[96,128]{1,0:T(8,128)(2,1)S(1)}, u32[]{:S(2)}, u32[]{:S(2)}) collective-permute-start(bf16[96,128]{1,0:T(8,128)(2,1)S(1)} %constant_dynamic-slice_fusion.2), channel_id=1, source_target_pairs={{0,8},{2,10},{4,12},{6,14},{8,0},{10,2},{12,4},{14,6},{1,9},{3,11}... | collective-permute-start | bytes 73736 | tf_op jit(solution)/shard_map/ppermute | solution.py:640
  104.8 11.6 %collective-permute-start.22 = (bf16[2,96,128]{2,1,0:T(8,128)(2,1)S(1)}, bf16[2,96,128]{2,1,0:T(8,128)(2,1)S(1)}, u32[]{:S(2)}, u32[]{:S(2)}) collective-permute-start(bf16[2,96,128]{2,1,0:T(8,128)(2,1)S(1)} %maximum_select_fusion.3), channel_id=1, source_target_pairs={{0,4},{2,6},{4,0},{6,2},{8,12},{10,14},{12,8},{14,10},{1,5},{3,7},... | collective-permute-start | bytes 147464 | tf_op jit(solution)/shard_map/ppermute | solution.py:640
  114.6 7.5 %collective-permute-start.32 = (bf16[64,2048]{1,0:T(8,128)(2,1)S(1)}, bf16[64,2048]{1,0:T(8,128)(2,1)S(1)}, u32[]{:S(2)}, u32[]{:S(2)}) collective-permute-start(bf16[64,2048]{1,0:T(8,128)(2,1)S(1)} %constant_dynamic-slice_fusion), channel_id=1, source_target_pairs={{0,4},{4,8},{8,12},{12,14},{14,10},{10,6},{6,2},{2,0},{5,1},{9,5},... | collective-permute-start | bytes 786440 | tf_op jit(solution)/shard_map/ppermute | solution.py:539
  122.2 7.1 %collective-permute-start.33 = (bf16[64,2048]{1,0:T(8,128)(2,1)S(1)}, bf16[64,2048]{1,0:T(8,128)(2,1)S(1)}, u32[]{:S(2)}, u32[]{:S(2)}) collective-permute-start(bf16[64,2048]{1,0:T(8,128)(2,1)S(1)} %add_convert_fusion.6), channel_id=1, source_target_pairs={{0,4},{4,8},{8,12},{12,14},{14,10},{10,6},{6,2},{2,0},{5,1},{9,5},... | collective-permute-start | bytes 786440 | tf_op jit(solution)/shard_map/ppermute | solution.py:539
  129.4 7.8 %collective-permute-start.34 = (bf16[64,2048]{1,0:T(8,128)(2,1)S(1)}, bf16[64,2048]{1,0:T(8,128)(2,1)S(1)}, u32[]{:S(2)}, u32[]{:S(2)}) collective-permute-start(bf16[64,2048]{1,0:T(8,128)(2,1)S(1)} %add_convert_fusion.5), channel_id=1, source_target_pairs={{0,4},{4,8},{8,12},{12,14},{14,10},{10,6},{6,2},{2,0},{5,1},{9,5},... | collective-permute-start | bytes 786440 | tf_op jit(solution)/shard_map/ppermute | solution.py:539
  137.2 8.3 %collective-permute-start.35 = (bf16[64,2048]{1,0:T(8,128)(2,1)S(1)}, bf16[64,2048]{1,0:T(8,128)(2,1)S(1)}, u32[]{:S(2)}, u32[]{:S(2)}) collective-permute-start(bf16[64,2048]{1,0:T(8,128)(2,1)S(1)} %add_convert_fusion.4), channel_id=1, source_target_pairs={{0,4},{4,8},{8,12},{12,14},{14,10},{10,6},{6,2},{2,0},{5,1},{9,5},... | collective-permute-start | bytes 786440 | tf_op jit(solution)/shard_map/ppermute | solution.py:539
  (64 other events, 494.1 us)
